TPU v7x, 32 devices: a whole 2x2x4 slice. The times are simulated.
32 devices in a mesh: groups: 2 (over y), node: 4 (over z), local: 4 (over x, core).
Axes of the slice: x: 2, y: 2, z: 4, core: 2. Of those that a mesh axis runs over, the one named last changes fastest.
Arguments:
- hidden_states: bfloat16 [128, 3584], P(('groups', 'node', 'local')), parts along dimension 0, may hold values from -6 to 6
- norm_gain: float32 [3584], replicated, may hold values from 0.5 to 1.5
- route_groups: int32 [128, 4], P(('groups', 'node', 'local')), parts along dimension 0, may hold values from 0 to 7, as said below
- route_picks: int32 [128, 8], P(('groups', 'node', 'local')), parts along dimension 0, may hold values from 0 to 15, as said below
- gate_weights: bfloat16 [128, 8], P(('groups', 'node', 'local')), parts along dimension 0, may hold values from 0.049804688 to 0.5
- expert_gate: bfloat16 [32, 3584, 1024], P('node', None, 'local'), may hold values from -0.09375 to 0.09375
- expert_up: bfloat16 [32, 3584, 1024], P('node', None, 'local'), may hold values from -0.09375 to 0.09375
- expert_down: bfloat16 [32, 1024, 3584], P('node', 'local'), may hold values from -0.1875 to 0.1875
- shared_gate: bfloat16 [1024, 3584], P('local', 'node'), may hold values from -0.09375 to 0.09375
- shared_up: bfloat16 [1024, 3584], P('local', 'node'), may hold values from -0.09375 to 0.09375
- shared_down: bfloat16 [1024, 3584], P('local', 'node'), may hold values from -0.1875 to 0.1875
Outputs:
- moe_out: bfloat16 [128, 3584], P(('groups', 'node', 'local')), parts along dimension 0
There are 2 independent parts, one for each index of `groups`. A program takes and returns all parts, laid end to end along the dimension named above; an argument that names none is the same for every part. Nothing has to cross between parts.
Inputs may be any that keep to these rules, and one draw needn't show every extreme that they name: `route_groups`: each row names 4 different node groups; the 4 tokens of every device name each node group exactly 2 times. `route_picks`: each row holds 8 different values; the value a * 4 + j picks expert route_groups[t, a] * 4 + j, and every a from 0 to 3 appears in 2 values of every row; of one device's tokens at most 2 pick any one expert, and in every draw some expert is picked by exactly 2 tokens of every device.
All inputs are finite; a program needn't handle non-finite values.
Results may differ from a plain program's by a relative error of at most 0.012.
Values may be sent and summed in bfloat16 or wider, within the bound.
No kernel may reach another device: no remote copies, remote signals or barrier semaphores. Data moves between devices by JAX's collectives and lax.ppermute only.
A program may use at most 128 MiB of HBM per device.

v0:
```python
import jax
import jax.numpy as jnp
from jax import lax
from jax.sharding import PartitionSpec as P

NODE_GROUPS = 8
TOP_GROUPS = 4


def shared_expert(normed, gate_rows, up_rows, down_rows):
    contract = (((1,), (1,)), ((), ()))
    gate_part = lax.dot_general(normed, gate_rows, contract, preferred_element_type=jnp.float32)
    up_part = lax.dot_general(normed, up_rows, contract, preferred_element_type=jnp.float32)
    shared_hidden = (jax.nn.silu(gate_part) * up_part).astype(jnp.bfloat16)
    return jnp.dot(shared_hidden, down_rows, preferred_element_type=jnp.float32).astype(
        jnp.bfloat16
    )


def local(
    hidden_states,
    norm_gain,
    route_groups,
    route_picks,
    gate_weights,
    expert_gate,
    expert_up,
    expert_down,
    shared_gate,
    shared_up,
    shared_down,
):
    node_count = lax.axis_size("node")
    local_count = lax.axis_size("local")
    token_count = hidden_states.shape[0]
    feature_count = hidden_states.shape[1]
    held = expert_gate.shape[0]
    expert_total = held * node_count
    per_group = expert_total // NODE_GROUPS
    capacity = token_count * TOP_GROUPS // NODE_GROUPS
    features = hidden_states.astype(jnp.float32)
    mean_square = jnp.mean(features * features, axis=1, keepdims=True)
    normed = (features * lax.rsqrt(mean_square + 1e-06) * norm_gain[None, :]).astype(jnp.bfloat16)
    group_slot = route_picks // per_group
    inner_pick = route_picks % per_group
    group_pick = jnp.take_along_axis(route_groups, group_slot, axis=1)
    expert_ids = group_pick * per_group + inner_pick
    expert_range = jnp.arange(expert_total, dtype=jnp.int32)
    hits = expert_ids[:, :, None] == expert_range[None, None, :]
    chosen = jnp.any(hits, axis=1).astype(jnp.int32)
    token_weight = jnp.sum(
        jnp.where(hits, gate_weights.astype(jnp.float32)[:, :, None], 0.0), axis=1
    )
    slot_rank = jnp.cumsum(chosen, axis=0) - chosen
    slot_range = jnp.arange(capacity, dtype=jnp.int32)
    placing_mask = (chosen.T[:, None, :] == 1) & (
        slot_rank.T[:, None, :] == slot_range[None, :, None]
    )
    placing = placing_mask.astype(jnp.bfloat16)
    slot_weight = jnp.einsum(
        "ect,te->ec",
        placing_mask.astype(jnp.float32),
        token_weight,
        precision=lax.Precision.HIGHEST,
    ).astype(jnp.bfloat16)
    send_rows = jnp.einsum(
        "ect,td->ecd", placing, normed, preferred_element_type=jnp.float32
    ).astype(jnp.bfloat16)
    received_rows, received_weight = (
        lax.all_to_all(send_rows, "node", split_axis=0, concat_axis=0, tiled=True),
        lax.all_to_all(slot_weight, "node", split_axis=0, concat_axis=0, tiled=True),
    )
    rows_grid = received_rows.reshape(node_count, held, capacity, feature_count)
    weight_grid = received_weight.reshape(node_count, held, capacity)
    row_block, weights = lax.all_gather((rows_grid, weight_grid), "local", axis=0, tiled=True)
    gate_part = jnp.einsum(
        "necd,edf->necf", row_block, expert_gate, preferred_element_type=jnp.float32
    )
    up_part = jnp.einsum("necd,edf->necf", row_block, expert_up, preferred_element_type=jnp.float32)
    block_hidden = (jax.nn.silu(gate_part) * up_part).astype(jnp.bfloat16)
    output = jnp.einsum(
        "necf,efd->necd", block_hidden, expert_down, preferred_element_type=jnp.float32
    )
    partials = (weights.astype(jnp.float32)[..., None] * output).astype(jnp.bfloat16)
    full_gate, full_up, full_down = (
        lax.all_gather(shared_gate, "node", axis=1, tiled=True),
        lax.all_gather(shared_up, "node", axis=1, tiled=True),
        lax.all_gather(shared_down, "node", axis=1, tiled=True),
    )
    shared_partial = shared_expert(
        lax.all_gather(normed, "local", axis=0, tiled=True), full_gate, full_up, full_down
    )
    shared_stack = shared_partial.reshape(local_count, token_count, feature_count)
    grid = partials.reshape(local_count, node_count, held * capacity, feature_count)
    returned = lax.all_to_all(grid, "node", split_axis=1, concat_axis=1, tiled=True)
    summed, shared_sum = (
        lax.psum_scatter(returned, "local", scatter_dimension=0, tiled=True).astype(jnp.float32),
        lax.psum_scatter(shared_stack, "local", scatter_dimension=0, tiled=True).astype(
            jnp.float32
        ),
    )
    expert_sum = summed.astype(jnp.bfloat16).reshape(expert_total, capacity, feature_count)
    routed = jnp.einsum("ect,ecd->td", placing, expert_sum, preferred_element_type=jnp.float32)
    return (shared_sum.reshape(token_count, feature_count) + routed).astype(jnp.bfloat16)


def solution(mesh):
    placed = (
        P(("groups", "node", "local"), None),
        P(),
        P(("groups", "node", "local"), None),
        P(("groups", "node", "local"), None),
        P(("groups", "node", "local"), None),
        P("node", None, "local"),
        P("node", None, "local"),
        P("node", "local", None),
        P("local", "node"),
        P("local", "node"),
        P("local", "node"),
    )
    return jax.shard_map(
        local,
        mesh=mesh,
        in_specs=placed,
        out_specs=P(("groups", "node", "local"), None),
        check_vma=False,
    )
```

profile of v0, /device:TPU:0, one launch (start us, length us, event | category | flops | bytes accessed | tf_op | source)
XLA Modules:
  0.0 269.9 jit_solution(8540469753656885823)
XLA Ops:
  6.6 0.9 fusion.41
  10.9 19.2 %all_to_all.19 = bf16[32,2,3584]{2,1,0:T(2,128)(2,1)S(1)} all-to-all(bf16[32,2,3584]{2,1,0:T(2,128)(2,1)S(1)} %copy.45), channel_id=1, replica_groups=mesh['groups'=2,'node'=4,'local'=4] {'node'}, dimensions={0} | all-to-all | bytes 917504 | tf_op jit(solution)/shard_map/all_to_all | solution.py:70
  33.2 3.2 %all-to-all-start = ((bf16[4,8,2]{1,2,0:T(2,128)(2,1)}), bf16[4,8,2]{1,2,0:T(2,128)(2,1)S(1)}, u32[]{:S(2)}, u32[]{:S(2)}) async-start(bf16[4,8,2]{1,2,0:T(2,128)(2,1)} %copy.42), calls=%async_computation | async-start | bytes 4096 | tf_op jit(solution)/shard_map/all_to_all | solution.py:71
  37.0 4.9 %all-to-all-done = bf16[4,8,2]{1,2,0:T(2,128)(2,1)S(1)} async-done(((bf16[4,8,2]{1,2,0:T(2,128)(2,1)}), bf16[4,8,2]{1,2,0:T(2,128)(2,1)S(1)}, u32[]{:S(2)}, u32[]{:S(2)}) %all-to-all-start) | async-done | bytes 160 | tf_op jit(solution)/shard_map/all_to_all | solution.py:71
  41.8 5.2 %all_gather.22 = bf16[16,8,2]{1,2,0:T(2,128)(2,1)S(1)} all-gather(bf16[4,8,2]{1,2,0:T(2,128)(2,1)S(1)} %all-to-all-done), channel_id=1, replica_groups=mesh['groups'=2,'node'=4,'local'=4] {'local'}, dimensions={0}, use_global_device_ids=true | all-gather | bytes 640 | tf_op jit(solution)/shard_map/all_gather | solution.py:75
  47.1 4.3 %all-gather.12.cloned.1.call-done = bf16[16,8,2,3584]{3,1,2,0:T(8,128)(2,1)} async-done(((bf16[4,8,2,3584]{3,1,2,0:T(8,128)(2,1)}), bf16[16,8,2,3584]{3,1,2,0:T(8,128)(2,1)}) %all-gather.12.cloned.1.call-update) | async-done | bytes 1835024 | tf_op jit(solution)/shard_map/all_gather | solution.py:75
  51.4 8.6 %fusion.19 = f32[16,8,2,256]{3,0,2,1:T(8,128)S(1)} fusion(bf16[8,3584,256]{2,1,0:T(8,128)(2,1)} %param.16, bf16[16,8,2,3584]{3,1,2,0:T(8,128)(2,1)} %all-gather.12.cloned.1.call-done), kind=kOutput, calls=%fused_computation.17 | convolution fusion | flops 469762048 | bytes 16777216 | tf_op jit(solution)/shard_map/necd,edf->necf/dot_general | solution.py:76
  60.0 1.6 copy-done.1
  62.3 2.7 %fusion.34 = bf16[16,8,2,256]{3,0,2,1:T(8,128)(2,1)S(1)} fusion(bf16[8,3584,256]{2,1,0:T(8,128)(2,1)S(1)} %copy-done.1, bf16[16,8,2,3584]{3,1,2,0:T(8,128)(2,1)S(1)} %copy-done.4, f32[16,8,2,256]{3,0,2,1:T(8,128)S(1)} %fusion.19), kind=kOutput, calls=%fused_computation.20 | convolution fusion | flops 470155264 | bytes 16908288 | tf_op jit(solution)/shard_map/necd,edf->necf/dot_general | solution.py:79
  65.0 2.4 copy-done.2
  67.5 3.8 %fusion.12 = bf16[16,8,2,3584]{3,0,2,1:T(8,128)(2,1)} fusion(bf16[16,8,2,256]{3,0,2,1:T(8,128)(2,1)S(1)} %fusion.34, bf16[8,256,3584]{2,1,0:T(8,128)(2,1)S(1)} %copy-done.2, f32[16,8,2]{0,2,1:T(2,128)S(1)} %copy.44), kind=kOutput, calls=%fused_computation.9 | convolution fusion | flops 471597056 | bytes 16647168 | tf_op jit(solution)/shard_map/necf,efd->necd/dot_general | solution.py:81
  71.3 3.1 %reshape.51 = bf16[4,4,16,3584]{3,1,0,2:T(4,128)(2,1)S(1)} reshape(bf16[16,8,2,3584]{3,0,2,1:T(8,128)(2,1)} %fusion.12) | data formatting | bytes 3670016 | tf_op jit(solution)/shard_map/reshape | solution.py:94
  74.4 2.3 copy.49
  76.7 4.5 %all-to-all-start.2 = ((bf16[4,4,16,3584]{3,2,0,1:T(8,128)(2,1)}), bf16[4,4,16,3584]{3,2,0,1:T(8,128)(2,1)S(1)}, u32[]{:S(2)}, u32[]{:S(2)}) async-start(bf16[4,4,16,3584]{3,2,0,1:T(8,128)(2,1)} %copy.49), calls=%async_computation.2 | async-start | bytes 3670016 | tf_op jit(solution)/shard_map/all_to_all | solution.py:95
  81.3 5.4 %all-gather = bf16[4,4,3584]{2,1,0:T(4,128)(2,1)S(1)} all-gather(bf16[1,4,3584]{2,1,0:T(4,128)(2,1)S(1)} %fusion.57), channel_id=1, replica_groups=mesh['groups'=2,'node'=4,'local'=4] {'local'}, dimensions={0}, use_global_device_ids=true | all-gather | bytes 143360 | tf_op jit(solution)/shard_map/all_gather | solution.py:91
  86.7 22.3 %all-gather.6.cloned.1.call-done = bf16[256,3584]{1,0:T(8,128)(2,1)} async-done(((bf16[256,896]{1,0:T(8,128)(2,1)}), bf16[256,3584]{1,0:T(8,128)(2,1)}) %all-gather.6.cloned.1.call-update) | async-done | bytes 1835024 | tf_op jit(solution)/shard_map/all_gather | solution.py:86
  109.0 2.1 fusion.59
  111.0 52.6 %all-gather.8.cloned.1.call-done = bf16[256,3584]{1,0:T(8,128)(2,1)} async-done(((bf16[256,896]{1,0:T(8,128)(2,1)}), bf16[256,3584]{1,0:T(8,128)(2,1)}) %all-gather.8.cloned.1.call-update) | async-done | bytes 1835024 | tf_op jit(solution)/shard_map/all_gather | solution.py:87
  163.6 41.8 %all-gather.10.cloned.1.call-done = bf16[256,3584]{1,0:T(8,128)(2,1)} async-done(((bf16[256,896]{1,0:T(8,128)(2,1)}), bf16[256,3584]{1,0:T(8,128)(2,1)}) %all-gather.10.cloned.1.call-update) | async-done | bytes 1835024 | tf_op jit(solution)/shard_map/all_gather | solution.py:88
  205.4 3.5 %convolution_convert_fusion.1 = bf16[16,3584]{1,0:T(8,128)(2,1)S(1)} fusion(bf16[256,3584]{1,0:T(8,128)(2,1)} %all-gather.10.cloned.1.call-done, bf16[16,3584]{1,0:T(8,128)(2,1)S(1)} %reshape.67, bf16[256,3584]{1,0:T(8,128)(2,1)} %all-gather.8.cloned.1.call-done, f32[16,256]{1,0:T(8,128)S(1)} %fusion.59), kind=kOutput, calls=%fused_computation.11 | convolution fusion | flops 58802176 | bytes 3915776 | tf_op jit(solution)/shard_map/dot_general | solution.py:15
  209.6 1.2 copy-done.3
  211.5 47.6 %all-reduce.5.cloned.1.call-done = (bf16[4,4,16,3584]{3,2,0,1:T(8,128)(2,1)}, bf16[4,4,3584]{2,1,0:T(4,128)(2,1)}) async-done(((bf16[4,4,16,3584]{3,2,0,1:T(8,128)(2,1)}, bf16[4,4,3584]{2,1,0:T(4,128)(2,1)}), (bf16[4,4,16,3584]{3,2,0,1:T(8,128)(2,1)}, bf16[4,4,3584]{2,1,0:T(4,128)(2,1)})) %all-reduce.5.cloned.1.call-update) | async-done | bytes 1949712
  259.1 1.7 constant_dynamic-slice_fusion
  261.1 2.3 fusion.16
  (51 shorter events, 9.4 us)
Async XLA Ops:
  6.5 2.4 copy-start
  6.5 3.6 %copy-start.5 = (bf16[4,3584]{1,0:T(4,128)(2,1)S(1)}, bf16[4,3584]{1,0:T(4,128)(2,1)}, u32[]{:S(2)}) copy-start(bf16[4,3584]{1,0:T(4,128)(2,1)} %param.11) | copy-start | bytes 86020
  6.5 3.3 %copy-start.7 = (s32[4,8]{1,0:T(4,128)S(1)}, s32[4,8]{1,0:T(4,128)}, u32[]{:S(2)}) copy-start(s32[4,8]{1,0:T(4,128)} %param.14) | copy-start | bytes 388
  6.5 3.6 %copy-start.6 = (f32[3584]{0:T(1024)S(1)}, f32[3584]{0:T(1024)}, u32[]{:S(2)}) copy-start(f32[3584]{0:T(1024)} %param.12) | copy-start | bytes 43012
  6.5 44.9 %all-gather.12.cloned.1.call-start = ((), (), s32[]{:S(2)}) async-start(), calls=%async_computation.6 | async-start | bytes 2293760 | tf_op jit(solution)/shard_map/all_gather | solution.py:75
  31.0 78.0 %all-gather.6.cloned.1.call-start = ((), (), s32[]{:S(2)}) async-start(), calls=%async_computation.3 | async-start | bytes 2293760 | tf_op jit(solution)/shard_map/all_gather | solution.py:86
  31.8 131.9 %all-gather.8.cloned.1.call-start = ((), (), s32[]{:S(2)}) async-start(), calls=%async_computation.4 | async-start | bytes 2293760 | tf_op jit(solution)/shard_map/all_gather | solution.py:87
  33.2 8.7 %all-to-all-start = ((bf16[4,8,2]{1,2,0:T(2,128)(2,1)}), bf16[4,8,2]{1,2,0:T(2,128)(2,1)S(1)}, u32[]{:S(2)}, u32[]{:S(2)}) async-start(bf16[4,8,2]{1,2,0:T(2,128)(2,1)} %copy.42), calls=%async_computation | async-start | bytes 4096 | tf_op jit(solution)/shard_map/all_to_all | solution.py:71
  36.4 169.0 %all-gather.10.cloned.1.call-start = ((), (), s32[]{:S(2)}) async-start(), calls=%async_computation.5 | async-start | bytes 2293760 | tf_op jit(solution)/shard_map/all_gather | solution.py:88
  51.4 10.2 %copy-start.1 = (bf16[8,3584,256]{2,1,0:T(8,128)(2,1)S(1)}, bf16[8,3584,256]{2,1,0:T(8,128)(2,1)}, u32[]{:S(2)}) copy-start(bf16[8,3584,256]{2,1,0:T(8,128)(2,1)} %param.17) | copy-start | bytes 44040196
  51.4 10.8 %copy-start.4 = (bf16[16,8,2,3584]{3,1,2,0:T(8,128)(2,1)S(1)}, bf16[16,8,2,3584]{3,1,2,0:T(8,128)(2,1)}, u32[]{:S(2)}) copy-start(bf16[16,8,2,3584]{3,1,2,0:T(8,128)(2,1)} %all-gather.12.cloned.1.call-done) | copy-start | bytes 5505028
  62.3 5.2 %copy-start.2 = (bf16[8,256,3584]{2,1,0:T(8,128)(2,1)S(1)}, bf16[8,256,3584]{2,1,0:T(8,128)(2,1)}, u32[]{:S(2)}) copy-start(bf16[8,256,3584]{2,1,0:T(8,128)(2,1)} %param.18) | copy-start | bytes 44040196
  76.7 132.9 %all-to-all-start.2 = ((bf16[4,4,16,3584]{3,2,0,1:T(8,128)(2,1)}), bf16[4,4,16,3584]{3,2,0,1:T(8,128)(2,1)S(1)}, u32[]{:S(2)}, u32[]{:S(2)}) async-start(bf16[4,4,16,3584]{3,2,0,1:T(8,128)(2,1)} %copy.49), calls=%async_computation.2 | async-start | bytes 3670016 | tf_op jit(solution)/shard_map/all_to_all | solution.py:95
  81.2 178.0 %all-reduce.5.cloned.1.call-start = ((), (), s32[]{:S(2)}) async-start(), calls=%async_computation.7 | async-start | bytes 3899392
  208.9 2.0 copy-start.8
  209.6 1.2 copy-start.3
Sparse Core Ops, SparseCore 0:
  31.1 20.2 all-gather.11
  53.0 55.8 all-gather.5
  110.6 52.9 all-gather.7
  165.1 40.3 all-gather.9
  211.0 48.1 all-reduce.4
where the time goes:
time: 271 us; the launch traced here: 270 us
  waiting for transfers between devices  175 us (65%)
  blocking collectives  29.7 us (11%)
  matrix products  23.3 us (9%)
  local copies, waits for them, and re-layouts  17.6 us (6%)
  between operations  13.2 us (5%)
  starting transfers between devices  7.88 us (3%)
    all_gather x1, waiting for transfers between devices, local(): lax.all_gather(shared_up, 'node', axis=1, tiled=True)  52.6 us
    unnamed x6, waiting for transfers between devices  49.6 us
    all_gather x1, waiting for transfers between devices, local(): lax.all_gather(shared_down, 'node', axis=1, tiled=True)  41.8 us
    all_gather x1, waiting for transfers between devices, local(): lax.all_gather(shared_gate, 'node', axis=1, tiled=True)  22.3 us
    all_to_all x1, blocking collectives, local(): lax.all_to_all(send_rows, 'node', split_axis=0, concat_axis=0, tiled=True)  19.2 us
    dot_general x1, matrix products, local(): jnp.einsum('necd,edf->necf', row_block, expert_gate, preferred_element_ty...  8.6 us
    unnamed x21, local copies, waits for them, and re-layouts  8.38 us
  transfers between devices with their start and end apart: 7, of which 6 were waited for; matrix products, arithmetic and copies ran while one was open for 10% of the time, Pallas kernels for 0%

commit v1 on v0

v1 whole, which is shorter than its diff:
```python
import jax
import jax.numpy as jnp
from jax import lax
from jax.sharding import PartitionSpec as P

NODE_GROUPS = 8


def local(
    hidden_states,
    norm_gain,
    route_groups,
    route_picks,
    gate_weights,
    expert_gate,
    expert_up,
    expert_down,
    shared_gate,
    shared_up,
    shared_down,
):
    node_count = lax.axis_size("node")
    local_count = lax.axis_size("local")
    node = lax.axis_index("node")
    token_count, feature_count = hidden_states.shape
    held, _, block = expert_gate.shape
    expert_total = held * node_count
    per_group = expert_total // NODE_GROUPS
    features = hidden_states.astype(jnp.float32)
    mean_square = jnp.mean(features * features, axis=1, keepdims=True)
    normed = (features * lax.rsqrt(mean_square + 1e-06) * norm_gain[None, :]).astype(jnp.bfloat16)
    group_pick = jnp.take_along_axis(route_groups, route_picks // per_group, axis=1)
    expert_ids = group_pick * per_group + route_picks % per_group
    hits = expert_ids[:, :, None] == jnp.arange(expert_total, dtype=jnp.int32)[None, None, :]
    token_weight = jnp.sum(
        jnp.where(hits, gate_weights.astype(jnp.float32)[:, :, None], 0.0), axis=1
    ).astype(jnp.bfloat16)
    packed = jnp.concatenate([normed, token_weight], axis=1)
    gathered = lax.all_gather(packed, ("node", "local"), axis=0, tiled=True)
    rows = gathered[:, :feature_count]
    weights = lax.dynamic_slice_in_dim(gathered, feature_count + node * held, held, axis=1)
    weights = weights.astype(jnp.float32)
    slab = shared_gate.shape[1]
    mine = lax.dynamic_slice_in_dim(rows, node * slab, slab, axis=1)
    contract = (((1,), (1,)), ((), ()))
    shared_parts = jnp.concatenate(
        [
            lax.dot_general(mine, shared_gate, contract, preferred_element_type=jnp.float32),
            lax.dot_general(mine, shared_up, contract, preferred_element_type=jnp.float32),
        ],
        axis=1,
    )
    shared_parts = lax.all_gather(shared_parts.astype(jnp.bfloat16), "node", axis=0, tiled=False)
    shared_in = jnp.sum(shared_parts.astype(jnp.float32), axis=0)
    shared_block = shared_gate.shape[0]
    shared_hidden = (
        jax.nn.silu(shared_in[:, :shared_block]) * shared_in[:, shared_block:]
    ).astype(jnp.bfloat16)
    hidden = []
    for e in range(held):
        gate_part = jnp.dot(rows, expert_gate[e], preferred_element_type=jnp.float32)
        up_part = jnp.dot(rows, expert_up[e], preferred_element_type=jnp.float32)
        hidden.append(
            (jax.nn.silu(gate_part) * up_part * weights[:, e : e + 1]).astype(jnp.bfloat16)
        )
    hidden = jnp.concatenate(hidden, axis=1)
    partial = jnp.dot(
        hidden,
        expert_down.reshape(held * block, feature_count),
        preferred_element_type=jnp.float32,
    )
    shared_partial = jnp.dot(shared_hidden, shared_down, preferred_element_type=jnp.float32)
    current = lax.dynamic_slice_in_dim(partial, node * slab, slab, axis=1)
    partial = lax.dynamic_update_slice_in_dim(
        partial, current + shared_partial, node * slab, axis=1
    ).astype(jnp.bfloat16)
    stack = partial.reshape(node_count * local_count, token_count, feature_count)
    returned = lax.all_to_all(stack, ("node", "local"), split_axis=0, concat_axis=0, tiled=True)
    return jnp.sum(returned.astype(jnp.float32), axis=0).astype(jnp.bfloat16)


def solution(mesh):
    placed = (
        P(("groups", "node", "local"), None),
        P(),
        P(("groups", "node", "local"), None),
        P(("groups", "node", "local"), None),
        P(("groups", "node", "local"), None),
        P("node", None, "local"),
        P("node", None, "local"),
        P("node", "local", None),
        P("local", "node"),
        P("local", "node"),
        P("local", "node"),
    )
    return jax.shard_map(
        local,
        mesh=mesh,
        in_specs=placed,
        out_specs=P(("groups", "node", "local"), None),
        check_vma=False,
    )
```

time: 271 us -> 105 us (0.39)
  waiting for transfers between devices: 175 us -> 0 us
  blocking collectives: 29.7 us -> 54.7 us
  matrix products: 23.3 us -> 42.1 us
  local copies, waits for them, and re-layouts: 17.6 us -> 2.16 us
  between operations: 13.2 us -> 0.2 us
  starting transfers between devices: 7.88 us -> 0 us
    all_gather x4 -> x0, waiting for transfers between devices: 121 us -> none  [the longest x1 52.6 us: local(): lax.all_gather(shared_up, 'node', axis=1, tiled=True)]
    unnamed x6 -> x0, waiting for transfers between devices: 49.6 us -> none
    all_gather x2, blocking collectives: 10.5 us -> 38.8 us  [the longest x1 24.4 us: local(): gathered = lax.all_gather(packed, ('node', 'local'), axis=0, tiled=True)]
    dot_general x7 -> x20, matrix products: 23.3 us -> 42.1 us  [the longest x8 20.6 us: local(): jnp.dot(rows, expert_gate[e], preferred_element_type=jnp.float32)]
    unnamed x21 -> x18, local copies, waits for them, and re-layouts: 8.38 us -> 0.33 us
    all_to_all x2 -> x0, starting transfers between devices: 7.72 us -> none  [the longest x1 4.5 us: local(): lax.all_to_all(grid, 'node', split_axis=1, concat_axis=1, tiled=True)]
    reshape x5 -> x1, local copies, waits for them, and re-layouts: 7.09 us -> 0.11 us  [local(): partial.reshape(node_count * local_count, token_count, feature_count)]
    all_to_all x2 -> x0, waiting for transfers between devices: 4.86 us -> none  [the longest x1 4.86 us: local(): lax.all_to_all(slot_weight, 'node', split_axis=0, concat_axis=0, tiled=True)]
  transfers between devices with their start and end apart: 7 -> 0, of which waited for: 6 -> 0; matrix products, arithmetic and copies ran while one was open for 10% -> 0% of each run, Pallas kernels for 0% -> 0%
where the time goes in v1:
time: 105 us; the launch traced here: 104 us
  blocking collectives  54.7 us (52%)
  matrix products  42.1 us (40%)
  other arithmetic  4.88 us (5%)
  local copies, waits for them, and re-layouts  2.16 us (2%)
    all_gather x1, blocking collectives, local(): gathered = lax.all_gather(packed, ('node', 'local'), axis=0, tiled=True)  24.4 us
    dot_general x8, matrix products, local(): jnp.dot(rows, expert_gate[e], preferred_element_type=jnp.float32)  20.6 us
    dot_general x8, matrix products, local(): up_part = jnp.dot(rows, expert_up[e], preferred_element_type=jnp.float32)  16 us
    all_to_all x1, blocking collectives, local(): lax.all_to_all(stack, ('node', 'local'), split_axis=0, concat_axis=0, til...  15.9 us
    all_gather x1, blocking collectives, local(): lax.all_gather(shared_parts.astype(jnp.bfloat16), 'node', axis=0, tiled=F...  14.4 us
    dot_general x1, matrix products, local(): jnp.dot(hidden, expert_down.reshape(held * block, feature_count), preferr...  2.62 us

profile of v1, /device:TPU:0, one launch (start us, length us, event | category | flops | bytes accessed | tf_op | source)
XLA Modules:
  0.0 104.1 jit_solution(8776455362678934410)
XLA Ops:
  0.0 0.9 fusion.150
  2.4 1.4 %gather_fusion = s32[32]{0:T(128)S(1)} fusion(s32[4,4]{1,0:T(4,128)} %param.13, s32[32]{0:T(128)S(1)} %reshape.60), kind=kCustom, calls=%fused_computation | custom fusion | bytes 512 | tf_op jit(solution)/shard_map/jit(take_along_axis)/gather | solution.py:32
  5.6 24.4 %all-gather = bf16[16,4,3616]{2,1,0:T(4,128)(2,1)S(1)} all-gather(bf16[1,4,3616]{2,1,0:T(4,128)(2,1)S(1)} %maximum_bitcast_fusion), channel_id=1, replica_groups=mesh['groups'=2,'node'=4,'local'=4] {'node','local'}, dimensions={0}, use_global_device_ids=true | all-gather | bytes 491776 | tf_op jit(solution)/shard_map/all_gather | solution.py:39
  30.2 2.6 %fusion.30 = f32[64,256]{1,0:T(8,128)} fusion(bf16[8,3584,256]{2,1,0:T(8,128)(2,1)} %param.16, bf16[64,3616]{1,0:T(8,128)(2,1)S(1)} %reshape.72), kind=kOutput, calls=%fused_computation.31 | convolution fusion | flops 117440512 | bytes 2359296 | tf_op jit(solution)/shard_map/dot_general | solution.py:61
  32.8 2.6 %fusion.26 = f32[64,256]{1,0:T(8,128)} fusion(bf16[8,3584,256]{2,1,0:T(8,128)(2,1)} %param.16, bf16[64,3616]{1,0:T(8,128)(2,1)S(1)} %reshape.72), kind=kOutput, calls=%fused_computation.27 | convolution fusion | flops 117440512 | bytes 2359296 | tf_op jit(solution)/shard_map/dot_general | solution.py:61
  35.3 2.6 %fusion.22 = f32[64,256]{1,0:T(8,128)} fusion(bf16[8,3584,256]{2,1,0:T(8,128)(2,1)} %param.16, bf16[64,3616]{1,0:T(8,128)(2,1)S(1)} %reshape.72), kind=kOutput, calls=%fused_computation.23 | convolution fusion | flops 117440512 | bytes 2359296 | tf_op jit(solution)/shard_map/dot_general | solution.py:61
  37.9 2.6 %fusion.18 = f32[64,256]{1,0:T(8,128)} fusion(bf16[8,3584,256]{2,1,0:T(8,128)(2,1)} %param.16, bf16[64,3616]{1,0:T(8,128)(2,1)S(1)} %reshape.72), kind=kOutput, calls=%fused_computation.19 | convolution fusion | flops 117440512 | bytes 2359296 | tf_op jit(solution)/shard_map/dot_general | solution.py:61
  40.5 2.6 %fusion.14 = f32[64,256]{1,0:T(8,128)} fusion(bf16[8,3584,256]{2,1,0:T(8,128)(2,1)} %param.16, bf16[64,3616]{1,0:T(8,128)(2,1)S(1)} %reshape.72), kind=kOutput, calls=%fused_computation.15 | convolution fusion | flops 117440512 | bytes 2359296 | tf_op jit(solution)/shard_map/dot_general | solution.py:61
  43.0 2.6 %fusion.10 = f32[64,256]{1,0:T(8,128)} fusion(bf16[8,3584,256]{2,1,0:T(8,128)(2,1)} %param.16, bf16[64,3616]{1,0:T(8,128)(2,1)S(1)} %reshape.72), kind=kOutput, calls=%fused_computation.11 | convolution fusion | flops 117440512 | bytes 2359296 | tf_op jit(solution)/shard_map/dot_general | solution.py:61
  45.6 2.6 %fusion.6 = f32[64,256]{1,0:T(8,128)} fusion(bf16[8,3584,256]{2,1,0:T(8,128)(2,1)} %param.16, bf16[64,3616]{1,0:T(8,128)(2,1)S(1)} %reshape.72), kind=kOutput, calls=%fused_computation.7 | convolution fusion | flops 117440512 | bytes 2359296 | tf_op jit(solution)/shard_map/dot_general | solution.py:61
  48.1 2.7 %fusion.2 = f32[64,256]{1,0:T(8,128)} fusion(bf16[8,3584,256]{2,1,0:T(8,128)(2,1)} %param.16, bf16[64,3616]{1,0:T(8,128)(2,1)S(1)} %reshape.72), kind=kOutput, calls=%fused_computation.3 | convolution fusion | flops 117440512 | bytes 2359296 | tf_op jit(solution)/shard_map/dot_general | solution.py:61
  51.1 1.3 %fusion.146 = bf16[1,64,256]{2,1,0:T(8,128)(2,1)S(1)} fusion(bf16[256,896]{1,0:T(8,128)(2,1)} %param.20, bf16[64,3584]{1,0:T(8,128)(2,1)S(1)} %slice.110, s32[]{:T(128)S(6)} %select_n.38), kind=kOutput, calls=%fused_computation.86 | convolution fusion | flops 29376512 | bytes 606212 | tf_op jit(solution)/shard_map/dot_general | solution.py:49
  52.4 1.3 %fusion.145 = bf16[1,64,256]{2,1,0:T(8,128)(2,1)S(1)} fusion(bf16[256,896]{1,0:T(8,128)(2,1)} %param.19, bf16[64,3584]{1,0:T(8,128)(2,1)S(1)} %slice.110, s32[]{:T(128)S(6)} %select_n.38), kind=kOutput, calls=%fused_computation.85 | convolution fusion | flops 29376512 | bytes 606212 | tf_op jit(solution)/shard_map/dot_general | solution.py:48
  53.8 14.4 %all_gather.8 = bf16[4,64,512]{2,1,0:T(8,128)(2,1)S(1)} all-gather(bf16[1,64,512]{2,1,0:T(8,128)(2,1)S(1)} %pad_maximum_fusion), channel_id=1, replica_groups=mesh['groups'=2,'node'=4,'local'=4] {'node'}, dimensions={0}, use_global_device_ids=true | all-gather | bytes 327680 | tf_op jit(solution)/shard_map/all_gather | solution.py:53
  68.2 2.1 %fusion.142 = bf16[64,2048]{1,0:T(8,128)(2,1)S(1)} fusion(bf16[8,3584,256]{2,1,0:T(8,128)(2,1)} %param.17, f32[64,256]{1,0:T(8,128)} %fusion.30, f32[64]{0:T(128)S(1)} %get-tuple-element.12, bf16[64,3616]{1,0:T(8,128)(2,1)S(1)} %reshape.72), kind=kOutput, calls=%fused_computation.82 | convolution fusion | flops 117555200 | bytes 2392576 | tf_op jit(solution)/shard_map/dot_general | solution.py:62
  70.3 2.0 %fusion.136 = bf16[64,2048]{1,0:T(8,128)(2,1)S(1)} fusion(bf16[64,2048]{1,0:T(8,128)(2,1)S(1)} %fusion.142, bf16[8,3584,256]{2,1,0:T(8,128)(2,1)} %param.17, f32[64,256]{1,0:T(8,128)} %fusion.26, f32[64]{0:T(128)S(1)} %get-tuple-element.11, bf16[64,3616]{1,0:T(8,128)(2,1)S(1)} %reshape.72), kind=kOutput, calls=%fused_computation.80 | convolution fusion | flops 117555200 | bytes 2392576 | tf_op jit(solution)/shard_map/dot_general | solution.py:62
  72.3 2.0 %fusion.130 = bf16[64,2048]{1,0:T(8,128)(2,1)S(1)} fusion(bf16[64,2048]{1,0:T(8,128)(2,1)S(1)} %fusion.136, bf16[8,3584,256]{2,1,0:T(8,128)(2,1)} %param.17, f32[64,256]{1,0:T(8,128)} %fusion.22, f32[64]{0:T(128)S(1)} %get-tuple-element.10, bf16[64,3616]{1,0:T(8,128)(2,1)S(1)} %reshape.72), kind=kOutput, calls=%fused_computation.78 | convolution fusion | flops 117555200 | bytes 2392576 | tf_op jit(solution)/shard_map/dot_general | solution.py:62
  74.2 2.1 %fusion.124 = bf16[64,2048]{1,0:T(8,128)(2,1)S(1)} fusion(bf16[64,2048]{1,0:T(8,128)(2,1)S(1)} %fusion.130, bf16[8,3584,256]{2,1,0:T(8,128)(2,1)} %param.17, f32[64,256]{1,0:T(8,128)} %fusion.18, f32[64]{0:T(128)S(1)} %get-tuple-element.9, bf16[64,3616]{1,0:T(8,128)(2,1)S(1)} %reshape.72), kind=kOutput, calls=%fused_computation.76 | convolution fusion | flops 117555200 | bytes 2392576 | tf_op jit(solution)/shard_map/dot_general | solution.py:62
  76.3 2.0 %fusion.118 = bf16[64,2048]{1,0:T(8,128)(2,1)S(1)} fusion(bf16[64,2048]{1,0:T(8,128)(2,1)S(1)} %fusion.124, bf16[8,3584,256]{2,1,0:T(8,128)(2,1)} %param.17, f32[64,256]{1,0:T(8,128)} %fusion.14, f32[64]{0:T(128)S(1)} %get-tuple-element.8, bf16[64,3616]{1,0:T(8,128)(2,1)S(1)} %reshape.72), kind=kOutput, calls=%fused_computation.74 | convolution fusion | flops 117555200 | bytes 2392576 | tf_op jit(solution)/shard_map/dot_general | solution.py:62
  78.3 2.1 %fusion.112 = bf16[64,2048]{1,0:T(8,128)(2,1)S(1)} fusion(bf16[64,2048]{1,0:T(8,128)(2,1)S(1)} %fusion.118, bf16[8,3584,256]{2,1,0:T(8,128)(2,1)} %param.17, f32[64,256]{1,0:T(8,128)S(1)} %copy-done.3, f32[64]{0:T(128)S(1)} %get-tuple-element.7, bf16[64,3616]{1,0:T(8,128)(2,1)S(1)} %reshape.72), kind=kOutput, calls=%fused_computation.72 | convolution fusion | flops 117555200 | bytes 2392576 | tf_op jit(solution)/shard_map/dot_general | solution.py:62
  80.4 1.9 %fusion.106 = bf16[64,2048]{1,0:T(8,128)(2,1)S(1)} fusion(bf16[64,2048]{1,0:T(8,128)(2,1)S(1)} %fusion.112, bf16[8,3584,256]{2,1,0:T(8,128)(2,1)} %param.17, f32[64,256]{1,0:T(8,128)S(1)} %copy-done.2, f32[64]{0:T(128)S(1)} %get-tuple-element.6, bf16[64,3616]{1,0:T(8,128)(2,1)S(1)} %reshape.72), kind=kOutput, calls=%fused_computation.70 | convolution fusion | flops 117555200 | bytes 2392576 | tf_op jit(solution)/shard_map/dot_general | solution.py:62
  82.4 1.9 %fusion.100 = bf16[64,2048]{1,0:T(8,128)(2,1)S(1)} fusion(bf16[64,2048]{1,0:T(8,128)(2,1)S(1)} %fusion.106, bf16[8,3584,256]{2,1,0:T(8,128)(2,1)} %param.17, f32[64,256]{1,0:T(8,128)S(1)} %copy-done.1, f32[64]{0:T(128)S(1)} %get-tuple-element.5, bf16[64,3616]{1,0:T(8,128)(2,1)S(1)} %reshape.72), kind=kOutput, calls=%fused_computation.68 | convolution fusion | flops 117555200 | bytes 2392576 | tf_op jit(solution)/shard_map/dot_general | solution.py:62
  84.4 2.6 %fusion.176 = f32[64,3584]{1,0:T(8,128)S(1)} fusion(bf16[64,2048]{1,0:T(8,128)(2,1)S(1)} %fusion.100, bf16[2048,3584]{1,0:T(8,128)(2,1)S(1)} %bitcast.146), kind=kOutput, calls=%fused_computation.142 | convolution fusion | flops 939524096 | bytes 15859712 | tf_op jit(solution)/shard_map/dot_general | solution.py:67
  87.4 15.9 %all_to_all.5 = bf16[16,4,3584]{2,1,0:T(4,128)(2,1)S(1)} all-to-all(bf16[16,4,3584]{2,1,0:T(4,128)(2,1)S(1)} %reshape.59), channel_id=1, replica_groups=mesh['groups'=2,'node'=4,'local'=4] {'node','local'}, dimensions={0} | all-to-all | bytes 917504 | tf_op jit(solution)/shard_map/all_to_all | solution.py:78
  (38 shorter events, 4.9 us)
Async XLA Ops:
  0.0 87.0 %copy-start = (bf16[256,896]{1,0:T(8,128)(2,1)S(1)}, bf16[256,896]{1,0:T(8,128)(2,1)}, u32[]{:S(2)}) copy-start(bf16[256,896]{1,0:T(8,128)(2,1)} %param.21) | copy-start | bytes 1376260
  48.1 36.2 %slice-start = ((s8[14680064]{0:T(1024)(128)(4,1)}), s8[2097152]{0:T(1024)(128)(4,1)S(1)}, s32[]{:S(2)}) async-start(s8[14680064]{0:T(1024)(128)(4,1)} %bitcast.144), calls=%async_computation.1 | async-start | bytes 4194304
  51.1 27.2 %copy-start.3 = (f32[64,256]{1,0:T(8,128)S(1)}, f32[64,256]{1,0:T(8,128)}, u32[]{:S(2)}) copy-start(f32[64,256]{1,0:T(8,128)} %fusion.10) | copy-start | bytes 196612
  51.1 29.3 %copy-start.2 = (f32[64,256]{1,0:T(8,128)S(1)}, f32[64,256]{1,0:T(8,128)}, u32[]{:S(2)}) copy-start(f32[64,256]{1,0:T(8,128)} %fusion.6) | copy-start | bytes 196612
  51.1 31.3 %copy-start.1 = (f32[64,256]{1,0:T(8,128)S(1)}, f32[64,256]{1,0:T(8,128)}, u32[]{:S(2)}) copy-start(f32[64,256]{1,0:T(8,128)} %fusion.2) | copy-start | bytes 196612
  68.2 16.1 %slice-start.1 = ((s8[14680064]{0:T(1024)(128)(4,1)}), s8[4194304]{0:T(1024)(128)(4,1)S(1)}, s32[]{:S(2)}) async-start(s8[14680064]{0:T(1024)(128)(4,1)} %bitcast.144), calls=%async_computation.2 | async-start | bytes 8388608
  74.2 10.1 %slice-start.2 = ((s8[14680064]{0:T(1024)(128)(4,1)}), s8[4194304]{0:T(1024)(128)(4,1)S(1)}, s32[]{:S(2)}) async-start(s8[14680064]{0:T(1024)(128)(4,1)} %bitcast.144), calls=%async_computation.3 | async-start | bytes 8388608
  78.3 6.0 %slice-start.3 = ((s8[14680064]{0:T(1024)(128)(4,1)}), s8[4194304]{0:T(1024)(128)(4,1)S(1)}, s32[]{:S(2)}) async-start(s8[14680064]{0:T(1024)(128)(4,1)} %bitcast.144), calls=%async_computation.4 | async-start | bytes 8388608

commit v2 on v1

v2 whole, which is shorter than its diff:
```python
import functools

import jax
import jax.numpy as jnp
from jax import lax
from jax.experimental import pallas as pl
from jax.experimental.pallas import tpu as pltpu
from jax.sharding import PartitionSpec as P

NODE_GROUPS = 8
LANES = 128
VMEM_BYTES = 56 * 2**20


def pack_kernel(per_group, x_ref, gain_ref, groups_ref, picks_ref, weight_ref, out_ref):
    features = x_ref[...].astype(jnp.float32)
    count = features.shape[1]
    mean_square = jnp.mean(features * features, axis=1, keepdims=True)
    normed = features * lax.rsqrt(mean_square + 1e-06) * gain_ref[...]
    out_ref[:, :count] = normed.astype(jnp.bfloat16)
    picks = picks_ref[...]
    groups = groups_ref[...]
    weight = weight_ref[...].astype(jnp.float32)
    slot = lax.div(picks, jnp.full_like(picks, per_group))
    inner = picks - slot * per_group
    group = jnp.zeros_like(picks)
    for a in range(groups.shape[1]):
        group = jnp.where(slot == a, groups[:, a : a + 1], group)
    ids = group * per_group + inner
    width = out_ref.shape[1] - count
    lane = lax.broadcasted_iota(jnp.int32, (picks.shape[0], width), 1)
    total = jnp.zeros((picks.shape[0], width), jnp.float32)
    for k in range(picks.shape[1]):
        total = total + jnp.where(ids[:, k : k + 1] == lane, weight[:, k : k + 1], 0.0)
    out_ref[:, count:] = total.astype(jnp.bfloat16)


def shared_in_kernel(start_ref, x_ref, gate_ref, up_ref, out_ref):
    contract = (((1,), (1,)), ((), ()))
    block, slab = gate_ref.shape
    x = x_ref[...]
    if x.shape[1] != slab:
        x = x_ref[:, pl.ds(pl.multiple_of(start_ref[0], LANES), slab)]
    for i, ref in enumerate((gate_ref, up_ref)):
        part = lax.dot_general(x, ref[...], contract, preferred_element_type=jnp.float32)
        out_ref[:, i * block : (i + 1) * block] = part.astype(jnp.bfloat16)


def hidden_kernel(first_ref, x_ref, gate_ref, up_ref, out_ref):
    count = gate_ref.shape[1]
    x = x_ref[:, :count]
    gate = jnp.dot(x, gate_ref[0], preferred_element_type=jnp.float32)
    up = jnp.dot(x, up_ref[0], preferred_element_type=jnp.float32)
    weight = x_ref[:, count:].astype(jnp.float32)
    lane = lax.broadcasted_iota(jnp.int32, weight.shape, 1)
    chosen = first_ref[0] + pl.program_id(0)
    weight = jnp.sum(jnp.where(lane == chosen, weight, 0.0), axis=1, keepdims=True)
    out_ref[...] = (jax.nn.silu(gate) * up * weight).astype(jnp.bfloat16)


def down_kernel(tokens, start_ref, hidden_ref, down_ref, shared_down_ref, *refs):
    parts, out_ref, acc = refs[:-2], refs[-2], refs[-1]
    step = pl.program_id(0)
    term = jnp.dot(hidden_ref[...], down_ref[0], preferred_element_type=jnp.float32)

    @pl.when(step == 0)
    def _():
        acc[...] = term

    @pl.when(step > 0)
    def _():
        acc[...] += term

    @pl.when(step == pl.num_programs(0) - 1)
    def _():
        block, slab = shared_down_ref.shape
        count = out_ref.shape[0]
        total = parts[0][...].astype(jnp.float32)
        to = lax.broadcasted_iota(jnp.int32, (count, count), 0)
        come = lax.broadcasted_iota(jnp.int32, (count, count), 1)
        for k in range(1, len(parts)):
            place = (come == (to ^ (k * tokens))).astype(jnp.bfloat16)
            total += jnp.dot(place, parts[k][...], preferred_element_type=jnp.float32)
        hidden = (jax.nn.silu(total[:, :block]) * total[:, block:]).astype(jnp.bfloat16)
        shared = jnp.dot(hidden, shared_down_ref[...], preferred_element_type=jnp.float32)
        if slab == out_ref.shape[1]:
            acc[...] += shared
        else:
            acc[:, pl.ds(pl.multiple_of(start_ref[0], LANES), slab)] += shared
        out_ref[...] = acc[...].astype(jnp.bfloat16)


def exchange(value, axis, bit):
    size = lax.axis_size(axis)
    return lax.ppermute(value, axis, [(i, i ^ bit) for i in range(size)])


def add_rows(one, other):
    return (one.astype(jnp.float32) + other.astype(jnp.float32)).astype(jnp.bfloat16)


def local(
    hidden_states,
    norm_gain,
    route_groups,
    route_picks,
    gate_weights,
    expert_gate,
    expert_up,
    expert_down,
    shared_gate,
    shared_up,
    shared_down,
):
    node_count = lax.axis_size("node")
    local_count = lax.axis_size("local")
    node = lax.axis_index("node")
    token_count, feature_count = hidden_states.shape
    held, _, block = expert_gate.shape
    expert_total = held * node_count
    per_group = expert_total // NODE_GROUPS
    width = feature_count + -(-expert_total // LANES) * LANES
    slab = shared_gate.shape[1]
    shared_block = shared_gate.shape[0]
    params = pltpu.CompilerParams(vmem_limit_bytes=VMEM_BYTES)

    rows = pl.pallas_call(
        functools.partial(pack_kernel, per_group),
        out_shape=jax.ShapeDtypeStruct((token_count, width), jnp.bfloat16),
    )(hidden_states, norm_gain.reshape(1, -1), route_groups, route_picks, gate_weights)

    bit = 1
    while bit < node_count:
        rows = jnp.concatenate([rows, exchange(rows, "node", bit)], axis=0)
        bit *= 2
    bit = local_count // 2
    while bit:
        rows = jnp.concatenate([rows, exchange(rows, "local", bit)], axis=0)
        bit //= 2
    row_count = rows.shape[0]

    start = (node * slab).astype(jnp.int32)
    aligned = slab % LANES == 0
    smem = pl.BlockSpec(memory_space=pltpu.SMEM)
    vmem = pl.BlockSpec(memory_space=pltpu.VMEM)
    mine = rows if aligned else lax.dynamic_slice_in_dim(rows, start, slab, axis=1)
    shared_part = pl.pallas_call(
        shared_in_kernel,
        out_shape=jax.ShapeDtypeStruct((row_count, 2 * shared_block), jnp.bfloat16),
        in_specs=[smem, vmem, vmem, vmem],
        compiler_params=params,
    )(start.reshape(1), mine, shared_gate, shared_up)
    parts = [shared_part] + [exchange(shared_part, "node", k) for k in range(1, node_count)]

    hidden = pl.pallas_call(
        hidden_kernel,
        grid=(held,),
        out_shape=jax.ShapeDtypeStruct((row_count, held * block), jnp.bfloat16),
        in_specs=[
            smem,
            vmem,
            pl.BlockSpec((1, feature_count, block), lambda e: (e, 0, 0)),
            pl.BlockSpec((1, feature_count, block), lambda e: (e, 0, 0)),
        ],
        out_specs=pl.BlockSpec((row_count, block), lambda e: (0, e)),
        compiler_params=params,
    )((node * held).astype(jnp.int32).reshape(1), rows, expert_gate, expert_up)

    if not aligned:
        shared_down = lax.dynamic_update_slice_in_dim(
            jnp.zeros((shared_block, feature_count), shared_down.dtype), shared_down, start, axis=1
        )
    out = pl.pallas_call(
        functools.partial(down_kernel, token_count),
        grid=(held,),
        out_shape=jax.ShapeDtypeStruct((row_count, feature_count), jnp.bfloat16),
        in_specs=[
            smem,
            pl.BlockSpec((row_count, block), lambda e: (0, e)),
            pl.BlockSpec((1, block, feature_count), lambda e: (e, 0, 0)),
            vmem,
        ]
        + [vmem] * node_count,
        out_specs=vmem,
        scratch_shapes=[pltpu.VMEM((row_count, feature_count), jnp.float32)],
        compiler_params=params,
    )(start.reshape(1), hidden, expert_down, shared_down, *parts)

    bit = 1
    while bit < local_count:
        half = out.shape[0] // 2
        out = add_rows(out[:half], exchange(out[half:], "local", bit))
        bit *= 2
    bit = node_count // 2
    while bit:
        half = out.shape[0] // 2
        out = add_rows(out[:half], exchange(out[half:], "node", bit))
        bit //= 2
    return out


def solution(mesh):
    placed = (
        P(("groups", "node", "local"), None),
        P(),
        P(("groups", "node", "local"), None),
        P(("groups", "node", "local"), None),
        P(("groups", "node", "local"), None),
        P("node", None, "local"),
        P("node", None, "local"),
        P("node", "local", None),
        P("local", "node"),
        P("local", "node"),
        P("local", "node"),
    )
    return jax.shard_map(
        local,
        mesh=mesh,
        in_specs=placed,
        out_specs=P(("groups", "node", "local"), None),
        check_vma=False,
    )
```

time: 105 us -> 78 us (0.74)
  blocking collectives: 54.7 us -> 0 us
  matrix products: 42.1 us -> 0 us
  Pallas kernels: 0 us -> 28.3 us
  waiting for transfers between devices: 0 us -> 19.3 us
  starting transfers between devices: 0 us -> 18.6 us
  local copies, waits for them, and re-layouts: 2.16 us -> 7.01 us
    dot_general x20 -> x0, matrix products: 42.1 us -> none  [the longest x8 20.6 us: local(): jnp.dot(rows, expert_gate[e], preferred_element_type=jnp.float32)]
    all_gather x2 -> x0, blocking collectives: 38.8 us -> none  [the longest x1 24.4 us: local(): gathered = lax.all_gather(packed, ('node', 'local'), axis=0, tiled=True)]
    pallas_call x0 -> x4, Pallas kernels: none -> 28.3 us  [the longest x1 13.8 us: local(): pl.pallas_call(hidden_kernel, grid=(held,), out_shape=jax.ShapeDtypeStruc...]
    ppermute x0 -> x11, waiting for transfers between devices: none -> 19.3 us  [exchange(): return lax.ppermute(value, axis, [(i, i ^ bit) for i in range(size)])]
    ppermute x0 -> x11, starting transfers between devices: none -> 18.6 us  [exchange(): return lax.ppermute(value, axis, [(i, i ^ bit) for i in range(size)])]
    all_to_all x1 -> x0, blocking collectives: 15.9 us -> none  [local(): lax.all_to_all(stack, ('node', 'local'), split_axis=0, concat_axis=0, til...]
    concatenate x0 -> x1, local copies, waits for them, and re-layouts: none -> 3.46 us  [local(): rows = jnp.concatenate([rows, exchange(rows, 'local', bit)], axis=0)]
    concatenate x1 -> x3, other arithmetic: 0.01 us -> 2.39 us  [the longest x2 1.59 us: local(): rows = jnp.concatenate([rows, exchange(rows, 'node', bit)], axis=0)]
  transfers between devices with their start and end apart: 0 -> 11, of which waited for: 0 -> 8; matrix products, arithmetic and copies ran while one was open for 0% -> 0% of each run, Pallas kernels for 0% -> 18%
where the time goes in v2:
time: 78 us; the launch traced here: 77.3 us
  Pallas kernels  28.3 us (36%)
  waiting for transfers between devices  19.3 us (25%)
  starting transfers between devices  18.6 us (24%)
  local copies, waits for them, and re-layouts  7.01 us (9%)
  other arithmetic  4.07 us (5%)
    ppermute x11, waiting for transfers between devices, exchange(): return lax.ppermute(value, axis, [(i, i ^ bit) for i in range(size)])  19.3 us
    ppermute x11, starting transfers between devices, exchange(): return lax.ppermute(value, axis, [(i, i ^ bit) for i in range(size)])  18.6 us
    pallas_call x1, Pallas kernels, local(): pl.pallas_call(hidden_kernel, grid=(held,), out_shape=jax.ShapeDtypeStruc...  13.8 us
    pallas_call x1, Pallas kernels, local(): pl.pallas_call(functools.partial(down_kernel, token_count), grid=(held,),...  10.6 us
    concatenate x1, local copies, waits for them, and re-layouts, local(): rows = jnp.concatenate([rows, exchange(rows, 'local', bit)], axis=0)  3.46 us
    pallas_call x1, Pallas kernels, local(): pl.pallas_call(shared_in_kernel, out_shape=jax.ShapeDtypeStruct((row_coun...  2.32 us
    convert_element_type x4, other arithmetic, add_rows(): (one.astype(jnp.float32) + other.astype(jnp.float32)).astype(jnp.bfloat16)  1.68 us
    concatenate x2, other arithmetic, local(): rows = jnp.concatenate([rows, exchange(rows, 'node', bit)], axis=0)  1.59 us
  transfers between devices with their start and end apart: 11, of which 8 were waited for; matrix products, arithmetic and copies ran while one was open for 0% of the time, Pallas kernels for 18%

profile of v2, /device:TPU:0, one launch (start us, length us, event | category | flops | bytes accessed | tf_op | source)
XLA Modules:
  0.0 77.3 jit_solution(5285052534047889805)
XLA Ops:
  0.0 1.3 %reshape.12.gain_ref = f32[1,3584]{1,0:T(1,128)} reshape(f32[3584]{0:T(1024)} %param.12) | data formatting | bytes 28672 | tf_op jit(solution)/shard_map/reshape | solution.py:130
  1.3 1.5 %shard_map.109 = bf16[4,3712]{1,0:T(4,128)(2,1)} custom-call(bf16[4,3584]{1,0:T(4,128)(2,1)} %x_ref.1, f32[1,3584]{1,0:T(1,128)} %reshape.12.gain_ref, s32[4,4]{1,0:T(4,128)} %groups_ref.1, s32[4,8]{1,0:T(4,128)} %picks_ref.1, bf16[4,8]{1,0:T(4,128)(2,1)} %weight_ref.1), custom_call_target="tpu_custom_call" | custom-call | tf_op jit(solution)/shard_map/pallas_call | solution.py:127
  2.9 3.0 %collective-permute-start = (bf16[4,3712]{1,0:T(4,128)(2,1)}, bf16[4,3712]{1,0:T(4,128)(2,1)S(1)}, u32[]{:S(2)}, u32[]{:S(2)}) collective-permute-start(bf16[4,3712]{1,0:T(4,128)(2,1)} %shard_map.109), channel_id=1, source_target_pairs={{0,4},{4,0},{8,12},{12,8},{1,5},{5,1},{9,13},{13,9},{2,6},{6,2},{1... | collective-permute-start | bytes 89096 | tf_op jit(solution)/shard_map/ppermute | solution.py:95
  5.9 2.1 %collective-permute-done = bf16[4,3712]{1,0:T(4,128)(2,1)S(1)} collective-permute-done((bf16[4,3712]{1,0:T(4,128)(2,1)}, bf16[4,3712]{1,0:T(4,128)(2,1)S(1)}, u32[]{:S(2)}, u32[]{:S(2)}) %collective-permute-start) | collective-permute-done | bytes 29728 | tf_op jit(solution)/shard_map/ppermute | solution.py:95
  8.8 3.1 %collective-permute-start.1 = (bf16[8,3712]{1,0:T(8,128)(2,1)S(1)}, bf16[8,3712]{1,0:T(8,128)(2,1)S(1)}, u32[]{:S(2)}, u32[]{:S(2)}) collective-permute-start(bf16[8,3712]{1,0:T(8,128)(2,1)S(1)} %pad_maximum_fusion.2), channel_id=1, source_target_pairs={{0,8},{4,12},{8,0},{12,4},{1,9},{5,13},{9,1},{13,5},{2,10},{6,14},... | collective-permute-start | bytes 178184 | tf_op jit(solution)/shard_map/ppermute | solution.py:95
  11.9 2.2 %collective-permute-done.1 = bf16[8,3712]{1,0:T(8,128)(2,1)S(1)} collective-permute-done((bf16[8,3712]{1,0:T(8,128)(2,1)S(1)}, bf16[8,3712]{1,0:T(8,128)(2,1)S(1)}, u32[]{:S(2)}, u32[]{:S(2)}) %collective-permute-start.1) | collective-permute-done | bytes 59424 | tf_op jit(solution)/shard_map/ppermute | solution.py:95
  14.8 1.9 %collective-permute-start.2 = (bf16[16,3712]{1,0:T(8,128)(2,1)S(1)}, bf16[16,3712]{1,0:T(8,128)(2,1)S(1)}, u32[]{:S(2)}, u32[]{:S(2)}) collective-permute-start(bf16[16,3712]{1,0:T(8,128)(2,1)S(1)} %pad_maximum_fusion.1), channel_id=1, source_target_pairs={{0,2},{1,3},{2,0},{3,1},{4,6},{5,7},{6,4},{7,5},{8,10},{9,11},{10,... | collective-permute-start | bytes 356360 | tf_op jit(solution)/shard_map/ppermute | solution.py:95
  16.7 3.0 %collective-permute-done.2 = bf16[16,3712]{1,0:T(8,128)(2,1)S(1)} collective-permute-done((bf16[16,3712]{1,0:T(8,128)(2,1)S(1)}, bf16[16,3712]{1,0:T(8,128)(2,1)S(1)}, u32[]{:S(2)}, u32[]{:S(2)}) %collective-permute-start.2) | collective-permute-done | bytes 118816 | tf_op jit(solution)/shard_map/ppermute | solution.py:95
  19.7 0.8 %pad_maximum_fusion = bf16[32,3712]{1,0:T(8,128)(2,1)S(1)} fusion(bf16[16,3712]{1,0:T(8,128)(2,1)S(1)} %collective-permute-done.2, bf16[8,3712]{1,0:T(8,128)(2,1)S(1)} %collective-permute-done.1, bf16[4,3712]{1,0:T(4,128)(2,1)S(1)} %collective-permute-done, bf16[4,3712]{1,0:T(4,128)(2,1)} %shard_map.109), kind=kLoop, calls=%fused_computation.1 | loop fusion | flops 950272 | bytes 475136 | tf_op jit(solution)/shard_map/concatenate | solution.py:138
  20.6 1.5 %collective-permute-done.3 = bf16[32,3712]{1,0:T(8,128)(2,1)S(1)} collective-permute-done((bf16[32,3712]{1,0:T(8,128)(2,1)S(1)}, bf16[32,3712]{1,0:T(8,128)(2,1)S(1)}, u32[]{:S(2)}, u32[]{:S(2)}) %collective-permute-start.3) | collective-permute-done | bytes 237600 | tf_op jit(solution)/shard_map/ppermute | solution.py:95
  22.1 3.5 %concatenate.18.x_ref = bf16[64,3712]{1,0:T(8,128)(2,1)} concatenate(bf16[4,3712]{1,0:T(4,128)(2,1)} %shard_map.109, bf16[4,3712]{1,0:T(4,128)(2,1)S(1)} %collective-permute-done, bf16[8,3712]{1,0:T(8,128)(2,1)S(1)} %collective-permute-done.1, bf16[16,3712]{1,0:T(8,128)(2,1)S(1)} %collective-permute-done.2, bf16[32,3712]{1,0:T(8,128)(2,1)S(1)} %collective-permute-done.3), dimensions={0} | concatenate | bytes 950272 | tf_op jit(solution)/shard_map/concatenate | solution.py:138
  25.6 2.3 %shard_map.111.refs_0_ = bf16[64,512]{1,0:T(8,128)(2,1)} custom-call(s32[1]{0:T(128)} %bitcast.start_ref, bf16[64,3712]{1,0:T(8,128)(2,1)} %concatenate.18.x_ref, bf16[256,896]{1,0:T(8,128)(2,1)} %gate_ref.3, bf16[256,896]{1,0:T(8,128)(2,1)} %up_ref.3), custom_call_target="tpu_custom_call" | custom-call | tf_op jit(solution)/shard_map/pallas_call | solution.py:147
  27.9 4.5 %collective-permute-start.6 = (bf16[64,512]{1,0:T(8,128)(2,1)}, bf16[64,512]{1,0:T(8,128)(2,1)S(1)}, u32[]{:S(2)}, u32[]{:S(2)}) collective-permute-start(bf16[64,512]{1,0:T(8,128)(2,1)} %shard_map.111.refs_0_), channel_id=1, source_target_pairs={{0,12},{4,8},{8,4},{12,0},{1,13},{5,9},{9,5},{13,1},{2,14},{6,10},... | collective-permute-start | bytes 196616 | tf_op jit(solution)/shard_map/ppermute | solution.py:95
  32.9 13.8 %shard_map.110.hidden_ref = bf16[64,2048]{1,0:T(8,128)(2,1)} custom-call(s32[1]{0:T(128)} %bitcast.1.first_ref, bf16[64,3712]{1,0:T(8,128)(2,1)} %concatenate.18.x_ref, bf16[8,3584,256]{2,1,0:T(8,128)(2,1)} %gate_ref.2, bf16[8,3584,256]{2,1,0:T(8,128)(2,1)} %up_ref.2), custom_call_target="tpu_custom_call" | custom-call | tf_op jit(solution)/shard_map/pallas_call | solution.py:155
  48.0 10.6 %shard_map.112 = bf16[64,3584]{1,0:T(8,128)(2,1)} custom-call(s32[1]{0:T(128)} %bitcast.start_ref, bf16[64,2048]{1,0:T(8,128)(2,1)} %shard_map.110.hidden_ref, bf16[8,256,3584]{2,1,0:T(8,128)(2,1)} %down_ref.1, bf16[256,896]{1,0:T(8,128)(2,1)} %shared_down_ref.1, bf16[64,512]{1,0:T(8,128)(2,1)} %shard_map.111.refs_0_, bf16[64,512]{1,0:T(8,128)(2,1)} %copy-done.2, ...), custom_call_target="tpu_custom_call" | custom-call | tf_op jit(solution)/shard_map/pallas_call | solution.py:173
  58.6 1.0 %slice.33 = bf16[32,3584]{1,0:T(8,128)(2,1)S(1)} slice(bf16[64,3584]{1,0:T(8,128)(2,1)} %shard_map.112), slice={[32:64], [0:3584]} | slice | bytes 458752 | tf_op jit(solution)/shard_map/slice | solution.py:192
  59.7 1.5 %collective-permute-done.7 = bf16[32,3584]{1,0:T(8,128)(2,1)S(1)} collective-permute-done((bf16[32,3584]{1,0:T(8,128)(2,1)S(1)}, bf16[32,3584]{1,0:T(8,128)(2,1)S(1)}, u32[]{:S(2)}, u32[]{:S(2)}) %collective-permute-start.7) | collective-permute-done | bytes 229408 | tf_op jit(solution)/shard_map/ppermute | solution.py:95
  61.1 1.0 %add_convert_fusion = bf16[32,3584]{1,0:T(8,128)(2,1)S(1)} fusion(bf16[32,3584]{1,0:T(8,128)(2,1)S(1)} %collective-permute-done.7, bf16[64,3584]{1,0:T(8,128)(2,1)} %shard_map.112), kind=kLoop, calls=%fused_computation | loop fusion | flops 458752 | bytes 688128 | tf_op jit(solution)/shard_map/convert_element_type | solution.py:99
  62.1 1.6 %collective-permute-start.8 = (bf16[16,3584]{1,0:T(8,128)(2,1)S(1)}, bf16[16,3584]{1,0:T(8,128)(2,1)S(1)}, u32[]{:S(2)}, u32[]{:S(2)}) collective-permute-start(bf16[16,3584]{1,0:T(8,128)(2,1)S(1)} %slice.35), channel_id=1, source_target_pairs={{0,2},{1,3},{2,0},{3,1},{4,6},{5,7},{6,4},{7,5},{8,10},{9,11},{10,... | collective-permute-start | bytes 344072 | tf_op jit(solution)/shard_map/ppermute | solution.py:95
  63.7 3.7 %collective-permute-done.8 = bf16[16,3584]{1,0:T(8,128)(2,1)S(1)} collective-permute-done((bf16[16,3584]{1,0:T(8,128)(2,1)S(1)}, bf16[16,3584]{1,0:T(8,128)(2,1)S(1)}, u32[]{:S(2)}, u32[]{:S(2)}) %collective-permute-start.8) | collective-permute-done | bytes 114720 | tf_op jit(solution)/shard_map/ppermute | solution.py:95
  67.4 2.4 %collective-permute-start.9 = (bf16[8,3584]{1,0:T(8,128)(2,1)S(1)}, bf16[8,3584]{1,0:T(8,128)(2,1)S(1)}, u32[]{:S(2)}, u32[]{:S(2)}) collective-permute-start(bf16[8,3584]{1,0:T(8,128)(2,1)S(1)} %slice.37), channel_id=1, source_target_pairs={{0,8},{4,12},{8,0},{12,4},{1,9},{5,13},{9,1},{13,5},{2,10},{6,14},... | collective-permute-start | bytes 172040 | tf_op jit(solution)/shard_map/ppermute | solution.py:95
  69.9 2.8 %collective-permute-done.9 = bf16[8,3584]{1,0:T(8,128)(2,1)S(1)} collective-permute-done((bf16[8,3584]{1,0:T(8,128)(2,1)S(1)}, bf16[8,3584]{1,0:T(8,128)(2,1)S(1)}, u32[]{:S(2)}, u32[]{:S(2)}) %collective-permute-start.9) | collective-permute-done | bytes 57376 | tf_op jit(solution)/shard_map/ppermute | solution.py:95
  72.8 1.4 %collective-permute-start.10 = (bf16[4,3584]{1,0:T(4,128)(2,1)S(1)}, bf16[4,3584]{1,0:T(4,128)(2,1)S(1)}, u32[]{:S(2)}, u32[]{:S(2)}) collective-permute-start(bf16[4,3584]{1,0:T(4,128)(2,1)S(1)} %slice.39), channel_id=1, source_target_pairs={{0,4},{4,0},{8,12},{12,8},{1,5},{5,1},{9,13},{13,9},{2,6},{6,2},{1... | collective-permute-start | bytes 86024 | tf_op jit(solution)/shard_map/ppermute | solution.py:95
  74.2 2.5 %collective-permute-done.10 = bf16[4,3584]{1,0:T(4,128)(2,1)S(1)} collective-permute-done((bf16[4,3584]{1,0:T(4,128)(2,1)S(1)}, bf16[4,3584]{1,0:T(4,128)(2,1)S(1)}, u32[]{:S(2)}, u32[]{:S(2)}) %collective-permute-start.10) | collective-permute-done | bytes 28704 | tf_op jit(solution)/shard_map/ppermute | solution.py:95
  (21 shorter events, 4.2 us)
Async XLA Ops:
  2.9 5.1 %collective-permute-start = (bf16[4,3712]{1,0:T(4,128)(2,1)}, bf16[4,3712]{1,0:T(4,128)(2,1)S(1)}, u32[]{:S(2)}, u32[]{:S(2)}) collective-permute-start(bf16[4,3712]{1,0:T(4,128)(2,1)} %shard_map.109), channel_id=1, source_target_pairs={{0,4},{4,0},{8,12},{12,8},{1,5},{5,1},{9,13},{13,9},{2,6},{6,2},{1... | collective-permute-start | bytes 89096 | tf_op jit(solution)/shard_map/ppermute | solution.py:95
  8.8 5.3 %collective-permute-start.1 = (bf16[8,3712]{1,0:T(8,128)(2,1)S(1)}, bf16[8,3712]{1,0:T(8,128)(2,1)S(1)}, u32[]{:S(2)}, u32[]{:S(2)}) collective-permute-start(bf16[8,3712]{1,0:T(8,128)(2,1)S(1)} %pad_maximum_fusion.2), channel_id=1, source_target_pairs={{0,8},{4,12},{8,0},{12,4},{1,9},{5,13},{9,1},{13,5},{2,10},{6,14},... | collective-permute-start | bytes 178184 | tf_op jit(solution)/shard_map/ppermute | solution.py:95
  14.8 4.9 %collective-permute-start.2 = (bf16[16,3712]{1,0:T(8,128)(2,1)S(1)}, bf16[16,3712]{1,0:T(8,128)(2,1)S(1)}, u32[]{:S(2)}, u32[]{:S(2)}) collective-permute-start(bf16[16,3712]{1,0:T(8,128)(2,1)S(1)} %pad_maximum_fusion.1), channel_id=1, source_target_pairs={{0,2},{1,3},{2,0},{3,1},{4,6},{5,7},{6,4},{7,5},{8,10},{9,11},{10,... | collective-permute-start | bytes 356360 | tf_op jit(solution)/shard_map/ppermute | solution.py:95
  20.5 1.6 %collective-permute-start.3 = (bf16[32,3712]{1,0:T(8,128)(2,1)S(1)}, bf16[32,3712]{1,0:T(8,128)(2,1)S(1)}, u32[]{:S(2)}, u32[]{:S(2)}) collective-permute-start(bf16[32,3712]{1,0:T(8,128)(2,1)S(1)} %pad_maximum_fusion), channel_id=1, source_target_pairs={{0,1},{1,0},{2,3},{3,2},{4,5},{5,4},{6,7},{7,6},{8,9},{9,8},{10,11... | collective-permute-start | bytes 712712 | tf_op jit(solution)/shard_map/ppermute | solution.py:95
  27.9 18.8 %collective-permute-start.6 = (bf16[64,512]{1,0:T(8,128)(2,1)}, bf16[64,512]{1,0:T(8,128)(2,1)S(1)}, u32[]{:S(2)}, u32[]{:S(2)}) collective-permute-start(bf16[64,512]{1,0:T(8,128)(2,1)} %shard_map.111.refs_0_), channel_id=1, source_target_pairs={{0,12},{4,8},{8,4},{12,0},{1,13},{5,9},{9,5},{13,1},{2,14},{6,10},... | collective-permute-start | bytes 196616 | tf_op jit(solution)/shard_map/ppermute | solution.py:95
  32.4 14.4 %collective-permute-start.5 = (bf16[64,512]{1,0:T(8,128)(2,1)}, bf16[64,512]{1,0:T(8,128)(2,1)S(1)}, u32[]{:S(2)}, u32[]{:S(2)}) collective-permute-start(bf16[64,512]{1,0:T(8,128)(2,1)} %shard_map.111.refs_0_), channel_id=1, source_target_pairs={{0,8},{4,12},{8,0},{12,4},{1,9},{5,13},{9,1},{13,5},{2,10},{6,14},... | collective-permute-start | bytes 196616 | tf_op jit(solution)/shard_map/ppermute | solution.py:95
  32.4 14.4 %collective-permute-start.4 = (bf16[64,512]{1,0:T(8,128)(2,1)}, bf16[64,512]{1,0:T(8,128)(2,1)S(1)}, u32[]{:S(2)}, u32[]{:S(2)}) collective-permute-start(bf16[64,512]{1,0:T(8,128)(2,1)} %shard_map.111.refs_0_), channel_id=1, source_target_pairs={{0,4},{4,0},{8,12},{12,8},{1,5},{5,1},{9,13},{13,9},{2,6},{6,2},{1... | collective-permute-start | bytes 196616 | tf_op jit(solution)/shard_map/ppermute | solution.py:95
  46.7 0.6 copy-start
  46.7 0.6 copy-start.1
  47.4 0.6 copy-start.2
  59.6 1.6 %collective-permute-start.7 = (bf16[32,3584]{1,0:T(8,128)(2,1)S(1)}, bf16[32,3584]{1,0:T(8,128)(2,1)S(1)}, u32[]{:S(2)}, u32[]{:S(2)}) collective-permute-start(bf16[32,3584]{1,0:T(8,128)(2,1)S(1)} %slice.33), channel_id=1, source_target_pairs={{0,1},{1,0},{2,3},{3,2},{4,5},{5,4},{6,7},{7,6},{8,9},{9,8},{10,11... | collective-permute-start | bytes 688136 | tf_op jit(solution)/shard_map/ppermute | solution.py:95
  62.1 5.3 %collective-permute-start.8 = (bf16[16,3584]{1,0:T(8,128)(2,1)S(1)}, bf16[16,3584]{1,0:T(8,128)(2,1)S(1)}, u32[]{:S(2)}, u32[]{:S(2)}) collective-permute-start(bf16[16,3584]{1,0:T(8,128)(2,1)S(1)} %slice.35), channel_id=1, source_target_pairs={{0,2},{1,3},{2,0},{3,1},{4,6},{5,7},{6,4},{7,5},{8,10},{9,11},{10,... | collective-permute-start | bytes 344072 | tf_op jit(solution)/shard_map/ppermute | solution.py:95
  67.4 5.3 %collective-permute-start.9 = (bf16[8,3584]{1,0:T(8,128)(2,1)S(1)}, bf16[8,3584]{1,0:T(8,128)(2,1)S(1)}, u32[]{:S(2)}, u32[]{:S(2)}) collective-permute-start(bf16[8,3584]{1,0:T(8,128)(2,1)S(1)} %slice.37), channel_id=1, source_target_pairs={{0,8},{4,12},{8,0},{12,4},{1,9},{5,13},{9,1},{13,5},{2,10},{6,14},... | collective-permute-start | bytes 172040 | tf_op jit(solution)/shard_map/ppermute | solution.py:95
  72.8 3.9 %collective-permute-start.10 = (bf16[4,3584]{1,0:T(4,128)(2,1)S(1)}, bf16[4,3584]{1,0:T(4,128)(2,1)S(1)}, u32[]{:S(2)}, u32[]{:S(2)}) collective-permute-start(bf16[4,3584]{1,0:T(4,128)(2,1)S(1)} %slice.39), channel_id=1, source_target_pairs={{0,4},{4,0},{8,12},{12,8},{1,5},{5,1},{9,13},{13,9},{2,6},{6,2},{1... | collective-permute-start | bytes 86024 | tf_op jit(solution)/shard_map/ppermute | solution.py:95

commit v3 on v2

v3 whole, which is shorter than its diff:
```python
import functools
import math

import jax
import jax.numpy as jnp
from jax import lax
from jax.experimental import pallas as pl
from jax.experimental.pallas import tpu as pltpu
from jax.sharding import PartitionSpec as P

NODE_GROUPS = 8
LANES = 128
MIB = 2**20
NEAR_PLAN = (0, 0, 0, 1)


def pack_kernel(per_group, *refs):
    count = len(refs) // 2 - 1
    sources, out_ref, staged, sems = refs[:count], refs[count], refs[count + 1 : -1], refs[-1]
    copies = [
        pltpu.make_async_copy(here, there, sems.at[i])
        for i, (here, there) in enumerate(zip(sources, staged))
    ]
    for copy in copies:
        copy.start()
    for copy in copies:
        copy.wait()
    x_ref, gain_ref, groups_ref, picks_ref, weight_ref = staged
    features = x_ref[...].astype(jnp.float32)
    count = features.shape[1]
    mean_square = jnp.mean(features * features, axis=1, keepdims=True)
    normed = features * lax.rsqrt(mean_square + 1e-06) * gain_ref[...].reshape(1, -1)
    out_ref[:, :count] = normed.astype(jnp.bfloat16)
    picks = picks_ref[...]
    groups = groups_ref[...]
    weight = weight_ref[...].astype(jnp.float32)
    slot = lax.div(picks, jnp.full_like(picks, per_group))
    inner = picks - slot * per_group
    group = jnp.zeros_like(picks)
    for a in range(groups.shape[1]):
        group = jnp.where(slot == a, groups[:, a : a + 1], group)
    ids = group * per_group + inner
    width = out_ref.shape[1] - count
    lane = lax.broadcasted_iota(jnp.int32, (picks.shape[0], width), 1)
    total = jnp.zeros((picks.shape[0], width), jnp.float32)
    for k in range(picks.shape[1]):
        total = total + jnp.where(ids[:, k : k + 1] == lane, weight[:, k : k + 1], 0.0)
    out_ref[:, count:] = total.astype(jnp.bfloat16)


def shared_in_kernel(start_ref, x_ref, gate_ref, up_ref, out_ref):
    contract = (((1,), (1,)), ((), ()))
    block, slab = gate_ref.shape
    x = x_ref[...]
    if x.shape[1] != slab:
        x = x_ref[:, pl.ds(pl.multiple_of(start_ref[0], LANES), slab)]
    for i, ref in enumerate((gate_ref, up_ref)):
        part = lax.dot_general(x, ref[...], contract, preferred_element_type=jnp.float32)
        out_ref[:, i * block : (i + 1) * block] = part.astype(jnp.bfloat16)


def routed_kernel(near_count, first_ref, x_ref, gate_hbm, up_hbm, down_hbm, *refs):
    near, out_ref = refs[:near_count], refs[near_count]
    far_refs, sems = refs[near_count + 1 : -1], refs[-1]
    held, count, _ = gate_hbm.shape
    copies = []
    for i, there in enumerate(far_refs):
        e, kind = divmod(near_count + i, 3)
        here = (gate_hbm, up_hbm, down_hbm)[kind].at[e]
        copies.append(pltpu.make_async_copy(here, there, sems.at[i]))
        copies[-1].start()

    def fetch(index):
        if index < near_count:
            return near[index][...]
        copies[index - near_count].wait()
        return far_refs[index - near_count][...]

    x = x_ref[:, :count]
    weights = x_ref[:, count:].astype(jnp.float32)
    lane = lax.broadcasted_iota(jnp.int32, weights.shape, 1)
    for e in range(held):
        chosen = jnp.where(lane == first_ref[0] + e, weights, 0.0)
        weight = jnp.sum(chosen, axis=1, keepdims=True)
        gate = jnp.dot(x, fetch(3 * e), preferred_element_type=jnp.float32)
        up = jnp.dot(x, fetch(3 * e + 1), preferred_element_type=jnp.float32)
        hidden = (jax.nn.silu(gate) * up * weight).astype(jnp.bfloat16)
        term = jnp.dot(hidden, fetch(3 * e + 2), preferred_element_type=jnp.float32)
        if e == 0:
            out_ref[...] = term
        else:
            out_ref[...] += term


def shared_out_kernel(tokens, start_ref, routed_ref, down_ref, *refs):
    parts, out_ref = refs[:-1], refs[-1]
    block, slab = down_ref.shape
    count, width = out_ref.shape
    total = parts[0][...].astype(jnp.float32)
    to = lax.broadcasted_iota(jnp.int32, (count, count), 0)
    come = lax.broadcasted_iota(jnp.int32, (count, count), 1)
    for k in range(1, len(parts)):
        place = (come == (to ^ (k * tokens))).astype(jnp.bfloat16)
        total += jnp.dot(place, parts[k][...], preferred_element_type=jnp.float32)
    hidden = (jax.nn.silu(total[:, :block]) * total[:, block:]).astype(jnp.bfloat16)
    shared = jnp.dot(hidden, down_ref[...], preferred_element_type=jnp.float32)
    if slab == width:
        out_ref[...] = (routed_ref[...] + shared).astype(jnp.bfloat16)
    else:
        out_ref[...] = routed_ref[...].astype(jnp.bfloat16)
        columns = pl.ds(pl.multiple_of(start_ref[0], LANES), slab)
        out_ref[:, columns] = (routed_ref[:, columns] + shared).astype(jnp.bfloat16)


def bring_kernel(which, rows_ref, *refs):
    count = len(which)
    sources, kept, sems = refs[:count], refs[count:-1], refs[-1]
    copies = []
    for i, e in enumerate(which):
        here = sources[i] if e is None else sources[i].at[e]
        copies.append(pltpu.make_async_copy(here, kept[i], sems.at[i]))
        copies[-1].start()
    for copy in copies:
        copy.wait()


def bring(wanted, rows):
    hbm = pl.BlockSpec(memory_space=pl.ANY)
    shapes = [w.shape if e is None else w.shape[1:] for w, e in wanted]
    return pl.pallas_call(
        functools.partial(bring_kernel, [e for _, e in wanted]),
        out_shape=[pltpu.VMEM(shape, jnp.bfloat16) for shape in shapes],
        in_specs=[hbm] * (1 + len(wanted)),
        out_specs=[pl.BlockSpec(memory_space=pltpu.VMEM)] * len(wanted),
        scratch_shapes=[pltpu.SemaphoreType.DMA((len(wanted),))],
        compiler_params=pltpu.CompilerParams(
            vmem_limit_bytes=2 * sum(math.prod(shape) for shape in shapes) + MIB
        ),
    )(rows, *(far(w) for w, _ in wanted))


def far(value):
    return pltpu.with_memory_space_constraint(value, pltpu.HBM)


def exchange(value, axis, bit):
    size = lax.axis_size(axis)
    return lax.ppermute(value, axis, [(i, i ^ bit) for i in range(size)])


def add_rows(one, other):
    return (one.astype(jnp.float32) + other.astype(jnp.float32)).astype(jnp.bfloat16)


def local(
    hidden_states,
    norm_gain,
    route_groups,
    route_picks,
    gate_weights,
    expert_gate,
    expert_up,
    expert_down,
    shared_gate,
    shared_up,
    shared_down,
):
    node_count = lax.axis_size("node")
    local_count = lax.axis_size("local")
    node = lax.axis_index("node")
    token_count, feature_count = hidden_states.shape
    held, _, block = expert_gate.shape
    expert_total = held * node_count
    per_group = expert_total // NODE_GROUPS
    width = feature_count + -(-expert_total // LANES) * LANES
    slab = shared_gate.shape[1]
    shared_block = shared_gate.shape[0]
    row_total = token_count * node_count * local_count
    params = pltpu.CompilerParams(
        vmem_limit_bytes=4 * MIB + (12 * width + 2 * node_count * 2 * shared_block) * row_total
    )
    smem = pl.BlockSpec(memory_space=pltpu.SMEM)
    vmem = pl.BlockSpec(memory_space=pltpu.VMEM)
    hbm = pl.BlockSpec(memory_space=pl.ANY)
    small = (hidden_states, norm_gain, route_groups, route_picks, gate_weights)
    rows = pl.pallas_call(
        functools.partial(pack_kernel, per_group),
        out_shape=jax.ShapeDtypeStruct((token_count, width), jnp.bfloat16),
        in_specs=[hbm] * len(small),
        out_specs=vmem,
        scratch_shapes=[pltpu.VMEM(a.shape, a.dtype) for a in small]
        + [pltpu.SemaphoreType.DMA((len(small),))],
        compiler_params=params,
    )(*(far(a) for a in small))

    weights = [(w, e) for e in range(held) for w in (expert_gate, expert_up, expert_down)]
    stages = [("node", 1 << i) for i in range(node_count.bit_length() - 1)]
    stages += [("local", 1 << i) for i in reversed(range(local_count.bit_length() - 1))]
    ready = []
    for stage, (axis, bit) in enumerate(stages):
        other = exchange(rows, axis, bit)
        take = NEAR_PLAN[stage] if stage < len(NEAR_PLAN) else 0
        wanted = weights[len(ready) : len(ready) + take]
        extra = [(shared_gate, None), (shared_up, None)] if stage == len(stages) - 2 else []
        if wanted or extra:
            got = bring(wanted + extra, rows)
            other, *got = lax.optimization_barrier((other, *got))
            ready += got[: len(wanted)]
            if extra:
                shared_gate, shared_up = got[len(wanted) :]
        rows = jnp.concatenate([rows, other], axis=0)
    row_count = rows.shape[0]

    start = (node * slab).astype(jnp.int32)
    aligned = slab % LANES == 0
    mine = rows if aligned else lax.dynamic_slice_in_dim(rows, start, slab, axis=1)
    shared_part = pl.pallas_call(
        shared_in_kernel,
        out_shape=jax.ShapeDtypeStruct((row_count, 2 * shared_block), jnp.bfloat16),
        in_specs=[smem, vmem, vmem, vmem],
        compiler_params=params,
    )(start.reshape(1), mine, shared_gate, shared_up)
    parts = [shared_part] + [exchange(shared_part, "node", k) for k in range(1, node_count)]

    late = weights[len(ready) :]
    late_bytes = 2 * sum(math.prod(w.shape[1:]) for w, _ in late)
    routed = pl.pallas_call(
        functools.partial(routed_kernel, len(ready)),
        out_shape=jax.ShapeDtypeStruct((row_count, feature_count), jnp.float32),
        in_specs=[smem, vmem, hbm, hbm, hbm] + [vmem] * len(ready),
        out_specs=vmem,
        scratch_shapes=[pltpu.VMEM(w.shape[1:], jnp.bfloat16) for w, _ in late]
        + [pltpu.SemaphoreType.DMA((max(len(late), 1),))],
        compiler_params=pltpu.CompilerParams(
            vmem_limit_bytes=late_bytes + 12 * row_count * width + 4 * MIB
        ),
    )(
        (node * held).astype(jnp.int32).reshape(1),
        rows,
        *(far(w) for w in (expert_gate, expert_up, expert_down)),
        *ready,
    )

    if not aligned:
        shared_down = lax.dynamic_update_slice_in_dim(
            jnp.zeros((shared_block, feature_count), shared_down.dtype), shared_down, start, axis=1
        )
    out = pl.pallas_call(
        functools.partial(shared_out_kernel, token_count),
        out_shape=jax.ShapeDtypeStruct((row_count, feature_count), jnp.bfloat16),
        in_specs=[smem] + [vmem] * (2 + node_count),
        out_specs=vmem,
        compiler_params=params,
    )(start.reshape(1), routed, shared_down, *parts)

    bit = 1
    while bit < local_count:
        half = out.shape[0] // 2
        out = add_rows(out[:half], exchange(out[half:], "local", bit))
        bit *= 2
    bit = node_count // 2
    while bit:
        half = out.shape[0] // 2
        out = add_rows(out[:half], exchange(out[half:], "node", bit))
        bit //= 2
    return out


def solution(mesh):
    placed = (
        P(("groups", "node", "local"), None),
        P(),
        P(("groups", "node", "local"), None),
        P(("groups", "node", "local"), None),
        P(("groups", "node", "local"), None),
        P("node", None, "local"),
        P("node", None, "local"),
        P("node", "local", None),
        P("local", "node"),
        P("local", "node"),
        P("local", "node"),
    )
    return jax.shard_map(
        local,
        mesh=mesh,
        in_specs=placed,
        out_specs=P(("groups", "node", "local"), None),
        check_vma=False,
    )
```

time: 78 us -> 56.4 us (0.72)
  Pallas kernels: 28.3 us -> 18.8 us
  local copies, waits for them, and re-layouts: 7.01 us -> 1.14 us
  other arithmetic: 4.07 us -> 0.87 us
  waiting for transfers between devices: 19.3 us -> 17.4 us
    pallas_call x2 -> x4, Pallas kernels: 24.4 us -> 17.4 us  [the longest x1 14.4 us: local(): pl.pallas_call(functools.partial(routed_kernel, len(ready)), out_shape=ja...]
    concatenate x1, local copies, waits for them, and re-layouts: 3.46 us -> 1.08 us  [local(): rows = jnp.concatenate([rows, other], axis=0)]
    concatenate x3, other arithmetic: 2.39 us -> 0.14 us  [local(): rows = jnp.concatenate([rows, other], axis=0)]
    ppermute x11, waiting for transfers between devices: 19.3 us -> 17.4 us  [exchange(): return lax.ppermute(value, axis, [(i, i ^ bit) for i in range(size)])]
    pallas_call x1, Pallas kernels: 2.32 us -> 0.4 us  [local(): pl.pallas_call(shared_in_kernel, out_shape=jax.ShapeDtypeStruct((row_coun...]
    reshape x1 -> x0, local copies, waits for them, and re-layouts: 1.33 us -> none  [local(): norm_gain.reshape(1, -1)]
    unnamed x6 -> x2, local copies, waits for them, and re-layouts: 1.23 us -> 0.01 us
    convert_element_type x4, other arithmetic: 1.68 us -> 0.73 us  [add_rows(): (one.astype(jnp.float32) + other.astype(jnp.float32)).astype(jnp.bfloat16)]
  transfers between devices with their start and end apart: 11 -> 11, of which waited for: 8 -> 8; matrix products, arithmetic and copies ran while one was open for 0% -> 0% of each run, Pallas kernels for 18% -> 30%
where the time goes in v3:
time: 56.4 us; the launch traced here: 56.2 us
  Pallas kernels  18.8 us (33%)
  starting transfers between devices  17.9 us (32%)
  waiting for transfers between devices  17.4 us (31%)
  local copies, waits for them, and re-layouts  1.14 us (2%)
  other arithmetic  0.87 us (2%)
    ppermute x11, starting transfers between devices, exchange(): return lax.ppermute(value, axis, [(i, i ^ bit) for i in range(size)])  17.9 us
    ppermute x11, waiting for transfers between devices, exchange(): return lax.ppermute(value, axis, [(i, i ^ bit) for i in range(size)])  17.4 us
    pallas_call x1, Pallas kernels, local(): pl.pallas_call(functools.partial(routed_kernel, len(ready)), out_shape=ja...  14.4 us
    pallas_call x2, Pallas kernels, bring(): pl.pallas_call(functools.partial(bring_kernel, [e for _, e in wanted]), o...  2.68 us
  transfers between devices with their start and end apart: 11, of which 8 were waited for; matrix products, arithmetic and copies ran while one was open for 0% of the time, Pallas kernels for 30%

profile of v3, /device:TPU:0, one launch (start us, length us, event | category | flops | bytes accessed | tf_op | source)
XLA Modules:
  0.0 56.2 jit_solution(8549837772500814818)
XLA Ops:
  0.0 1.0 %shard_map.109 = bf16[4,3712]{1,0:T(4,128)(2,1)S(1)} custom-call(bf16[4,3584]{1,0:T(4,128)(2,1)} %refs_0_.3, f32[3584]{0:T(1024)} %refs_1_.2, s32[4,4]{1,0:T(4,128)} %refs_2_.1, s32[4,8]{1,0:T(4,128)} %refs_3_.1, bf16[4,8]{1,0:T(4,128)(2,1)} %refs_4_.1), custom_call_target="tpu_custom_call" | custom-call | tf_op jit(solution)/shard_map/pallas_call | solution.py:186
  1.0 3.1 %collective-permute-start = (bf16[4,3712]{1,0:T(4,128)(2,1)S(1)}, bf16[4,3712]{1,0:T(4,128)(2,1)S(1)}, u32[]{:S(2)}, u32[]{:S(2)}) collective-permute-start(bf16[4,3712]{1,0:T(4,128)(2,1)S(1)} %shard_map.109), channel_id=1, source_target_pairs={{0,4},{4,0},{8,12},{12,8},{1,5},{5,1},{9,13},{13,9},{2,6},{6,2},{1... | collective-permute-start | bytes 89096 | tf_op jit(solution)/shard_map/ppermute | solution.py:148
  4.1 1.9 %collective-permute-done = bf16[4,3712]{1,0:T(4,128)(2,1)S(1)} collective-permute-done((bf16[4,3712]{1,0:T(4,128)(2,1)S(1)}, bf16[4,3712]{1,0:T(4,128)(2,1)S(1)}, u32[]{:S(2)}, u32[]{:S(2)}) %collective-permute-start) | collective-permute-done | bytes 29728 | tf_op jit(solution)/shard_map/ppermute | solution.py:148
  6.0 3.1 %collective-permute-start.1 = (bf16[8,3712]{1,0:T(8,128)(2,1)S(1)}, bf16[8,3712]{1,0:T(8,128)(2,1)S(1)}, u32[]{:S(2)}, u32[]{:S(2)}) collective-permute-start(bf16[8,3712]{1,0:T(8,128)(2,1)S(1)} %pad_maximum_fusion.2), channel_id=1, source_target_pairs={{0,8},{4,12},{8,0},{12,4},{1,9},{5,13},{9,1},{13,5},{2,10},{6,14},... | collective-permute-start | bytes 178184 | tf_op jit(solution)/shard_map/ppermute | solution.py:148
  9.1 2.2 %collective-permute-done.1 = bf16[8,3712]{1,0:T(8,128)(2,1)S(1)} collective-permute-done((bf16[8,3712]{1,0:T(8,128)(2,1)S(1)}, bf16[8,3712]{1,0:T(8,128)(2,1)S(1)}, u32[]{:S(2)}, u32[]{:S(2)}) %collective-permute-start.1) | collective-permute-done | bytes 59424 | tf_op jit(solution)/shard_map/ppermute | solution.py:148
  11.3 1.9 %collective-permute-start.2 = (bf16[16,3712]{1,0:T(8,128)(2,1)S(1)}, bf16[16,3712]{1,0:T(8,128)(2,1)S(1)}, u32[]{:S(2)}, u32[]{:S(2)}) collective-permute-start(bf16[16,3712]{1,0:T(8,128)(2,1)S(1)} %pad_maximum_fusion.1.rows_ref), channel_id=1, source_target_pairs={{0,2},{1,3},{2,0},{3,1},{4,6},{5,7},{6,4},{7,5},{8,10},{9,11},{10,... | collective-permute-start | bytes 356360 | tf_op jit(solution)/shard_map/ppermute | solution.py:148
  13.2 1.2 %shard_map.110 = (bf16[256,896]{1,0:T(8,128)(2,1)S(1)}, bf16[256,896]{1,0:T(8,128)(2,1)S(1)}) custom-call(bf16[16,3712]{1,0:T(8,128)(2,1)S(1)} %pad_maximum_fusion.1.rows_ref, bf16[256,896]{1,0:T(8,128)(2,1)} %refs_0_.4, bf16[256,896]{1,0:T(8,128)(2,1)} %refs_1_.3), custom_call_target="tpu_custom_call" | custom-call | tf_op jit(solution)/shard_map/pallas_call | solution.py:130
  14.4 1.8 %collective-permute-done.2 = bf16[16,3712]{1,0:T(8,128)(2,1)S(1)} collective-permute-done((bf16[16,3712]{1,0:T(8,128)(2,1)S(1)}, bf16[16,3712]{1,0:T(8,128)(2,1)S(1)}, u32[]{:S(2)}, u32[]{:S(2)}) %collective-permute-start.2) | collective-permute-done | bytes 118816 | tf_op jit(solution)/shard_map/ppermute | solution.py:148
  16.3 1.5 %shard_map.111.refs_0_ = bf16[3584,256]{1,0:T(8,128)(2,1)S(1)} custom-call(bf16[32,3712]{1,0:T(8,128)(2,1)S(1)} %pad_maximum_fusion.rows_ref, bf16[8,3584,256]{2,1,0:T(8,128)(2,1)} %gate_hbm.1), custom_call_target="tpu_custom_call" | custom-call | tf_op jit(solution)/shard_map/pallas_call | solution.py:130
  17.8 0.1 collective-permute-done.3
  17.9 1.1 %concatenate.18.x_ref = bf16[64,3712]{1,0:T(8,128)(2,1)S(1)} concatenate(bf16[4,3712]{1,0:T(4,128)(2,1)S(1)} %shard_map.109, bf16[4,3712]{1,0:T(4,128)(2,1)S(1)} %collective-permute-done, bf16[8,3712]{1,0:T(8,128)(2,1)S(1)} %collective-permute-done.1, bf16[16,3712]{1,0:T(8,128)(2,1)S(1)} %collective-permute-done.2, bf16[32,3712]{1,0:T(8,128)(2,1)} %collective-permute-done.3), dimensions={0} | concatenate | bytes 950272 | tf_op jit(solution)/shard_map/concatenate | solution.py:211
  19.0 0.4 shard_map.113.refs_0_
  19.4 2.0 %collective-permute-start.4 = (bf16[64,512]{1,0:T(8,128)(2,1)S(1)}, bf16[64,512]{1,0:T(8,128)(2,1)S(1)}, u32[]{:S(2)}, u32[]{:S(2)}) collective-permute-start(bf16[64,512]{1,0:T(8,128)(2,1)S(1)} %shard_map.113.refs_0_), channel_id=1, source_target_pairs={{0,4},{4,0},{8,12},{12,8},{1,5},{5,1},{9,13},{13,9},{2,6},{6,2},{1... | collective-permute-start | bytes 196616 | tf_op jit(solution)/shard_map/ppermute | solution.py:148
  21.4 3.1 %collective-permute-start.5 = (bf16[64,512]{1,0:T(8,128)(2,1)S(1)}, bf16[64,512]{1,0:T(8,128)(2,1)S(1)}, u32[]{:S(2)}, u32[]{:S(2)}) collective-permute-start(bf16[64,512]{1,0:T(8,128)(2,1)S(1)} %shard_map.113.refs_0_), channel_id=1, source_target_pairs={{0,8},{4,12},{8,0},{12,4},{1,9},{5,13},{9,1},{13,5},{2,10},{6,14},... | collective-permute-start | bytes 196616 | tf_op jit(solution)/shard_map/ppermute | solution.py:148
  24.5 14.4 %shard_map.112.routed_ref = f32[64,3584]{1,0:T(8,128)S(1)} custom-call(s32[1]{0:T(128)} %bitcast.1.first_ref, bf16[64,3712]{1,0:T(8,128)(2,1)S(1)} %concatenate.18.x_ref, bf16[8,3584,256]{2,1,0:T(8,128)(2,1)} %gate_hbm.1, bf16[8,3584,256]{2,1,0:T(8,128)(2,1)} %up_hbm.1, bf16[8,256,3584]{2,1,0:T(8,128)(2,1)} %down_hbm.1, bf16[3584,256]{1,0:T(8,128)(2,1)S(1)} %shard_map.111.refs_0_), custom_call_target="tpu_custom_call" | custom-call | tf_op jit(solution)/shard_map/pallas_call | solution.py:227
  38.9 0.4 shard_map.114
  39.4 1.5 %collective-permute-done.7 = bf16[32,3584]{1,0:T(8,128)(2,1)S(1)} collective-permute-done((bf16[32,3584]{1,0:T(8,128)(2,1)S(1)}, bf16[32,3584]{1,0:T(8,128)(2,1)S(1)}, u32[]{:S(2)}, u32[]{:S(2)}) %collective-permute-start.7) | collective-permute-done | bytes 229408 | tf_op jit(solution)/shard_map/ppermute | solution.py:148
  41.0 1.6 %collective-permute-start.8 = (bf16[16,3584]{1,0:T(8,128)(2,1)S(1)}, bf16[16,3584]{1,0:T(8,128)(2,1)S(1)}, u32[]{:S(2)}, u32[]{:S(2)}) collective-permute-start(bf16[16,3584]{1,0:T(8,128)(2,1)S(1)} %slice.35), channel_id=1, source_target_pairs={{0,2},{1,3},{2,0},{3,1},{4,6},{5,7},{6,4},{7,5},{8,10},{9,11},{10,... | collective-permute-start | bytes 344072 | tf_op jit(solution)/shard_map/ppermute | solution.py:148
  42.5 3.7 %collective-permute-done.8 = bf16[16,3584]{1,0:T(8,128)(2,1)S(1)} collective-permute-done((bf16[16,3584]{1,0:T(8,128)(2,1)S(1)}, bf16[16,3584]{1,0:T(8,128)(2,1)S(1)}, u32[]{:S(2)}, u32[]{:S(2)}) %collective-permute-start.8) | collective-permute-done | bytes 114720 | tf_op jit(solution)/shard_map/ppermute | solution.py:148
  46.3 1.6 %collective-permute-start.9 = (bf16[8,3584]{1,0:T(8,128)(2,1)S(1)}, bf16[8,3584]{1,0:T(8,128)(2,1)S(1)}, u32[]{:S(2)}, u32[]{:S(2)}) collective-permute-start(bf16[8,3584]{1,0:T(8,128)(2,1)S(1)} %slice.37), channel_id=1, source_target_pairs={{0,8},{4,12},{8,0},{12,4},{1,9},{5,13},{9,1},{13,5},{2,10},{6,14},... | collective-permute-start | bytes 172040 | tf_op jit(solution)/shard_map/ppermute | solution.py:148
  47.9 3.7 %collective-permute-done.9 = bf16[8,3584]{1,0:T(8,128)(2,1)S(1)} collective-permute-done((bf16[8,3584]{1,0:T(8,128)(2,1)S(1)}, bf16[8,3584]{1,0:T(8,128)(2,1)S(1)}, u32[]{:S(2)}, u32[]{:S(2)}) %collective-permute-start.9) | collective-permute-done | bytes 57376 | tf_op jit(solution)/shard_map/ppermute | solution.py:148
  51.6 1.4 %collective-permute-start.10 = (bf16[4,3584]{1,0:T(4,128)(2,1)S(1)}, bf16[4,3584]{1,0:T(4,128)(2,1)S(1)}, u32[]{:S(2)}, u32[]{:S(2)}) collective-permute-start(bf16[4,3584]{1,0:T(4,128)(2,1)S(1)} %slice.39), channel_id=1, source_target_pairs={{0,4},{4,0},{8,12},{12,8},{1,5},{5,1},{9,13},{13,9},{2,6},{6,2},{1... | collective-permute-start | bytes 86024 | tf_op jit(solution)/shard_map/ppermute | solution.py:148
  53.0 2.5 %collective-permute-done.10 = bf16[4,3584]{1,0:T(4,128)(2,1)S(1)} collective-permute-done((bf16[4,3584]{1,0:T(4,128)(2,1)S(1)}, bf16[4,3584]{1,0:T(4,128)(2,1)S(1)}, u32[]{:S(2)}, u32[]{:S(2)}) %collective-permute-start.10) | collective-permute-done | bytes 28704 | tf_op jit(solution)/shard_map/ppermute | solution.py:148
  55.5 0.6 %add_convert_fusion.3 = bf16[4,3584]{1,0:T(4,128)(2,1)} fusion(bf16[4,3584]{1,0:T(4,128)(2,1)S(1)} %collective-permute-done.10, bf16[8,3584]{1,0:T(8,128)(2,1)S(1)} %add_convert_fusion.2), kind=kLoop, calls=%fused_computation.6 | loop fusion | flops 57344 | bytes 86016 | tf_op jit(solution)/shard_map/convert_element_type | solution.py:152
  (18 shorter events, 0.4 us)
Async XLA Ops:
  1.0 5.0 %collective-permute-start = (bf16[4,3712]{1,0:T(4,128)(2,1)S(1)}, bf16[4,3712]{1,0:T(4,128)(2,1)S(1)}, u32[]{:S(2)}, u32[]{:S(2)}) collective-permute-start(bf16[4,3712]{1,0:T(4,128)(2,1)S(1)} %shard_map.109), channel_id=1, source_target_pairs={{0,4},{4,0},{8,12},{12,8},{1,5},{5,1},{9,13},{13,9},{2,6},{6,2},{1... | collective-permute-start | bytes 89096 | tf_op jit(solution)/shard_map/ppermute | solution.py:148
  6.0 5.3 %collective-permute-start.1 = (bf16[8,3712]{1,0:T(8,128)(2,1)S(1)}, bf16[8,3712]{1,0:T(8,128)(2,1)S(1)}, u32[]{:S(2)}, u32[]{:S(2)}) collective-permute-start(bf16[8,3712]{1,0:T(8,128)(2,1)S(1)} %pad_maximum_fusion.2), channel_id=1, source_target_pairs={{0,8},{4,12},{8,0},{12,4},{1,9},{5,13},{9,1},{13,5},{2,10},{6,14},... | collective-permute-start | bytes 178184 | tf_op jit(solution)/shard_map/ppermute | solution.py:148
  11.3 4.9 %collective-permute-start.2 = (bf16[16,3712]{1,0:T(8,128)(2,1)S(1)}, bf16[16,3712]{1,0:T(8,128)(2,1)S(1)}, u32[]{:S(2)}, u32[]{:S(2)}) collective-permute-start(bf16[16,3712]{1,0:T(8,128)(2,1)S(1)} %pad_maximum_fusion.1.rows_ref), channel_id=1, source_target_pairs={{0,2},{1,3},{2,0},{3,1},{4,6},{5,7},{6,4},{7,5},{8,10},{9,11},{10,... | collective-permute-start | bytes 356360 | tf_op jit(solution)/shard_map/ppermute | solution.py:148
  16.2 1.7 %collective-permute-start.3 = (bf16[32,3712]{1,0:T(8,128)(2,1)S(1)}, bf16[32,3712]{1,0:T(8,128)(2,1)}, u32[]{:S(2)}, u32[]{:S(2)}) collective-permute-start(bf16[32,3712]{1,0:T(8,128)(2,1)S(1)} %pad_maximum_fusion.rows_ref), channel_id=1, source_target_pairs={{0,1},{1,0},{2,3},{3,2},{4,5},{5,4},{6,7},{7,6},{8,9},{9,8},{10,11... | collective-permute-start | bytes 712712 | tf_op jit(solution)/shard_map/ppermute | solution.py:148
  19.4 19.5 %collective-permute-start.4 = (bf16[64,512]{1,0:T(8,128)(2,1)S(1)}, bf16[64,512]{1,0:T(8,128)(2,1)S(1)}, u32[]{:S(2)}, u32[]{:S(2)}) collective-permute-start(bf16[64,512]{1,0:T(8,128)(2,1)S(1)} %shard_map.113.refs_0_), channel_id=1, source_target_pairs={{0,4},{4,0},{8,12},{12,8},{1,5},{5,1},{9,13},{13,9},{2,6},{6,2},{1... | collective-permute-start | bytes 196616 | tf_op jit(solution)/shard_map/ppermute | solution.py:148
  21.4 17.5 %collective-permute-start.5 = (bf16[64,512]{1,0:T(8,128)(2,1)S(1)}, bf16[64,512]{1,0:T(8,128)(2,1)S(1)}, u32[]{:S(2)}, u32[]{:S(2)}) collective-permute-start(bf16[64,512]{1,0:T(8,128)(2,1)S(1)} %shard_map.113.refs_0_), channel_id=1, source_target_pairs={{0,8},{4,12},{8,0},{12,4},{1,9},{5,13},{9,1},{13,5},{2,10},{6,14},... | collective-permute-start | bytes 196616 | tf_op jit(solution)/shard_map/ppermute | solution.py:148
  24.5 14.4 %collective-permute-start.6 = (bf16[64,512]{1,0:T(8,128)(2,1)S(1)}, bf16[64,512]{1,0:T(8,128)(2,1)S(1)}, u32[]{:S(2)}, u32[]{:S(2)}) collective-permute-start(bf16[64,512]{1,0:T(8,128)(2,1)S(1)} %shard_map.113.refs_0_), channel_id=1, source_target_pairs={{0,12},{4,8},{8,4},{12,0},{1,13},{5,9},{9,5},{13,1},{2,14},{6,10},... | collective-permute-start | bytes 196616 | tf_op jit(solution)/shard_map/ppermute | solution.py:148
  24.5 14.4 %copy-start = (bf16[256,896]{1,0:T(8,128)(2,1)S(1)}, bf16[256,896]{1,0:T(8,128)(2,1)}, u32[]{:S(2)}) copy-start(bf16[256,896]{1,0:T(8,128)(2,1)} %down_ref.1) | copy-start | bytes 1376260
  39.3 1.6 %collective-permute-start.7 = (bf16[32,3584]{1,0:T(8,128)(2,1)S(1)}, bf16[32,3584]{1,0:T(8,128)(2,1)S(1)}, u32[]{:S(2)}, u32[]{:S(2)}) collective-permute-start(bf16[32,3584]{1,0:T(8,128)(2,1)S(1)} %slice.33), channel_id=1, source_target_pairs={{0,1},{1,0},{2,3},{3,2},{4,5},{5,4},{6,7},{7,6},{8,9},{9,8},{10,11... | collective-permute-start | bytes 688136 | tf_op jit(solution)/shard_map/ppermute | solution.py:148
  41.0 5.3 %collective-permute-start.8 = (bf16[16,3584]{1,0:T(8,128)(2,1)S(1)}, bf16[16,3584]{1,0:T(8,128)(2,1)S(1)}, u32[]{:S(2)}, u32[]{:S(2)}) collective-permute-start(bf16[16,3584]{1,0:T(8,128)(2,1)S(1)} %slice.35), channel_id=1, source_target_pairs={{0,2},{1,3},{2,0},{3,1},{4,6},{5,7},{6,4},{7,5},{8,10},{9,11},{10,... | collective-permute-start | bytes 344072 | tf_op jit(solution)/shard_map/ppermute | solution.py:148
  46.3 5.3 %collective-permute-start.9 = (bf16[8,3584]{1,0:T(8,128)(2,1)S(1)}, bf16[8,3584]{1,0:T(8,128)(2,1)S(1)}, u32[]{:S(2)}, u32[]{:S(2)}) collective-permute-start(bf16[8,3584]{1,0:T(8,128)(2,1)S(1)} %slice.37), channel_id=1, source_target_pairs={{0,8},{4,12},{8,0},{12,4},{1,9},{5,13},{9,1},{13,5},{2,10},{6,14},... | collective-permute-start | bytes 172040 | tf_op jit(solution)/shard_map/ppermute | solution.py:148
  51.6 3.9 %collective-permute-start.10 = (bf16[4,3584]{1,0:T(4,128)(2,1)S(1)}, bf16[4,3584]{1,0:T(4,128)(2,1)S(1)}, u32[]{:S(2)}, u32[]{:S(2)}) collective-permute-start(bf16[4,3584]{1,0:T(4,128)(2,1)S(1)} %slice.39), channel_id=1, source_target_pairs={{0,4},{4,0},{8,12},{12,8},{1,5},{5,1},{9,13},{13,9},{2,6},{6,2},{1... | collective-permute-start | bytes 86024 | tf_op jit(solution)/shard_map/ppermute | solution.py:148

commit v4 on v3

--- a/solution.py
+++ b/solution.py
@@ -11,10 +11,10 @@
 NODE_GROUPS = 8
 LANES = 128
 MIB = 2**20
-NEAR_PLAN = (0, 0, 0, 1)
-
-
-def pack_kernel(per_group, *refs):
+NEAR_PLAN = (2, 2, 4, 1)
+
+
+def pack_kernel(per_group, node_ref, *refs):
     count = len(refs) // 2 - 1
     sources, out_ref, staged, sems = refs[:count], refs[count], refs[count + 1 : -1], refs[-1]
     copies = [
@@ -48,18 +48,18 @@
     out_ref[:, count:] = total.astype(jnp.bfloat16)
 
 
-def shared_in_kernel(start_ref, x_ref, gate_ref, up_ref, out_ref):
+def shared_in_kernel(node_ref, x_ref, gate_ref, up_ref, out_ref):
     contract = (((1,), (1,)), ((), ()))
     block, slab = gate_ref.shape
     x = x_ref[...]
     if x.shape[1] != slab:
-        x = x_ref[:, pl.ds(pl.multiple_of(start_ref[0], LANES), slab)]
+        x = x_ref[:, pl.ds(pl.multiple_of(node_ref[0] * slab, LANES), slab)]
     for i, ref in enumerate((gate_ref, up_ref)):
         part = lax.dot_general(x, ref[...], contract, preferred_element_type=jnp.float32)
         out_ref[:, i * block : (i + 1) * block] = part.astype(jnp.bfloat16)
 
 
-def routed_kernel(near_count, first_ref, x_ref, gate_hbm, up_hbm, down_hbm, *refs):
+def routed_kernel(near_count, node_ref, x_ref, gate_hbm, up_hbm, down_hbm, *refs):
     near, out_ref = refs[:near_count], refs[near_count]
     far_refs, sems = refs[near_count + 1 : -1], refs[-1]
     held, count, _ = gate_hbm.shape
@@ -80,7 +80,7 @@
     weights = x_ref[:, count:].astype(jnp.float32)
     lane = lax.broadcasted_iota(jnp.int32, weights.shape, 1)
     for e in range(held):
-        chosen = jnp.where(lane == first_ref[0] + e, weights, 0.0)
+        chosen = jnp.where(lane == node_ref[0] * held + e, weights, 0.0)
         weight = jnp.sum(chosen, axis=1, keepdims=True)
         gate = jnp.dot(x, fetch(3 * e), preferred_element_type=jnp.float32)
         up = jnp.dot(x, fetch(3 * e + 1), preferred_element_type=jnp.float32)
@@ -92,7 +92,7 @@
             out_ref[...] += term
 
 
-def shared_out_kernel(tokens, start_ref, routed_ref, down_ref, *refs):
+def shared_out_kernel(tokens, node_ref, routed_ref, down_ref, *refs):
     parts, out_ref = refs[:-1], refs[-1]
     block, slab = down_ref.shape
     count, width = out_ref.shape
@@ -108,7 +108,7 @@
         out_ref[...] = (routed_ref[...] + shared).astype(jnp.bfloat16)
     else:
         out_ref[...] = routed_ref[...].astype(jnp.bfloat16)
-        columns = pl.ds(pl.multiple_of(start_ref[0], LANES), slab)
+        columns = pl.ds(pl.multiple_of(node_ref[0] * slab, LANES), slab)
         out_ref[:, columns] = (routed_ref[:, columns] + shared).astype(jnp.bfloat16)
 
 
@@ -137,6 +137,22 @@
             vmem_limit_bytes=2 * sum(math.prod(shape) for shape in shapes) + MIB
         ),
     )(rows, *(far(w) for w, _ in wanted))
+
+
+def join_kernel(one_ref, other_ref, out_ref):
+    both = [ref[...].astype(jnp.float32) for ref in (one_ref, other_ref)]
+    out_ref[...] = jnp.concatenate(both, axis=0).astype(jnp.bfloat16)
+
+
+def join(one, other):
+    vmem = pl.BlockSpec(memory_space=pltpu.VMEM)
+    return pl.pallas_call(
+        join_kernel,
+        out_shape=jax.ShapeDtypeStruct((2 * one.shape[0], one.shape[1]), one.dtype),
+        in_specs=[vmem, vmem],
+        out_specs=vmem,
+        compiler_params=pltpu.CompilerParams(vmem_limit_bytes=24 * one.size + MIB),
+    )(one, other)
 
 
 def far(value):
@@ -168,6 +184,7 @@
     node_count = lax.axis_size("node")
     local_count = lax.axis_size("local")
     node = lax.axis_index("node")
+    place = node.astype(jnp.int32).reshape(1)
     token_count, feature_count = hidden_states.shape
     held, _, block = expert_gate.shape
     expert_total = held * node_count
@@ -186,12 +203,12 @@
     rows = pl.pallas_call(
         functools.partial(pack_kernel, per_group),
         out_shape=jax.ShapeDtypeStruct((token_count, width), jnp.bfloat16),
-        in_specs=[hbm] * len(small),
+        in_specs=[smem] + [hbm] * len(small),
         out_specs=vmem,
         scratch_shapes=[pltpu.VMEM(a.shape, a.dtype) for a in small]
         + [pltpu.SemaphoreType.DMA((len(small),))],
         compiler_params=params,
-    )(*(far(a) for a in small))
+    )(place, *(far(a) for a in small))
 
     weights = [(w, e) for e in range(held) for w in (expert_gate, expert_up, expert_down)]
     stages = [("node", 1 << i) for i in range(node_count.bit_length() - 1)]
@@ -208,18 +225,17 @@
             ready += got[: len(wanted)]
             if extra:
                 shared_gate, shared_up = got[len(wanted) :]
-        rows = jnp.concatenate([rows, other], axis=0)
+        rows = join(rows, other)
     row_count = rows.shape[0]
 
-    start = (node * slab).astype(jnp.int32)
     aligned = slab % LANES == 0
-    mine = rows if aligned else lax.dynamic_slice_in_dim(rows, start, slab, axis=1)
+    mine = rows if aligned else lax.dynamic_slice_in_dim(rows, node * slab, slab, axis=1)
     shared_part = pl.pallas_call(
         shared_in_kernel,
         out_shape=jax.ShapeDtypeStruct((row_count, 2 * shared_block), jnp.bfloat16),
         in_specs=[smem, vmem, vmem, vmem],
         compiler_params=params,
-    )(start.reshape(1), mine, shared_gate, shared_up)
+    )(place, mine, shared_gate, shared_up)
     parts = [shared_part] + [exchange(shared_part, "node", k) for k in range(1, node_count)]
 
     late = weights[len(ready) :]
@@ -235,7 +251,7 @@
             vmem_limit_bytes=late_bytes + 12 * row_count * width + 4 * MIB
         ),
     )(
-        (node * held).astype(jnp.int32).reshape(1),
+        place,
         rows,
         *(far(w) for w in (expert_gate, expert_up, expert_down)),
         *ready,
@@ -243,7 +259,7 @@
 
     if not aligned:
         shared_down = lax.dynamic_update_slice_in_dim(
-            jnp.zeros((shared_block, feature_count), shared_down.dtype), shared_down, start, axis=1
+            jnp.zeros((shared_block, feature_count), shared_down.dtype), shared_down, node * slab, axis=1
         )
     out = pl.pallas_call(
         functools.partial(shared_out_kernel, token_count),
@@ -251,7 +267,7 @@
         in_specs=[smem] + [vmem] * (2 + node_count),
         out_specs=vmem,
         compiler_params=params,
-    )(start.reshape(1), routed, shared_down, *parts)
+    )(place, routed, shared_down, *parts)
 
     bit = 1
     while bit < local_count:

time: 56.4 us -> 52.5 us (0.931)
  waiting for transfers between devices: 17.4 us -> 11.7 us
  Pallas kernels: 18.8 us -> 22.5 us
  local copies, waits for them, and re-layouts: 1.14 us -> 0.06 us
  starting transfers between devices: 17.9 us -> 17.1 us
    pallas_call x2 -> x4, Pallas kernels: 2.68 us -> 9.01 us  [bring(): pl.pallas_call(functools.partial(bring_kernel, [e for _, e in wanted]), o...]
    ppermute x11, waiting for transfers between devices: 17.4 us -> 11.7 us  [exchange(): return lax.ppermute(value, axis, [(i, i ^ bit) for i in range(size)])]
    pallas_call x1, Pallas kernels: 14.4 us -> 11.7 us  [local(): pl.pallas_call(functools.partial(routed_kernel, len(ready)), out_shape=ja...]
    concatenate x1 -> x0, local copies, waits for them, and re-layouts: 1.08 us -> none  [local(): rows = jnp.concatenate([rows, other], axis=0)]
    ppermute x11, starting transfers between devices: 17.9 us -> 17.1 us  [exchange(): return lax.ppermute(value, axis, [(i, i ^ bit) for i in range(size)])]
  transfers between devices with their start and end apart: 11 -> 11, of which waited for: 8 -> 5; matrix products, arithmetic and copies ran while one was open for 0% -> 0% of each run, Pallas kernels for 30% -> 40%
where the time goes in v4:
time: 52.5 us; the launch traced here: 52.3 us
  Pallas kernels  22.5 us (43%)
  starting transfers between devices  17.1 us (33%)
  waiting for transfers between devices  11.7 us (22%)
  other arithmetic  0.73 us (1%)
    ppermute x11, starting transfers between devices, exchange(): return lax.ppermute(value, axis, [(i, i ^ bit) for i in range(size)])  17.1 us
    pallas_call x1, Pallas kernels, local(): pl.pallas_call(functools.partial(routed_kernel, len(ready)), out_shape=ja...  11.7 us
    ppermute x11, waiting for transfers between devices, exchange(): return lax.ppermute(value, axis, [(i, i ^ bit) for i in range(size)])  11.7 us
    pallas_call x4, Pallas kernels, bring(): pl.pallas_call(functools.partial(bring_kernel, [e for _, e in wanted]), o...  9.01 us
  transfers between devices with their start and end apart: 11, of which 5 were waited for; matrix products, arithmetic and copies ran while one was open for 0% of the time, Pallas kernels for 40%

profile of v4, /device:TPU:0, one launch (start us, length us, event | category | flops | bytes accessed | tf_op | source)
XLA Modules:
  0.0 52.3 jit_solution(12490885258245174378)
XLA Ops:
  0.0 1.0 %shard_map.109.rows_ref.one_ref = bf16[4,3712]{1,0:T(4,128)(2,1)S(1)} custom-call(s32[1]{0:T(128)} %bitcast.node_ref, bf16[4,3584]{1,0:T(4,128)(2,1)} %refs_0_.5, f32[3584]{0:T(1024)} %refs_1_.4, s32[4,4]{1,0:T(4,128)} %refs_2_.2, s32[4,8]{1,0:T(4,128)} %refs_3_.2, bf16[4,8]{1,0:T(4,128)(2,1)} %refs_4_.2), custom_call_target="tpu_custom_call" | custom-call | tf_op jit(solution)/shard_map/pallas_call | solution.py:203
  1.0 3.1 %collective-permute-start = (bf16[4,3712]{1,0:T(4,128)(2,1)S(1)}, bf16[4,3712]{1,0:T(4,128)(2,1)S(1)}, u32[]{:S(2)}, u32[]{:S(2)}) collective-permute-start(bf16[4,3712]{1,0:T(4,128)(2,1)S(1)} %shard_map.109.rows_ref.one_ref), channel_id=1, source_target_pairs={{0,4},{4,0},{8,12},{12,8},{1,5},{5,1},{9,13},{13,9},{2,6},{6,2},{1... | collective-permute-start | bytes 89096 | tf_op jit(solution)/shard_map/ppermute | solution.py:164
  4.1 2.1 %shard_map.110 = (bf16[3584,256]{1,0:T(8,128)(2,1)S(1)}, bf16[3584,256]{1,0:T(8,128)(2,1)S(1)}) custom-call(bf16[4,3712]{1,0:T(4,128)(2,1)S(1)} %shard_map.109.rows_ref.one_ref, bf16[8,3584,256]{2,1,0:T(8,128)(2,1)} %gate_hbm.1, bf16[8,3584,256]{2,1,0:T(8,128)(2,1)} %up_hbm.1), custom_call_target="tpu_custom_call" | custom-call | tf_op jit(solution)/shard_map/pallas_call | solution.py:130
  6.2 2.9 %collective-permute-start.1 = (bf16[8,3712]{1,0:T(8,128)(2,1)S(1)}, bf16[8,3712]{1,0:T(8,128)(2,1)S(1)}, u32[]{:S(2)}, u32[]{:S(2)}) collective-permute-start(bf16[8,3712]{1,0:T(8,128)(2,1)S(1)} %shard_map.111.rows_ref.one_ref), channel_id=1, source_target_pairs={{0,8},{4,12},{8,0},{12,4},{1,9},{5,13},{9,1},{13,5},{2,10},{6,14},... | collective-permute-start | bytes 178184 | tf_op jit(solution)/shard_map/ppermute | solution.py:164
  9.0 2.1 %shard_map.112 = (bf16[256,3584]{1,0:T(8,128)(2,1)S(1)}, bf16[3584,256]{1,0:T(8,128)(2,1)S(1)}) custom-call(bf16[8,3712]{1,0:T(8,128)(2,1)S(1)} %shard_map.111.rows_ref.one_ref, bf16[8,256,3584]{2,1,0:T(8,128)(2,1)} %down_hbm.1, bf16[8,3584,256]{2,1,0:T(8,128)(2,1)} %gate_hbm.1), custom_call_target="tpu_custom_call" | custom-call | tf_op jit(solution)/shard_map/pallas_call | solution.py:130
  11.1 0.2 collective-permute-done.1.other_ref
  11.3 1.8 %collective-permute-start.2 = (bf16[16,3712]{1,0:T(8,128)(2,1)S(1)}, bf16[16,3712]{1,0:T(8,128)(2,1)S(1)}, u32[]{:S(2)}, u32[]{:S(2)}) collective-permute-start(bf16[16,3712]{1,0:T(8,128)(2,1)S(1)} %shard_map.113.rows_ref.one_ref), channel_id=1, source_target_pairs={{0,2},{1,3},{2,0},{3,1},{4,6},{5,7},{6,4},{7,5},{8,10},{9,11},{10,... | collective-permute-start | bytes 356360 | tf_op jit(solution)/shard_map/ppermute | solution.py:164
  13.1 3.4 %shard_map.114 = (bf16[3584,256]{1,0:T(8,128)(2,1)S(1)}, bf16[256,3584]{1,0:T(8,128)(2,1)S(1)}, bf16[3584,256]{1,0:T(8,128)(2,1)S(1)}, bf16[3584,256]{1,0:T(8,12...) custom-call(bf16[16,3712]{1,0:T(8,128)(2,1)S(1)} %shard_map.113.rows_ref.one_ref, ...), custom_call_target="tpu_custom_call" | custom-call | tf_op jit(solution)/shard_map/pallas_call | solution.py:130
  16.5 0.1 collective-permute-start.3
  16.6 1.5 %shard_map.116.refs_8_ = bf16[256,3584]{1,0:T(8,128)(2,1)S(1)} custom-call(bf16[32,3712]{1,0:T(8,128)(2,1)S(1)} %shard_map.115.rows_ref.one_ref, bf16[8,256,3584]{2,1,0:T(8,128)(2,1)} %down_hbm.1), custom_call_target="tpu_custom_call" | custom-call | tf_op jit(solution)/shard_map/pallas_call | solution.py:130
  18.2 0.4 shard_map.119.refs_0_
  18.6 1.6 %collective-permute-start.4 = (bf16[64,512]{1,0:T(8,128)(2,1)S(1)}, bf16[64,512]{1,0:T(8,128)(2,1)S(1)}, u32[]{:S(2)}, u32[]{:S(2)}) collective-permute-start(bf16[64,512]{1,0:T(8,128)(2,1)S(1)} %shard_map.119.refs_0_), channel_id=1, source_target_pairs={{0,4},{4,0},{8,12},{12,8},{1,5},{5,1},{9,13},{13,9},{2,6},{6,2},{1... | collective-permute-start | bytes 196616 | tf_op jit(solution)/shard_map/ppermute | solution.py:164
  20.2 3.1 %collective-permute-start.5 = (bf16[64,512]{1,0:T(8,128)(2,1)S(1)}, bf16[64,512]{1,0:T(8,128)(2,1)S(1)}, u32[]{:S(2)}, u32[]{:S(2)}) collective-permute-start(bf16[64,512]{1,0:T(8,128)(2,1)S(1)} %shard_map.119.refs_0_), channel_id=1, source_target_pairs={{0,8},{4,12},{8,0},{12,4},{1,9},{5,13},{9,1},{13,5},{2,10},{6,14},... | collective-permute-start | bytes 196616 | tf_op jit(solution)/shard_map/ppermute | solution.py:164
  23.4 11.7 %shard_map.118.routed_ref = f32[64,3584]{1,0:T(8,128)S(1)} custom-call(s32[1]{0:T(128)} %bitcast.node_ref, bf16[64,3712]{1,0:T(8,128)(2,1)S(1)} %shard_map.117.x_ref, bf16[8,3584,256]{2,1,0:T(8,128)(2,1)} %gate_hbm.1, bf16[8,3584,256]{2,1,0:T(8,128)(2,1)} %up_hbm.1, bf16[8,256,3584]{2,1,0:T(8,128)(2,1)} %down_hbm.1, ...), custom_call_target="tpu_custom_call" | custom-call | tf_op jit(solution)/shard_map/pallas_call | solution.py:243
  35.1 0.4 shard_map.120
  35.5 0.1 collective-permute-start.7
  35.6 1.5 %collective-permute-done.7 = bf16[32,3584]{1,0:T(8,128)(2,1)S(1)} collective-permute-done((bf16[32,3584]{1,0:T(8,128)(2,1)S(1)}, bf16[32,3584]{1,0:T(8,128)(2,1)S(1)}, u32[]{:S(2)}, u32[]{:S(2)}) %collective-permute-start.7) | collective-permute-done | bytes 229408 | tf_op jit(solution)/shard_map/ppermute | solution.py:164
  37.1 1.5 %collective-permute-start.8 = (bf16[16,3584]{1,0:T(8,128)(2,1)S(1)}, bf16[16,3584]{1,0:T(8,128)(2,1)S(1)}, u32[]{:S(2)}, u32[]{:S(2)}) collective-permute-start(bf16[16,3584]{1,0:T(8,128)(2,1)S(1)} %slice.35), channel_id=1, source_target_pairs={{0,2},{1,3},{2,0},{3,1},{4,6},{5,7},{6,4},{7,5},{8,10},{9,11},{10,... | collective-permute-start | bytes 344072 | tf_op jit(solution)/shard_map/ppermute | solution.py:164
  38.6 3.7 %collective-permute-done.8 = bf16[16,3584]{1,0:T(8,128)(2,1)S(1)} collective-permute-done((bf16[16,3584]{1,0:T(8,128)(2,1)S(1)}, bf16[16,3584]{1,0:T(8,128)(2,1)S(1)}, u32[]{:S(2)}, u32[]{:S(2)}) %collective-permute-start.8) | collective-permute-done | bytes 114720 | tf_op jit(solution)/shard_map/ppermute | solution.py:164
  42.4 1.6 %collective-permute-start.9 = (bf16[8,3584]{1,0:T(8,128)(2,1)S(1)}, bf16[8,3584]{1,0:T(8,128)(2,1)S(1)}, u32[]{:S(2)}, u32[]{:S(2)}) collective-permute-start(bf16[8,3584]{1,0:T(8,128)(2,1)S(1)} %slice.37), channel_id=1, source_target_pairs={{0,8},{4,12},{8,0},{12,4},{1,9},{5,13},{9,1},{13,5},{2,10},{6,14},... | collective-permute-start | bytes 172040 | tf_op jit(solution)/shard_map/ppermute | solution.py:164
  44.0 3.7 %collective-permute-done.9 = bf16[8,3584]{1,0:T(8,128)(2,1)S(1)} collective-permute-done((bf16[8,3584]{1,0:T(8,128)(2,1)S(1)}, bf16[8,3584]{1,0:T(8,128)(2,1)S(1)}, u32[]{:S(2)}, u32[]{:S(2)}) %collective-permute-start.9) | collective-permute-done | bytes 57376 | tf_op jit(solution)/shard_map/ppermute | solution.py:164
  47.7 1.4 %collective-permute-start.10 = (bf16[4,3584]{1,0:T(4,128)(2,1)S(1)}, bf16[4,3584]{1,0:T(4,128)(2,1)S(1)}, u32[]{:S(2)}, u32[]{:S(2)}) collective-permute-start(bf16[4,3584]{1,0:T(4,128)(2,1)S(1)} %slice.39), channel_id=1, source_target_pairs={{0,4},{4,0},{8,12},{12,8},{1,5},{5,1},{9,13},{13,9},{2,6},{6,2},{1... | collective-permute-start | bytes 86024 | tf_op jit(solution)/shard_map/ppermute | solution.py:164
  49.1 2.5 %collective-permute-done.10 = bf16[4,3584]{1,0:T(4,128)(2,1)S(1)} collective-permute-done((bf16[4,3584]{1,0:T(4,128)(2,1)S(1)}, bf16[4,3584]{1,0:T(4,128)(2,1)S(1)}, u32[]{:S(2)}, u32[]{:S(2)}) %collective-permute-start.10) | collective-permute-done | bytes 28704 | tf_op jit(solution)/shard_map/ppermute | solution.py:164
  51.7 0.6 %add_convert_fusion.3 = bf16[4,3584]{1,0:T(4,128)(2,1)} fusion(bf16[4,3584]{1,0:T(4,128)(2,1)S(1)} %collective-permute-done.10, bf16[8,3584]{1,0:T(8,128)(2,1)S(1)} %add_convert_fusion.2), kind=kLoop, calls=%fused_computation.3 | loop fusion | flops 57344 | bytes 86016 | tf_op jit(solution)/shard_map/convert_element_type | solution.py:168
  (20 shorter events, 0.3 us)
Async XLA Ops:
  1.0 5.2 %collective-permute-start = (bf16[4,3712]{1,0:T(4,128)(2,1)S(1)}, bf16[4,3712]{1,0:T(4,128)(2,1)S(1)}, u32[]{:S(2)}, u32[]{:S(2)}) collective-permute-start(bf16[4,3712]{1,0:T(4,128)(2,1)S(1)} %shard_map.109.rows_ref.one_ref), channel_id=1, source_target_pairs={{0,4},{4,0},{8,12},{12,8},{1,5},{5,1},{9,13},{13,9},{2,6},{6,2},{1... | collective-permute-start | bytes 89096 | tf_op jit(solution)/shard_map/ppermute | solution.py:164
  6.2 5.2 %collective-permute-start.1 = (bf16[8,3712]{1,0:T(8,128)(2,1)S(1)}, bf16[8,3712]{1,0:T(8,128)(2,1)S(1)}, u32[]{:S(2)}, u32[]{:S(2)}) collective-permute-start(bf16[8,3712]{1,0:T(8,128)(2,1)S(1)} %shard_map.111.rows_ref.one_ref), channel_id=1, source_target_pairs={{0,8},{4,12},{8,0},{12,4},{1,9},{5,13},{9,1},{13,5},{2,10},{6,14},... | collective-permute-start | bytes 178184 | tf_op jit(solution)/shard_map/ppermute | solution.py:164
  11.3 5.1 %collective-permute-start.2 = (bf16[16,3712]{1,0:T(8,128)(2,1)S(1)}, bf16[16,3712]{1,0:T(8,128)(2,1)S(1)}, u32[]{:S(2)}, u32[]{:S(2)}) collective-permute-start(bf16[16,3712]{1,0:T(8,128)(2,1)S(1)} %shard_map.113.rows_ref.one_ref), channel_id=1, source_target_pairs={{0,2},{1,3},{2,0},{3,1},{4,6},{5,7},{6,4},{7,5},{8,10},{9,11},{10,... | collective-permute-start | bytes 356360 | tf_op jit(solution)/shard_map/ppermute | solution.py:164
  16.5 1.6 %collective-permute-start.3 = (bf16[32,3712]{1,0:T(8,128)(2,1)S(1)}, bf16[32,3712]{1,0:T(8,128)(2,1)S(1)}, u32[]{:S(2)}, u32[]{:S(2)}) collective-permute-start(bf16[32,3712]{1,0:T(8,128)(2,1)S(1)} %shard_map.115.rows_ref.one_ref), channel_id=1, source_target_pairs={{0,1},{1,0},{2,3},{3,2},{4,5},{5,4},{6,7},{7,6},{8,9},{9,8},{10,11... | collective-permute-start | bytes 712712 | tf_op jit(solution)/shard_map/ppermute | solution.py:164
  18.6 16.5 %copy-start = (bf16[256,896]{1,0:T(8,128)(2,1)S(1)}, bf16[256,896]{1,0:T(8,128)(2,1)}, u32[]{:S(2)}) copy-start(bf16[256,896]{1,0:T(8,128)(2,1)} %down_ref.1) | copy-start | bytes 1376260
  18.6 16.4 %collective-permute-start.4 = (bf16[64,512]{1,0:T(8,128)(2,1)S(1)}, bf16[64,512]{1,0:T(8,128)(2,1)S(1)}, u32[]{:S(2)}, u32[]{:S(2)}) collective-permute-start(bf16[64,512]{1,0:T(8,128)(2,1)S(1)} %shard_map.119.refs_0_), channel_id=1, source_target_pairs={{0,4},{4,0},{8,12},{12,8},{1,5},{5,1},{9,13},{13,9},{2,6},{6,2},{1... | collective-permute-start | bytes 196616 | tf_op jit(solution)/shard_map/ppermute | solution.py:164
  20.2 14.8 %collective-permute-start.5 = (bf16[64,512]{1,0:T(8,128)(2,1)S(1)}, bf16[64,512]{1,0:T(8,128)(2,1)S(1)}, u32[]{:S(2)}, u32[]{:S(2)}) collective-permute-start(bf16[64,512]{1,0:T(8,128)(2,1)S(1)} %shard_map.119.refs_0_), channel_id=1, source_target_pairs={{0,8},{4,12},{8,0},{12,4},{1,9},{5,13},{9,1},{13,5},{2,10},{6,14},... | collective-permute-start | bytes 196616 | tf_op jit(solution)/shard_map/ppermute | solution.py:164
  23.3 11.7 %collective-permute-start.6 = (bf16[64,512]{1,0:T(8,128)(2,1)S(1)}, bf16[64,512]{1,0:T(8,128)(2,1)S(1)}, u32[]{:S(2)}, u32[]{:S(2)}) collective-permute-start(bf16[64,512]{1,0:T(8,128)(2,1)S(1)} %shard_map.119.refs_0_), channel_id=1, source_target_pairs={{0,12},{4,8},{8,4},{12,0},{1,13},{5,9},{9,5},{13,1},{2,14},{6,10},... | collective-permute-start | bytes 196616 | tf_op jit(solution)/shard_map/ppermute | solution.py:164
  35.5 1.6 %collective-permute-start.7 = (bf16[32,3584]{1,0:T(8,128)(2,1)S(1)}, bf16[32,3584]{1,0:T(8,128)(2,1)S(1)}, u32[]{:S(2)}, u32[]{:S(2)}) collective-permute-start(bf16[32,3584]{1,0:T(8,128)(2,1)S(1)} %slice.33), channel_id=1, source_target_pairs={{0,1},{1,0},{2,3},{3,2},{4,5},{5,4},{6,7},{7,6},{8,9},{9,8},{10,11... | collective-permute-start | bytes 688136 | tf_op jit(solution)/shard_map/ppermute | solution.py:164
  37.1 5.3 %collective-permute-start.8 = (bf16[16,3584]{1,0:T(8,128)(2,1)S(1)}, bf16[16,3584]{1,0:T(8,128)(2,1)S(1)}, u32[]{:S(2)}, u32[]{:S(2)}) collective-permute-start(bf16[16,3584]{1,0:T(8,128)(2,1)S(1)} %slice.35), channel_id=1, source_target_pairs={{0,2},{1,3},{2,0},{3,1},{4,6},{5,7},{6,4},{7,5},{8,10},{9,11},{10,... | collective-permute-start | bytes 344072 | tf_op jit(solution)/shard_map/ppermute | solution.py:164
  42.4 5.3 %collective-permute-start.9 = (bf16[8,3584]{1,0:T(8,128)(2,1)S(1)}, bf16[8,3584]{1,0:T(8,128)(2,1)S(1)}, u32[]{:S(2)}, u32[]{:S(2)}) collective-permute-start(bf16[8,3584]{1,0:T(8,128)(2,1)S(1)} %slice.37), channel_id=1, source_target_pairs={{0,8},{4,12},{8,0},{12,4},{1,9},{5,13},{9,1},{13,5},{2,10},{6,14},... | collective-permute-start | bytes 172040 | tf_op jit(solution)/shard_map/ppermute | solution.py:164
  47.7 3.9 %collective-permute-start.10 = (bf16[4,3584]{1,0:T(4,128)(2,1)S(1)}, bf16[4,3584]{1,0:T(4,128)(2,1)S(1)}, u32[]{:S(2)}, u32[]{:S(2)}) collective-permute-start(bf16[4,3584]{1,0:T(4,128)(2,1)S(1)} %slice.39), channel_id=1, source_target_pairs={{0,4},{4,0},{8,12},{12,8},{1,5},{5,1},{9,13},{13,9},{2,6},{6,2},{1... | collective-permute-start | bytes 86024 | tf_op jit(solution)/shard_map/ppermute | solution.py:164

commit v5 on v4

--- a/solution.py
+++ b/solution.py
@@ -11,7 +11,8 @@
 NODE_GROUPS = 8
 LANES = 128
 MIB = 2**20
-NEAR_PLAN = (2, 2, 4, 1)
+NEAR_PLAN = (0, 0, 4, 1)
+WORTH = 40 * 10**9
 
 
 def pack_kernel(per_group, node_ref, *refs):
@@ -59,37 +60,44 @@
         out_ref[:, i * block : (i + 1) * block] = part.astype(jnp.bfloat16)
 
 
-def routed_kernel(near_count, node_ref, x_ref, gate_hbm, up_hbm, down_hbm, *refs):
-    near, out_ref = refs[:near_count], refs[near_count]
+def routed_kernel(near_count, node_ref, x_ref, gate_hbm, up_ref, down_ref, *refs):
+    near_refs, out_ref = refs[:near_count], refs[near_count]
     far_refs, sems = refs[near_count + 1 : -1], refs[-1]
-    held, count, _ = gate_hbm.shape
+    held, count, _ = up_ref.shape
     copies = []
     for i, there in enumerate(far_refs):
-        e, kind = divmod(near_count + i, 3)
-        here = (gate_hbm, up_hbm, down_hbm)[kind].at[e]
-        copies.append(pltpu.make_async_copy(here, there, sems.at[i]))
+        copies.append(pltpu.make_async_copy(gate_hbm.at[near_count + i], there, sems.at[i]))
         copies[-1].start()
-
-    def fetch(index):
-        if index < near_count:
-            return near[index][...]
-        copies[index - near_count].wait()
-        return far_refs[index - near_count][...]
 
     x = x_ref[:, :count]
     weights = x_ref[:, count:].astype(jnp.float32)
     lane = lax.broadcasted_iota(jnp.int32, weights.shape, 1)
+
+    def gate_and_up(e):
+        if e < near_count:
+            gate_ref = near_refs[e]
+        else:
+            gate_ref = far_refs[e - near_count]
+            copies[e - near_count].wait()
+        return [
+            jnp.dot(x, weight, preferred_element_type=jnp.float32)
+            for weight in (gate_ref[...], up_ref[e])
+        ]
+
+    gate, up = gate_and_up(0)
     for e in range(held):
         chosen = jnp.where(lane == node_ref[0] * held + e, weights, 0.0)
         weight = jnp.sum(chosen, axis=1, keepdims=True)
-        gate = jnp.dot(x, fetch(3 * e), preferred_element_type=jnp.float32)
-        up = jnp.dot(x, fetch(3 * e + 1), preferred_element_type=jnp.float32)
+        if e + 1 < held:
+            later = gate_and_up(e + 1)
         hidden = (jax.nn.silu(gate) * up * weight).astype(jnp.bfloat16)
-        term = jnp.dot(hidden, fetch(3 * e + 2), preferred_element_type=jnp.float32)
+        term = jnp.dot(hidden, down_ref[e], preferred_element_type=jnp.float32)
         if e == 0:
             out_ref[...] = term
         else:
             out_ref[...] += term
+        if e + 1 < held:
+            gate, up = later
 
 
 def shared_out_kernel(tokens, node_ref, routed_ref, down_ref, *refs):
@@ -153,6 +161,10 @@
         out_specs=vmem,
         compiler_params=pltpu.CompilerParams(vmem_limit_bytes=24 * one.size + MIB),
     )(one, other)
+
+
+def near(value):
+    return pltpu.with_memory_space_constraint(value, pltpu.VMEM)
 
 
 def far(value):
@@ -208,9 +220,10 @@
         scratch_shapes=[pltpu.VMEM(a.shape, a.dtype) for a in small]
         + [pltpu.SemaphoreType.DMA((len(small),))],
         compiler_params=params,
+        cost_estimate=pl.CostEstimate(flops=WORTH, transcendentals=0, bytes_accessed=0),
     )(place, *(far(a) for a in small))
 
-    weights = [(w, e) for e in range(held) for w in (expert_gate, expert_up, expert_down)]
+    weights = [(expert_gate, e) for e in range(held)]
     stages = [("node", 1 << i) for i in range(node_count.bit_length() - 1)]
     stages += [("local", 1 << i) for i in reversed(range(local_count.bit_length() - 1))]
     ready = []
@@ -243,7 +256,7 @@
     routed = pl.pallas_call(
         functools.partial(routed_kernel, len(ready)),
         out_shape=jax.ShapeDtypeStruct((row_count, feature_count), jnp.float32),
-        in_specs=[smem, vmem, hbm, hbm, hbm] + [vmem] * len(ready),
+        in_specs=[smem, vmem, hbm, vmem, vmem] + [vmem] * len(ready),
         out_specs=vmem,
         scratch_shapes=[pltpu.VMEM(w.shape[1:], jnp.bfloat16) for w, _ in late]
         + [pltpu.SemaphoreType.DMA((max(len(late), 1),))],
@@ -253,7 +266,9 @@
     )(
         place,
         rows,
-        *(far(w) for w in (expert_gate, expert_up, expert_down)),
+        far(expert_gate),
+        near(expert_up),
+        near(expert_down),
         *ready,
     )
 

time: 52.5 us -> 49.2 us (0.937)
  Pallas kernels: 22.5 us -> 14.9 us
  waiting for transfers between devices: 11.7 us -> 15.5 us
    pallas_call x4 -> x2, Pallas kernels: 9.01 us -> 4.88 us  [bring(): pl.pallas_call(functools.partial(bring_kernel, [e for _, e in wanted]), o...]
    ppermute x11, waiting for transfers between devices: 11.7 us -> 15.5 us  [exchange(): return lax.ppermute(value, axis, [(i, i ^ bit) for i in range(size)])]
    pallas_call x1, Pallas kernels: 11.7 us -> 8.12 us  [local(): pl.pallas_call(functools.partial(routed_kernel, len(ready)), out_shape=ja...]
  transfers between devices with their start and end apart: 11 -> 11, of which waited for: 5 -> 6; matrix products, arithmetic and copies ran while one was open for 0% -> 0% of each run, Pallas kernels for 40% -> 27%
where the time goes in v5:
time: 49.2 us; the launch traced here: 49 us
  starting transfers between devices  17.5 us (36%)
  waiting for transfers between devices  15.5 us (32%)
  Pallas kernels  14.9 us (30%)
  other arithmetic  0.73 us (1%)
    ppermute x11, starting transfers between devices, exchange(): return lax.ppermute(value, axis, [(i, i ^ bit) for i in range(size)])  17.5 us
    ppermute x11, waiting for transfers between devices, exchange(): return lax.ppermute(value, axis, [(i, i ^ bit) for i in range(size)])  15.5 us
    pallas_call x1, Pallas kernels, local(): pl.pallas_call(functools.partial(routed_kernel, len(ready)), out_shape=ja...  8.12 us
    pallas_call x2, Pallas kernels, bring(): pl.pallas_call(functools.partial(bring_kernel, [e for _, e in wanted]), o...  4.88 us
    pallas_call x1, Pallas kernels, local(): pl.pallas_call(functools.partial(pack_kernel, per_group), out_shape=jax.S...  1.11 us
  transfers between devices with their start and end apart: 11, of which 6 were waited for; matrix products, arithmetic and copies ran while one was open for 0% of the time, Pallas kernels for 27%

profile of v5, /device:TPU:0, one launch (start us, length us, event | category | flops | bytes accessed | tf_op | source)
XLA Modules:
  0.0 49.0 jit_solution(13146220426877929478)
XLA Ops:
  0.0 1.1 %shard_map.109.one_ref = bf16[4,3712]{1,0:T(4,128)(2,1)S(1)} custom-call(s32[1]{0:T(128)} %bitcast.node_ref, bf16[4,3584]{1,0:T(4,128)(2,1)} %refs_0_.3, f32[3584]{0:T(1024)} %refs_1_.2, s32[4,4]{1,0:T(4,128)} %refs_2_.2, s32[4,8]{1,0:T(4,128)} %refs_3_.2, bf16[4,8]{1,0:T(4,128)(2,1)} %refs_4_.2), custom_call_target="tpu_custom_call" | custom-call | flops 40000000000 | tf_op jit(solution)/shard_map/pallas_call | solution.py:215
  1.1 3.1 %collective-permute-start = (bf16[4,3712]{1,0:T(4,128)(2,1)S(1)}, bf16[4,3712]{1,0:T(4,128)(2,1)S(1)}, u32[]{:S(2)}, u32[]{:S(2)}) collective-permute-start(bf16[4,3712]{1,0:T(4,128)(2,1)S(1)} %shard_map.109.one_ref), channel_id=1, source_target_pairs={{0,4},{4,0},{8,12},{12,8},{1,5},{5,1},{9,13},{13,9},{2,6},{6,2},{1... | collective-permute-start | bytes 89096 | tf_op jit(solution)/shard_map/ppermute | solution.py:176
  4.2 1.9 %collective-permute-done.other_ref = bf16[4,3712]{1,0:T(4,128)(2,1)S(1)} collective-permute-done((bf16[4,3712]{1,0:T(4,128)(2,1)S(1)}, bf16[4,3712]{1,0:T(4,128)(2,1)S(1)}, u32[]{:S(2)}, u32[]{:S(2)}) %collective-permute-start) | collective-permute-done | bytes 29728 | tf_op jit(solution)/shard_map/ppermute | solution.py:176
  6.1 3.1 %collective-permute-start.1 = (bf16[8,3712]{1,0:T(8,128)(2,1)S(1)}, bf16[8,3712]{1,0:T(8,128)(2,1)S(1)}, u32[]{:S(2)}, u32[]{:S(2)}) collective-permute-start(bf16[8,3712]{1,0:T(8,128)(2,1)S(1)} %shard_map.110.one_ref), channel_id=1, source_target_pairs={{0,8},{4,12},{8,0},{12,4},{1,9},{5,13},{9,1},{13,5},{2,10},{6,14},... | collective-permute-start | bytes 178184 | tf_op jit(solution)/shard_map/ppermute | solution.py:176
  9.2 2.2 %collective-permute-done.1.other_ref = bf16[8,3712]{1,0:T(8,128)(2,1)S(1)} collective-permute-done((bf16[8,3712]{1,0:T(8,128)(2,1)S(1)}, bf16[8,3712]{1,0:T(8,128)(2,1)S(1)}, u32[]{:S(2)}, u32[]{:S(2)}) %collective-permute-start.1) | collective-permute-done | bytes 59424 | tf_op jit(solution)/shard_map/ppermute | solution.py:176
  11.5 1.9 %collective-permute-start.2 = (bf16[16,3712]{1,0:T(8,128)(2,1)S(1)}, bf16[16,3712]{1,0:T(8,128)(2,1)S(1)}, u32[]{:S(2)}, u32[]{:S(2)}) collective-permute-start(bf16[16,3712]{1,0:T(8,128)(2,1)S(1)} %shard_map.111.rows_ref.one_ref), channel_id=1, source_target_pairs={{0,2},{1,3},{2,0},{3,1},{4,6},{5,7},{6,4},{7,5},{8,10},{9,11},{10,... | collective-permute-start | bytes 356360 | tf_op jit(solution)/shard_map/ppermute | solution.py:176
  13.3 3.4 %shard_map.112 = (bf16[3584,256]{1,0:T(8,128)(2,1)S(1)}, bf16[3584,256]{1,0:T(8,128)(2,1)S(1)}, bf16[3584,256]{1,0:T(8,128)(2,1)S(1)}, bf16[3584,256]{1,0:T(8,12...) custom-call(bf16[16,3712]{1,0:T(8,128)(2,1)S(1)} %shard_map.111.rows_ref.one_ref, ...), custom_call_target="tpu_custom_call" | custom-call | tf_op jit(solution)/shard_map/pallas_call | solution.py:138
  16.7 0.1 collective-permute-start.3
  16.8 1.5 %shard_map.114.refs_4_ = bf16[3584,256]{1,0:T(8,128)(2,1)S(1)} custom-call(bf16[32,3712]{1,0:T(8,128)(2,1)S(1)} %shard_map.113.rows_ref.one_ref, bf16[8,3584,256]{2,1,0:T(8,128)(2,1)} %gate_hbm.1), custom_call_target="tpu_custom_call" | custom-call | tf_op jit(solution)/shard_map/pallas_call | solution.py:138
  18.4 0.4 shard_map.117.refs_0_
  18.8 1.6 %collective-permute-start.4 = (bf16[64,512]{1,0:T(8,128)(2,1)S(1)}, bf16[64,512]{1,0:T(8,128)(2,1)S(1)}, u32[]{:S(2)}, u32[]{:S(2)}) collective-permute-start(bf16[64,512]{1,0:T(8,128)(2,1)S(1)} %shard_map.117.refs_0_), channel_id=1, source_target_pairs={{0,4},{4,0},{8,12},{12,8},{1,5},{5,1},{9,13},{13,9},{2,6},{6,2},{1... | collective-permute-start | bytes 196616 | tf_op jit(solution)/shard_map/ppermute | solution.py:176
  20.5 3.1 %collective-permute-start.5 = (bf16[64,512]{1,0:T(8,128)(2,1)S(1)}, bf16[64,512]{1,0:T(8,128)(2,1)S(1)}, u32[]{:S(2)}, u32[]{:S(2)}) collective-permute-start(bf16[64,512]{1,0:T(8,128)(2,1)S(1)} %shard_map.117.refs_0_), channel_id=1, source_target_pairs={{0,8},{4,12},{8,0},{12,4},{1,9},{5,13},{9,1},{13,5},{2,10},{6,14},... | collective-permute-start | bytes 196616 | tf_op jit(solution)/shard_map/ppermute | solution.py:176
  23.7 8.1 %shard_map.116.routed_ref = f32[64,3584]{1,0:T(8,128)S(1)} custom-call(s32[1]{0:T(128)} %bitcast.node_ref, bf16[64,3712]{1,0:T(8,128)(2,1)S(1)} %shard_map.115.x_ref, bf16[8,3584,256]{2,1,0:T(8,128)(2,1)} %gate_hbm.1, bf16[8,3584,256]{2,1,0:T(8,128)(2,1)S(1)} %bitcast.2, bf16[8,256,3584]{2,1,0:T(8,128)(2,1)S(1)} %bitcast.4, ...), custom_call_target="tpu_custom_call" | custom-call | tf_op jit(solution)/shard_map/pallas_call | solution.py:256
  31.8 0.4 shard_map.118
  32.2 0.1 collective-permute-start.7
  32.3 1.5 %collective-permute-done.7 = bf16[32,3584]{1,0:T(8,128)(2,1)S(1)} collective-permute-done((bf16[32,3584]{1,0:T(8,128)(2,1)S(1)}, bf16[32,3584]{1,0:T(8,128)(2,1)S(1)}, u32[]{:S(2)}, u32[]{:S(2)}) %collective-permute-start.7) | collective-permute-done | bytes 229408 | tf_op jit(solution)/shard_map/ppermute | solution.py:176
  33.8 0.1 add_convert_fusion
  33.9 1.5 %collective-permute-start.8 = (bf16[16,3584]{1,0:T(8,128)(2,1)S(1)}, bf16[16,3584]{1,0:T(8,128)(2,1)S(1)}, u32[]{:S(2)}, u32[]{:S(2)}) collective-permute-start(bf16[16,3584]{1,0:T(8,128)(2,1)S(1)} %slice.35), channel_id=1, source_target_pairs={{0,2},{1,3},{2,0},{3,1},{4,6},{5,7},{6,4},{7,5},{8,10},{9,11},{10,... | collective-permute-start | bytes 344072 | tf_op jit(solution)/shard_map/ppermute | solution.py:176
  35.4 3.7 %collective-permute-done.8 = bf16[16,3584]{1,0:T(8,128)(2,1)S(1)} collective-permute-done((bf16[16,3584]{1,0:T(8,128)(2,1)S(1)}, bf16[16,3584]{1,0:T(8,128)(2,1)S(1)}, u32[]{:S(2)}, u32[]{:S(2)}) %collective-permute-start.8) | collective-permute-done | bytes 114720 | tf_op jit(solution)/shard_map/ppermute | solution.py:176
  39.2 1.6 %collective-permute-start.9 = (bf16[8,3584]{1,0:T(8,128)(2,1)S(1)}, bf16[8,3584]{1,0:T(8,128)(2,1)S(1)}, u32[]{:S(2)}, u32[]{:S(2)}) collective-permute-start(bf16[8,3584]{1,0:T(8,128)(2,1)S(1)} %slice.37), channel_id=1, source_target_pairs={{0,8},{4,12},{8,0},{12,4},{1,9},{5,13},{9,1},{13,5},{2,10},{6,14},... | collective-permute-start | bytes 172040 | tf_op jit(solution)/shard_map/ppermute | solution.py:176
  40.7 3.7 %collective-permute-done.9 = bf16[8,3584]{1,0:T(8,128)(2,1)S(1)} collective-permute-done((bf16[8,3584]{1,0:T(8,128)(2,1)S(1)}, bf16[8,3584]{1,0:T(8,128)(2,1)S(1)}, u32[]{:S(2)}, u32[]{:S(2)}) %collective-permute-start.9) | collective-permute-done | bytes 57376 | tf_op jit(solution)/shard_map/ppermute | solution.py:176
  44.5 1.4 %collective-permute-start.10 = (bf16[4,3584]{1,0:T(4,128)(2,1)S(1)}, bf16[4,3584]{1,0:T(4,128)(2,1)S(1)}, u32[]{:S(2)}, u32[]{:S(2)}) collective-permute-start(bf16[4,3584]{1,0:T(4,128)(2,1)S(1)} %slice.39), channel_id=1, source_target_pairs={{0,4},{4,0},{8,12},{12,8},{1,5},{5,1},{9,13},{13,9},{2,6},{6,2},{1... | collective-permute-start | bytes 86024 | tf_op jit(solution)/shard_map/ppermute | solution.py:176
  45.9 2.5 %collective-permute-done.10 = bf16[4,3584]{1,0:T(4,128)(2,1)S(1)} collective-permute-done((bf16[4,3584]{1,0:T(4,128)(2,1)S(1)}, bf16[4,3584]{1,0:T(4,128)(2,1)S(1)}, u32[]{:S(2)}, u32[]{:S(2)}) %collective-permute-start.10) | collective-permute-done | bytes 28704 | tf_op jit(solution)/shard_map/ppermute | solution.py:176
  48.4 0.6 %add_convert_fusion.3 = bf16[4,3584]{1,0:T(4,128)(2,1)} fusion(bf16[4,3584]{1,0:T(4,128)(2,1)S(1)} %collective-permute-done.10, bf16[8,3584]{1,0:T(8,128)(2,1)S(1)} %add_convert_fusion.2), kind=kLoop, calls=%fused_computation.3 | loop fusion | flops 57344 | bytes 86016 | tf_op jit(solution)/shard_map/convert_element_type | solution.py:180
  (36 shorter events, 0.2 us)
Async XLA Ops:
  0.0 23.6 %slice-start = ((s8[14680064]{0:T(1024)(128)(4,1)}), s8[4194304]{0:T(1024)(128)(4,1)S(1)}, s32[]{:S(2)}) async-start(s8[14680064]{0:T(1024)(128)(4,1)} %bitcast.1), calls=%async_computation | async-start | bytes 8388608
  0.0 23.6 %slice-start.1 = ((s8[14680064]{0:T(1024)(128)(4,1)}), s8[4194304]{0:T(1024)(128)(4,1)S(1)}, s32[]{:S(2)}) async-start(s8[14680064]{0:T(1024)(128)(4,1)} %bitcast.1), calls=%async_computation.1 | async-start | bytes 8388608
  0.0 23.6 %slice-start.2 = ((s8[14680064]{0:T(1024)(128)(4,1)}), s8[4194304]{0:T(1024)(128)(4,1)S(1)}, s32[]{:S(2)}) async-start(s8[14680064]{0:T(1024)(128)(4,1)} %bitcast.1), calls=%async_computation.2 | async-start | bytes 8388608
  0.0 23.6 %slice-start.4 = ((s8[14680064]{0:T(1024)(128)(4,1)}), s8[4194304]{0:T(1024)(128)(4,1)S(1)}, s32[]{:S(2)}) async-start(s8[14680064]{0:T(1024)(128)(4,1)} %bitcast.3), calls=%async_computation.4 | async-start | bytes 8388608
  0.0 23.6 %slice-start.5 = ((s8[14680064]{0:T(1024)(128)(4,1)}), s8[4194304]{0:T(1024)(128)(4,1)S(1)}, s32[]{:S(2)}) async-start(s8[14680064]{0:T(1024)(128)(4,1)} %bitcast.3), calls=%async_computation.5 | async-start | bytes 8388608
  0.0 23.6 %slice-start.6 = ((s8[14680064]{0:T(1024)(128)(4,1)}), s8[4194304]{0:T(1024)(128)(4,1)S(1)}, s32[]{:S(2)}) async-start(s8[14680064]{0:T(1024)(128)(4,1)} %bitcast.3), calls=%async_computation.6 | async-start | bytes 8388608
  1.1 5.0 %collective-permute-start = (bf16[4,3712]{1,0:T(4,128)(2,1)S(1)}, bf16[4,3712]{1,0:T(4,128)(2,1)S(1)}, u32[]{:S(2)}, u32[]{:S(2)}) collective-permute-start(bf16[4,3712]{1,0:T(4,128)(2,1)S(1)} %shard_map.109.one_ref), channel_id=1, source_target_pairs={{0,4},{4,0},{8,12},{12,8},{1,5},{5,1},{9,13},{13,9},{2,6},{6,2},{1... | collective-permute-start | bytes 89096 | tf_op jit(solution)/shard_map/ppermute | solution.py:176
  6.1 5.3 %collective-permute-start.1 = (bf16[8,3712]{1,0:T(8,128)(2,1)S(1)}, bf16[8,3712]{1,0:T(8,128)(2,1)S(1)}, u32[]{:S(2)}, u32[]{:S(2)}) collective-permute-start(bf16[8,3712]{1,0:T(8,128)(2,1)S(1)} %shard_map.110.one_ref), channel_id=1, source_target_pairs={{0,8},{4,12},{8,0},{12,4},{1,9},{5,13},{9,1},{13,5},{2,10},{6,14},... | collective-permute-start | bytes 178184 | tf_op jit(solution)/shard_map/ppermute | solution.py:176
  11.4 12.2 %slice-start.3 = ((s8[14680064]{0:T(1024)(128)(4,1)}), s8[2097152]{0:T(1024)(128)(4,1)S(1)}, s32[]{:S(2)}) async-start(s8[14680064]{0:T(1024)(128)(4,1)} %bitcast.1), calls=%async_computation.3 | async-start | bytes 4194304
  11.4 12.2 %slice-start.7 = ((s8[14680064]{0:T(1024)(128)(4,1)}), s8[2097152]{0:T(1024)(128)(4,1)S(1)}, s32[]{:S(2)}) async-start(s8[14680064]{0:T(1024)(128)(4,1)} %bitcast.3), calls=%async_computation.7 | async-start | bytes 4194304
  11.5 5.3 %collective-permute-start.2 = (bf16[16,3712]{1,0:T(8,128)(2,1)S(1)}, bf16[16,3712]{1,0:T(8,128)(2,1)S(1)}, u32[]{:S(2)}, u32[]{:S(2)}) collective-permute-start(bf16[16,3712]{1,0:T(8,128)(2,1)S(1)} %shard_map.111.rows_ref.one_ref), channel_id=1, source_target_pairs={{0,2},{1,3},{2,0},{3,1},{4,6},{5,7},{6,4},{7,5},{8,10},{9,11},{10,... | collective-permute-start | bytes 356360 | tf_op jit(solution)/shard_map/ppermute | solution.py:176
  16.7 1.6 %collective-permute-start.3 = (bf16[32,3712]{1,0:T(8,128)(2,1)S(1)}, bf16[32,3712]{1,0:T(8,128)(2,1)S(1)}, u32[]{:S(2)}, u32[]{:S(2)}) collective-permute-start(bf16[32,3712]{1,0:T(8,128)(2,1)S(1)} %shard_map.113.rows_ref.one_ref), channel_id=1, source_target_pairs={{0,1},{1,0},{2,3},{3,2},{4,5},{5,4},{6,7},{7,6},{8,9},{9,8},{10,11... | collective-permute-start | bytes 712712 | tf_op jit(solution)/shard_map/ppermute | solution.py:176
  18.8 13.0 %copy-start = (bf16[256,896]{1,0:T(8,128)(2,1)S(1)}, bf16[256,896]{1,0:T(8,128)(2,1)}, u32[]{:S(2)}) copy-start(bf16[256,896]{1,0:T(8,128)(2,1)} %down_ref.3) | copy-start | bytes 1376260
  18.8 13.0 %collective-permute-start.4 = (bf16[64,512]{1,0:T(8,128)(2,1)S(1)}, bf16[64,512]{1,0:T(8,128)(2,1)S(1)}, u32[]{:S(2)}, u32[]{:S(2)}) collective-permute-start(bf16[64,512]{1,0:T(8,128)(2,1)S(1)} %shard_map.117.refs_0_), channel_id=1, source_target_pairs={{0,4},{4,0},{8,12},{12,8},{1,5},{5,1},{9,13},{13,9},{2,6},{6,2},{1... | collective-permute-start | bytes 196616 | tf_op jit(solution)/shard_map/ppermute | solution.py:176
  20.5 11.3 %collective-permute-start.5 = (bf16[64,512]{1,0:T(8,128)(2,1)S(1)}, bf16[64,512]{1,0:T(8,128)(2,1)S(1)}, u32[]{:S(2)}, u32[]{:S(2)}) collective-permute-start(bf16[64,512]{1,0:T(8,128)(2,1)S(1)} %shard_map.117.refs_0_), channel_id=1, source_target_pairs={{0,8},{4,12},{8,0},{12,4},{1,9},{5,13},{9,1},{13,5},{2,10},{6,14},... | collective-permute-start | bytes 196616 | tf_op jit(solution)/shard_map/ppermute | solution.py:176
  23.6 8.2 %collective-permute-start.6 = (bf16[64,512]{1,0:T(8,128)(2,1)S(1)}, bf16[64,512]{1,0:T(8,128)(2,1)S(1)}, u32[]{:S(2)}, u32[]{:S(2)}) collective-permute-start(bf16[64,512]{1,0:T(8,128)(2,1)S(1)} %shard_map.117.refs_0_), channel_id=1, source_target_pairs={{0,12},{4,8},{8,4},{12,0},{1,13},{5,9},{9,5},{13,1},{2,14},{6,10},... | collective-permute-start | bytes 196616 | tf_op jit(solution)/shard_map/ppermute | solution.py:176
  32.2 1.6 %collective-permute-start.7 = (bf16[32,3584]{1,0:T(8,128)(2,1)S(1)}, bf16[32,3584]{1,0:T(8,128)(2,1)S(1)}, u32[]{:S(2)}, u32[]{:S(2)}) collective-permute-start(bf16[32,3584]{1,0:T(8,128)(2,1)S(1)} %slice.33), channel_id=1, source_target_pairs={{0,1},{1,0},{2,3},{3,2},{4,5},{5,4},{6,7},{7,6},{8,9},{9,8},{10,11... | collective-permute-start | bytes 688136 | tf_op jit(solution)/shard_map/ppermute | solution.py:176
  33.9 5.3 %collective-permute-start.8 = (bf16[16,3584]{1,0:T(8,128)(2,1)S(1)}, bf16[16,3584]{1,0:T(8,128)(2,1)S(1)}, u32[]{:S(2)}, u32[]{:S(2)}) collective-permute-start(bf16[16,3584]{1,0:T(8,128)(2,1)S(1)} %slice.35), channel_id=1, source_target_pairs={{0,2},{1,3},{2,0},{3,1},{4,6},{5,7},{6,4},{7,5},{8,10},{9,11},{10,... | collective-permute-start | bytes 344072 | tf_op jit(solution)/shard_map/ppermute | solution.py:176
  39.2 5.3 %collective-permute-start.9 = (bf16[8,3584]{1,0:T(8,128)(2,1)S(1)}, bf16[8,3584]{1,0:T(8,128)(2,1)S(1)}, u32[]{:S(2)}, u32[]{:S(2)}) collective-permute-start(bf16[8,3584]{1,0:T(8,128)(2,1)S(1)} %slice.37), channel_id=1, source_target_pairs={{0,8},{4,12},{8,0},{12,4},{1,9},{5,13},{9,1},{13,5},{2,10},{6,14},... | collective-permute-start | bytes 172040 | tf_op jit(solution)/shard_map/ppermute | solution.py:176
  44.5 3.9 %collective-permute-start.10 = (bf16[4,3584]{1,0:T(4,128)(2,1)S(1)}, bf16[4,3584]{1,0:T(4,128)(2,1)S(1)}, u32[]{:S(2)}, u32[]{:S(2)}) collective-permute-start(bf16[4,3584]{1,0:T(4,128)(2,1)S(1)} %slice.39), channel_id=1, source_target_pairs={{0,4},{4,0},{8,12},{12,8},{1,5},{5,1},{9,13},{13,9},{2,6},{6,2},{1... | collective-permute-start | bytes 86024 | tf_op jit(solution)/shard_map/ppermute | solution.py:176

commit v6 on v5

--- a/solution.py
+++ b/solution.py
@@ -11,7 +11,8 @@
 NODE_GROUPS = 8
 LANES = 128
 MIB = 2**20
-NEAR_PLAN = (0, 0, 4, 1)
+NEAR_PLAN = (0, 4, 1)
+DIRECT = 4
 WORTH = 40 * 10**9
 
 
@@ -100,7 +101,7 @@
             gate, up = later
 
 
-def shared_out_kernel(tokens, node_ref, routed_ref, down_ref, *refs):
+def shared_out_kernel(unit, node_ref, routed_ref, down_ref, *refs):
     parts, out_ref = refs[:-1], refs[-1]
     block, slab = down_ref.shape
     count, width = out_ref.shape
@@ -108,7 +109,7 @@
     to = lax.broadcasted_iota(jnp.int32, (count, count), 0)
     come = lax.broadcasted_iota(jnp.int32, (count, count), 1)
     for k in range(1, len(parts)):
-        place = (come == (to ^ (k * tokens))).astype(jnp.bfloat16)
+        place = (come == (to ^ (k * unit))).astype(jnp.bfloat16)
         total += jnp.dot(place, parts[k][...], preferred_element_type=jnp.float32)
     hidden = (jax.nn.silu(total[:, :block]) * total[:, block:]).astype(jnp.bfloat16)
     shared = jnp.dot(hidden, down_ref[...], preferred_element_type=jnp.float32)
@@ -147,20 +148,23 @@
     )(rows, *(far(w) for w, _ in wanted))
 
 
-def join_kernel(one_ref, other_ref, out_ref):
-    both = [ref[...].astype(jnp.float32) for ref in (one_ref, other_ref)]
-    out_ref[...] = jnp.concatenate(both, axis=0).astype(jnp.bfloat16)
-
-
-def join(one, other):
+def join_kernel(*refs):
+    rows = [ref[...].astype(jnp.float32) for ref in refs[:-1]]
+    refs[-1][...] = jnp.concatenate(rows, axis=0).astype(jnp.bfloat16)
+
+
+def join(*pieces):
     vmem = pl.BlockSpec(memory_space=pltpu.VMEM)
+    count, width = pieces[0].shape
     return pl.pallas_call(
         join_kernel,
-        out_shape=jax.ShapeDtypeStruct((2 * one.shape[0], one.shape[1]), one.dtype),
-        in_specs=[vmem, vmem],
+        out_shape=jax.ShapeDtypeStruct((len(pieces) * count, width), pieces[0].dtype),
+        in_specs=[vmem] * len(pieces),
         out_specs=vmem,
-        compiler_params=pltpu.CompilerParams(vmem_limit_bytes=24 * one.size + MIB),
-    )(one, other)
+        compiler_params=pltpu.CompilerParams(
+            vmem_limit_bytes=12 * len(pieces) * count * width + MIB
+        ),
+    )(*pieces)
 
 
 def near(value):
@@ -174,10 +178,6 @@
 def exchange(value, axis, bit):
     size = lax.axis_size(axis)
     return lax.ppermute(value, axis, [(i, i ^ bit) for i in range(size)])
-
-
-def add_rows(one, other):
-    return (one.astype(jnp.float32) + other.astype(jnp.float32)).astype(jnp.bfloat16)
 
 
 def local(
@@ -224,21 +224,26 @@
     )(place, *(far(a) for a in small))
 
     weights = [(expert_gate, e) for e in range(held)]
-    stages = [("node", 1 << i) for i in range(node_count.bit_length() - 1)]
-    stages += [("local", 1 << i) for i in reversed(range(local_count.bit_length() - 1))]
+    halves = [("local", (1 << i,)) for i in reversed(range(local_count.bit_length() - 1))]
+    if node_count <= DIRECT:
+        stages = halves[:-1] + [("node", tuple(range(1, node_count)))] + halves[-1:]
+    else:
+        doubling = [("node", (1 << i,)) for i in range(node_count.bit_length() - 1)]
+        stages = halves[:-1] + doubling + halves[-1:]
+    node_unit = token_count << max(len(halves) - 1, 0)
     ready = []
-    for stage, (axis, bit) in enumerate(stages):
-        other = exchange(rows, axis, bit)
+    for stage, (axis, bits) in enumerate(stages):
+        others = [exchange(rows, axis, bit) for bit in bits]
         take = NEAR_PLAN[stage] if stage < len(NEAR_PLAN) else 0
         wanted = weights[len(ready) : len(ready) + take]
         extra = [(shared_gate, None), (shared_up, None)] if stage == len(stages) - 2 else []
         if wanted or extra:
             got = bring(wanted + extra, rows)
-            other, *got = lax.optimization_barrier((other, *got))
+            others, got = lax.optimization_barrier((others, got))
             ready += got[: len(wanted)]
             if extra:
                 shared_gate, shared_up = got[len(wanted) :]
-        rows = join(rows, other)
+        rows = join(rows, *others)
     row_count = rows.shape[0]
 
     aligned = slab % LANES == 0
@@ -277,23 +282,20 @@
             jnp.zeros((shared_block, feature_count), shared_down.dtype), shared_down, node * slab, axis=1
         )
     out = pl.pallas_call(
-        functools.partial(shared_out_kernel, token_count),
+        functools.partial(shared_out_kernel, node_unit),
         out_shape=jax.ShapeDtypeStruct((row_count, feature_count), jnp.bfloat16),
         in_specs=[smem] + [vmem] * (2 + node_count),
         out_specs=vmem,
         compiler_params=params,
     )(place, routed, shared_down, *parts)
 
-    bit = 1
-    while bit < local_count:
-        half = out.shape[0] // 2
-        out = add_rows(out[:half], exchange(out[half:], "local", bit))
-        bit *= 2
-    bit = node_count // 2
-    while bit:
-        half = out.shape[0] // 2
-        out = add_rows(out[:half], exchange(out[half:], "node", bit))
-        bit //= 2
+    for axis, bits in reversed(stages):
+        unit = out.shape[0] // (len(bits) + 1)
+        total = out[:unit].astype(jnp.float32)
+        for i in reversed(range(len(bits))):
+            piece = out[unit * (i + 1) : unit * (i + 2)]
+            total = total + exchange(piece, axis, bits[i]).astype(jnp.float32)
+        out = total.astype(jnp.bfloat16)
     return out
 
 

time: 49.2 us -> 46.3 us (0.941)
  waiting for transfers between devices: 15.5 us -> 11.7 us
  starting transfers between devices: 17.5 us -> 18.4 us
    ppermute x11 -> x13, waiting for transfers between devices: 15.5 us -> 11.7 us  [exchange(): return lax.ppermute(value, axis, [(i, i ^ bit) for i in range(size)])]
    ppermute x11 -> x13, starting transfers between devices: 17.5 us -> 18.4 us  [exchange(): return lax.ppermute(value, axis, [(i, i ^ bit) for i in range(size)])]
  transfers between devices with their start and end apart: 11 -> 13, of which waited for: 6 -> 7; matrix products, arithmetic and copies ran while one was open for 0% -> 0% of each run, Pallas kernels for 27% -> 28%
where the time goes in v6:
time: 46.3 us; the launch traced here: 46.1 us
  starting transfers between devices  18.4 us (40%)
  Pallas kernels  14.9 us (32%)
  waiting for transfers between devices  11.7 us (25%)
  other arithmetic  0.72 us (2%)
    ppermute x13, starting transfers between devices, exchange(): return lax.ppermute(value, axis, [(i, i ^ bit) for i in range(size)])  18.4 us
    ppermute x13, waiting for transfers between devices, exchange(): return lax.ppermute(value, axis, [(i, i ^ bit) for i in range(size)])  11.7 us
    pallas_call x1, Pallas kernels, local(): pl.pallas_call(functools.partial(routed_kernel, len(ready)), out_shape=ja...  8.12 us
    pallas_call x2, Pallas kernels, bring(): pl.pallas_call(functools.partial(bring_kernel, [e for _, e in wanted]), o...  4.88 us
    pallas_call x1, Pallas kernels, local(): pl.pallas_call(functools.partial(pack_kernel, per_group), out_shape=jax.S...  1.11 us
  transfers between devices with their start and end apart: 13, of which 7 were waited for; matrix products, arithmetic and copies ran while one was open for 0% of the time, Pallas kernels for 28%

profile of v6, /device:TPU:0, one launch (start us, length us, event | category | flops | bytes accessed | tf_op | source)
XLA Modules:
  0.0 46.1 jit_solution(11211126711845721891)
XLA Ops:
  0.0 1.1 %shard_map.109.refs_0_ = bf16[4,3712]{1,0:T(4,128)(2,1)S(1)} custom-call(s32[1]{0:T(128)} %bitcast.node_ref, bf16[4,3584]{1,0:T(4,128)(2,1)} %refs_0_.3, f32[3584]{0:T(1024)} %refs_1_.2, s32[4,4]{1,0:T(4,128)} %refs_2_.2, s32[4,8]{1,0:T(4,128)} %refs_3_.2, bf16[4,8]{1,0:T(4,128)(2,1)} %refs_4_.2), custom_call_target="tpu_custom_call" | custom-call | flops 40000000000 | tf_op jit(solution)/shard_map/pallas_call | solution.py:215
  1.1 3.0 %collective-permute-start = (bf16[4,3712]{1,0:T(4,128)(2,1)S(1)}, bf16[4,3712]{1,0:T(4,128)(2,1)S(1)}, u32[]{:S(2)}, u32[]{:S(2)}) collective-permute-start(bf16[4,3712]{1,0:T(4,128)(2,1)S(1)} %shard_map.109.refs_0_), channel_id=1, source_target_pairs={{0,2},{1,3},{2,0},{3,1},{4,6},{5,7},{6,4},{7,5},{8,10},{9,11},{10,... | collective-permute-start | bytes 89096 | tf_op jit(solution)/shard_map/ppermute | solution.py:180
  4.2 1.9 %collective-permute-done.refs_1_ = bf16[4,3712]{1,0:T(4,128)(2,1)S(1)} collective-permute-done((bf16[4,3712]{1,0:T(4,128)(2,1)S(1)}, bf16[4,3712]{1,0:T(4,128)(2,1)S(1)}, u32[]{:S(2)}, u32[]{:S(2)}) %collective-permute-start) | collective-permute-done | bytes 29728 | tf_op jit(solution)/shard_map/ppermute | solution.py:180
  6.1 2.2 %collective-permute-start.1 = (bf16[8,3712]{1,0:T(8,128)(2,1)S(1)}, bf16[8,3712]{1,0:T(8,128)(2,1)S(1)}, u32[]{:S(2)}, u32[]{:S(2)}) collective-permute-start(bf16[8,3712]{1,0:T(8,128)(2,1)S(1)} %shard_map.110.rows_ref.refs_0_), channel_id=1, source_target_pairs={{0,4},{4,0},{8,12},{12,8},{1,5},{5,1},{9,13},{13,9},{2,6},{6,2},{1... | collective-permute-start | bytes 178184 | tf_op jit(solution)/shard_map/ppermute | solution.py:180
  8.2 2.6 %collective-permute-start.2 = (bf16[8,3712]{1,0:T(8,128)(2,1)S(1)}, bf16[8,3712]{1,0:T(8,128)(2,1)S(1)}, u32[]{:S(2)}, u32[]{:S(2)}) collective-permute-start(bf16[8,3712]{1,0:T(8,128)(2,1)S(1)} %shard_map.110.rows_ref.refs_0_), channel_id=1, source_target_pairs={{0,8},{4,12},{8,0},{12,4},{1,9},{5,13},{9,1},{13,5},{2,10},{6,14},... | collective-permute-start | bytes 178184 | tf_op jit(solution)/shard_map/ppermute | solution.py:180
  10.8 3.4 %shard_map.111 = (bf16[3584,256]{1,0:T(8,128)(2,1)S(1)}, bf16[3584,256]{1,0:T(8,128)(2,1)S(1)}, bf16[3584,256]{1,0:T(8,128)(2,1)S(1)}, bf16[3584,256]{1,0:T(8,12...) custom-call(bf16[8,3712]{1,0:T(8,128)(2,1)S(1)} %shard_map.110.rows_ref.refs_0_, ...), custom_call_target="tpu_custom_call" | custom-call | tf_op jit(solution)/shard_map/pallas_call | solution.py:139
  14.2 0.4 collective-permute-done.2.refs_2_
  14.6 2.2 %collective-permute-done.3.refs_3_ = bf16[8,3712]{1,0:T(8,128)(2,1)S(1)} collective-permute-done((bf16[8,3712]{1,0:T(8,128)(2,1)S(1)}, bf16[8,3712]{1,0:T(8,128)(2,1)S(1)}, u32[]{:S(2)}, u32[]{:S(2)}) %collective-permute-start.3) | collective-permute-done | bytes 59424 | tf_op jit(solution)/shard_map/ppermute | solution.py:180
  16.9 0.1 collective-permute-start.4
  16.9 1.5 %shard_map.113.refs_4_ = bf16[3584,256]{1,0:T(8,128)(2,1)S(1)} custom-call(bf16[32,3712]{1,0:T(8,128)(2,1)S(1)} %shard_map.112.rows_ref.refs_0_, bf16[8,3584,256]{2,1,0:T(8,128)(2,1)} %gate_hbm.1), custom_call_target="tpu_custom_call" | custom-call | tf_op jit(solution)/shard_map/pallas_call | solution.py:139
  18.5 0.4 shard_map.116.refs_0_
  19.0 1.8 %collective-permute-start.6 = (bf16[64,512]{1,0:T(8,128)(2,1)S(1)}, bf16[64,512]{1,0:T(8,128)(2,1)S(1)}, u32[]{:S(2)}, u32[]{:S(2)}) collective-permute-start(bf16[64,512]{1,0:T(8,128)(2,1)S(1)} %shard_map.116.refs_0_), channel_id=1, source_target_pairs={{0,8},{4,12},{8,0},{12,4},{1,9},{5,13},{9,1},{13,5},{2,10},{6,14},... | collective-permute-start | bytes 196616 | tf_op jit(solution)/shard_map/ppermute | solution.py:180
  20.8 2.6 %collective-permute-start.7 = (bf16[64,512]{1,0:T(8,128)(2,1)S(1)}, bf16[64,512]{1,0:T(8,128)(2,1)S(1)}, u32[]{:S(2)}, u32[]{:S(2)}) collective-permute-start(bf16[64,512]{1,0:T(8,128)(2,1)S(1)} %shard_map.116.refs_0_), channel_id=1, source_target_pairs={{0,12},{4,8},{8,4},{12,0},{1,13},{5,9},{9,5},{13,1},{2,14},{6,10},... | collective-permute-start | bytes 196616 | tf_op jit(solution)/shard_map/ppermute | solution.py:180
  23.4 8.1 %shard_map.115.routed_ref = f32[64,3584]{1,0:T(8,128)S(1)} custom-call(s32[1]{0:T(128)} %bitcast.node_ref, bf16[64,3712]{1,0:T(8,128)(2,1)S(1)} %shard_map.114.x_ref, bf16[8,3584,256]{2,1,0:T(8,128)(2,1)} %gate_hbm.1, bf16[8,3584,256]{2,1,0:T(8,128)(2,1)S(1)} %bitcast.2, bf16[8,256,3584]{2,1,0:T(8,128)(2,1)S(1)} %bitcast.4, ...), custom_call_target="tpu_custom_call" | custom-call | tf_op jit(solution)/shard_map/pallas_call | solution.py:261
  31.6 0.4 shard_map.117
  32.0 0.1 collective-permute-start.8
  32.1 1.5 %collective-permute-done.8 = bf16[32,3584]{1,0:T(8,128)(2,1)S(1)} collective-permute-done((bf16[32,3584]{1,0:T(8,128)(2,1)S(1)}, bf16[32,3584]{1,0:T(8,128)(2,1)S(1)}, u32[]{:S(2)}, u32[]{:S(2)}) %collective-permute-start.8) | collective-permute-done | bytes 229408 | tf_op jit(solution)/shard_map/ppermute | solution.py:180
  33.7 1.8 %collective-permute-start.11 = (bf16[8,3584]{1,0:T(8,128)(2,1)S(1)}, bf16[8,3584]{1,0:T(8,128)(2,1)S(1)}, u32[]{:S(2)}, u32[]{:S(2)}) collective-permute-start(bf16[8,3584]{1,0:T(8,128)(2,1)S(1)} %get-tuple-element.40), channel_id=1, source_target_pairs={{0,4},{4,0},{8,12},{12,8},{1,5},{5,1},{9,13},{13,9},{2,6},{6,2},{1... | collective-permute-start | bytes 172040 | tf_op jit(solution)/shard_map/ppermute | solution.py:180
  35.5 2.6 %collective-permute-start.9 = (bf16[8,3584]{1,0:T(8,128)(2,1)S(1)}, bf16[8,3584]{1,0:T(8,128)(2,1)S(1)}, u32[]{:S(2)}, u32[]{:S(2)}) collective-permute-start(bf16[8,3584]{1,0:T(8,128)(2,1)S(1)} %get-tuple-element.39), channel_id=1, source_target_pairs={{0,12},{4,8},{8,4},{12,0},{1,13},{5,9},{9,5},{13,1},{2,14},{6,10},... | collective-permute-start | bytes 172040 | tf_op jit(solution)/shard_map/ppermute | solution.py:180
  38.1 1.2 %collective-permute-done.10 = bf16[8,3584]{1,0:T(8,128)(2,1)S(1)} collective-permute-done((bf16[8,3584]{1,0:T(8,128)(2,1)S(1)}, bf16[8,3584]{1,0:T(8,128)(2,1)S(1)}, u32[]{:S(2)}, u32[]{:S(2)}) %collective-permute-start.10) | collective-permute-done | bytes 57376 | tf_op jit(solution)/shard_map/ppermute | solution.py:180
  39.3 2.2 %collective-permute-done.9 = bf16[8,3584]{1,0:T(8,128)(2,1)S(1)} collective-permute-done((bf16[8,3584]{1,0:T(8,128)(2,1)S(1)}, bf16[8,3584]{1,0:T(8,128)(2,1)S(1)}, u32[]{:S(2)}, u32[]{:S(2)}) %collective-permute-start.9) | collective-permute-done | bytes 57376 | tf_op jit(solution)/shard_map/ppermute | solution.py:180
  41.5 1.6 %collective-permute-start.12 = (bf16[4,3584]{1,0:T(4,128)(2,1)S(1)}, bf16[4,3584]{1,0:T(4,128)(2,1)S(1)}, u32[]{:S(2)}, u32[]{:S(2)}) collective-permute-start(bf16[4,3584]{1,0:T(4,128)(2,1)S(1)} %slice.39), channel_id=1, source_target_pairs={{0,2},{1,3},{2,0},{3,1},{4,6},{5,7},{6,4},{7,5},{8,10},{9,11},{10,... | collective-permute-start | bytes 86024 | tf_op jit(solution)/shard_map/ppermute | solution.py:180
  43.1 2.4 %collective-permute-done.12 = bf16[4,3584]{1,0:T(4,128)(2,1)S(1)} collective-permute-done((bf16[4,3584]{1,0:T(4,128)(2,1)S(1)}, bf16[4,3584]{1,0:T(4,128)(2,1)S(1)}, u32[]{:S(2)}, u32[]{:S(2)}) %collective-permute-start.12) | collective-permute-done | bytes 28704 | tf_op jit(solution)/shard_map/ppermute | solution.py:180
  45.5 0.6 %add_convert_fusion.2 = bf16[4,3584]{1,0:T(4,128)(2,1)} fusion(bf16[4,3584]{1,0:T(4,128)(2,1)S(1)} %collective-permute-done.12, bf16[8,3584]{1,0:T(8,128)(2,1)S(1)} %add_convert_fusion.1), kind=kLoop, calls=%fused_computation.2 | loop fusion | flops 57344 | bytes 86016 | tf_op jit(solution)/shard_map/convert_element_type | solution.py:298
  (37 shorter events, 0.4 us)
Async XLA Ops:
  0.0 23.4 %slice-start = ((s8[14680064]{0:T(1024)(128)(4,1)}), s8[4194304]{0:T(1024)(128)(4,1)S(1)}, s32[]{:S(2)}) async-start(s8[14680064]{0:T(1024)(128)(4,1)} %bitcast.1), calls=%async_computation | async-start | bytes 8388608
  0.0 23.4 %slice-start.1 = ((s8[14680064]{0:T(1024)(128)(4,1)}), s8[4194304]{0:T(1024)(128)(4,1)S(1)}, s32[]{:S(2)}) async-start(s8[14680064]{0:T(1024)(128)(4,1)} %bitcast.1), calls=%async_computation.1 | async-start | bytes 8388608
  0.0 23.4 %slice-start.2 = ((s8[14680064]{0:T(1024)(128)(4,1)}), s8[4194304]{0:T(1024)(128)(4,1)S(1)}, s32[]{:S(2)}) async-start(s8[14680064]{0:T(1024)(128)(4,1)} %bitcast.1), calls=%async_computation.2 | async-start | bytes 8388608
  0.0 23.4 %slice-start.4 = ((s8[14680064]{0:T(1024)(128)(4,1)}), s8[4194304]{0:T(1024)(128)(4,1)S(1)}, s32[]{:S(2)}) async-start(s8[14680064]{0:T(1024)(128)(4,1)} %bitcast.3), calls=%async_computation.4 | async-start | bytes 8388608
  0.0 23.4 %slice-start.5 = ((s8[14680064]{0:T(1024)(128)(4,1)}), s8[4194304]{0:T(1024)(128)(4,1)S(1)}, s32[]{:S(2)}) async-start(s8[14680064]{0:T(1024)(128)(4,1)} %bitcast.3), calls=%async_computation.5 | async-start | bytes 8388608
  0.0 23.4 %slice-start.6 = ((s8[14680064]{0:T(1024)(128)(4,1)}), s8[4194304]{0:T(1024)(128)(4,1)S(1)}, s32[]{:S(2)}) async-start(s8[14680064]{0:T(1024)(128)(4,1)} %bitcast.3), calls=%async_computation.6 | async-start | bytes 8388608
  1.1 4.9 %collective-permute-start = (bf16[4,3712]{1,0:T(4,128)(2,1)S(1)}, bf16[4,3712]{1,0:T(4,128)(2,1)S(1)}, u32[]{:S(2)}, u32[]{:S(2)}) collective-permute-start(bf16[4,3712]{1,0:T(4,128)(2,1)S(1)} %shard_map.109.refs_0_), channel_id=1, source_target_pairs={{0,2},{1,3},{2,0},{3,1},{4,6},{5,7},{6,4},{7,5},{8,10},{9,11},{10,... | collective-permute-start | bytes 89096 | tf_op jit(solution)/shard_map/ppermute | solution.py:180
  6.0 17.4 %slice-start.3 = ((s8[14680064]{0:T(1024)(128)(4,1)}), s8[2097152]{0:T(1024)(128)(4,1)S(1)}, s32[]{:S(2)}) async-start(s8[14680064]{0:T(1024)(128)(4,1)} %bitcast.1), calls=%async_computation.3 | async-start | bytes 4194304
  6.1 17.4 %slice-start.7 = ((s8[14680064]{0:T(1024)(128)(4,1)}), s8[2097152]{0:T(1024)(128)(4,1)S(1)}, s32[]{:S(2)}) async-start(s8[14680064]{0:T(1024)(128)(4,1)} %bitcast.3), calls=%async_computation.7 | async-start | bytes 4194304
  6.1 8.1 %collective-permute-start.1 = (bf16[8,3712]{1,0:T(8,128)(2,1)S(1)}, bf16[8,3712]{1,0:T(8,128)(2,1)S(1)}, u32[]{:S(2)}, u32[]{:S(2)}) collective-permute-start(bf16[8,3712]{1,0:T(8,128)(2,1)S(1)} %shard_map.110.rows_ref.refs_0_), channel_id=1, source_target_pairs={{0,4},{4,0},{8,12},{12,8},{1,5},{5,1},{9,13},{13,9},{2,6},{6,2},{1... | collective-permute-start | bytes 178184 | tf_op jit(solution)/shard_map/ppermute | solution.py:180
  8.2 6.4 %collective-permute-start.2 = (bf16[8,3712]{1,0:T(8,128)(2,1)S(1)}, bf16[8,3712]{1,0:T(8,128)(2,1)S(1)}, u32[]{:S(2)}, u32[]{:S(2)}) collective-permute-start(bf16[8,3712]{1,0:T(8,128)(2,1)S(1)} %shard_map.110.rows_ref.refs_0_), channel_id=1, source_target_pairs={{0,8},{4,12},{8,0},{12,4},{1,9},{5,13},{9,1},{13,5},{2,10},{6,14},... | collective-permute-start | bytes 178184 | tf_op jit(solution)/shard_map/ppermute | solution.py:180
  10.8 6.0 %collective-permute-start.3 = (bf16[8,3712]{1,0:T(8,128)(2,1)S(1)}, bf16[8,3712]{1,0:T(8,128)(2,1)S(1)}, u32[]{:S(2)}, u32[]{:S(2)}) collective-permute-start(bf16[8,3712]{1,0:T(8,128)(2,1)S(1)} %shard_map.110.rows_ref.refs_0_), channel_id=1, source_target_pairs={{0,12},{4,8},{8,4},{12,0},{1,13},{5,9},{9,5},{13,1},{2,14},{6,10},... | collective-permute-start | bytes 178184 | tf_op jit(solution)/shard_map/ppermute | solution.py:180
  16.9 1.6 %collective-permute-start.4 = (bf16[32,3712]{1,0:T(8,128)(2,1)S(1)}, bf16[32,3712]{1,0:T(8,128)(2,1)S(1)}, u32[]{:S(2)}, u32[]{:S(2)}) collective-permute-start(bf16[32,3712]{1,0:T(8,128)(2,1)S(1)} %shard_map.112.rows_ref.refs_0_), channel_id=1, source_target_pairs={{0,1},{1,0},{2,3},{3,2},{4,5},{5,4},{6,7},{7,6},{8,9},{9,8},{10,11... | collective-permute-start | bytes 712712 | tf_op jit(solution)/shard_map/ppermute | solution.py:180
  18.9 12.7 %copy-start = (bf16[256,896]{1,0:T(8,128)(2,1)S(1)}, bf16[256,896]{1,0:T(8,128)(2,1)}, u32[]{:S(2)}) copy-start(bf16[256,896]{1,0:T(8,128)(2,1)} %down_ref.3) | copy-start | bytes 1376260
  18.9 12.7 %collective-permute-start.5 = (bf16[64,512]{1,0:T(8,128)(2,1)S(1)}, bf16[64,512]{1,0:T(8,128)(2,1)S(1)}, u32[]{:S(2)}, u32[]{:S(2)}) collective-permute-start(bf16[64,512]{1,0:T(8,128)(2,1)S(1)} %shard_map.116.refs_0_), channel_id=1, source_target_pairs={{0,4},{4,0},{8,12},{12,8},{1,5},{5,1},{9,13},{13,9},{2,6},{6,2},{1... | collective-permute-start | bytes 196616 | tf_op jit(solution)/shard_map/ppermute | solution.py:180
  19.0 12.6 %collective-permute-start.6 = (bf16[64,512]{1,0:T(8,128)(2,1)S(1)}, bf16[64,512]{1,0:T(8,128)(2,1)S(1)}, u32[]{:S(2)}, u32[]{:S(2)}) collective-permute-start(bf16[64,512]{1,0:T(8,128)(2,1)S(1)} %shard_map.116.refs_0_), channel_id=1, source_target_pairs={{0,8},{4,12},{8,0},{12,4},{1,9},{5,13},{9,1},{13,5},{2,10},{6,14},... | collective-permute-start | bytes 196616 | tf_op jit(solution)/shard_map/ppermute | solution.py:180
  20.8 10.8 %collective-permute-start.7 = (bf16[64,512]{1,0:T(8,128)(2,1)S(1)}, bf16[64,512]{1,0:T(8,128)(2,1)S(1)}, u32[]{:S(2)}, u32[]{:S(2)}) collective-permute-start(bf16[64,512]{1,0:T(8,128)(2,1)S(1)} %shard_map.116.refs_0_), channel_id=1, source_target_pairs={{0,12},{4,8},{8,4},{12,0},{1,13},{5,9},{9,5},{13,1},{2,14},{6,10},... | collective-permute-start | bytes 196616 | tf_op jit(solution)/shard_map/ppermute | solution.py:180
  32.0 1.6 %collective-permute-start.8 = (bf16[32,3584]{1,0:T(8,128)(2,1)S(1)}, bf16[32,3584]{1,0:T(8,128)(2,1)S(1)}, u32[]{:S(2)}, u32[]{:S(2)}) collective-permute-start(bf16[32,3584]{1,0:T(8,128)(2,1)S(1)} %slice.33), channel_id=1, source_target_pairs={{0,1},{1,0},{2,3},{3,2},{4,5},{5,4},{6,7},{7,6},{8,9},{9,8},{10,11... | collective-permute-start | bytes 688136 | tf_op jit(solution)/shard_map/ppermute | solution.py:180
  33.6 5.6 %collective-permute-start.10 = (bf16[8,3584]{1,0:T(8,128)(2,1)S(1)}, bf16[8,3584]{1,0:T(8,128)(2,1)S(1)}, u32[]{:S(2)}, u32[]{:S(2)}) collective-permute-start(bf16[8,3584]{1,0:T(8,128)(2,1)S(1)} %get-tuple-element.41), channel_id=1, source_target_pairs={{0,8},{4,12},{8,0},{12,4},{1,9},{5,13},{9,1},{13,5},{2,10},{6,14},... | collective-permute-start | bytes 172040 | tf_op jit(solution)/shard_map/ppermute | solution.py:180
  33.7 5.5 %collective-permute-start.11 = (bf16[8,3584]{1,0:T(8,128)(2,1)S(1)}, bf16[8,3584]{1,0:T(8,128)(2,1)S(1)}, u32[]{:S(2)}, u32[]{:S(2)}) collective-permute-start(bf16[8,3584]{1,0:T(8,128)(2,1)S(1)} %get-tuple-element.40), channel_id=1, source_target_pairs={{0,4},{4,0},{8,12},{12,8},{1,5},{5,1},{9,13},{13,9},{2,6},{6,2},{1... | collective-permute-start | bytes 172040 | tf_op jit(solution)/shard_map/ppermute | solution.py:180
  35.5 6.0 %collective-permute-start.9 = (bf16[8,3584]{1,0:T(8,128)(2,1)S(1)}, bf16[8,3584]{1,0:T(8,128)(2,1)S(1)}, u32[]{:S(2)}, u32[]{:S(2)}) collective-permute-start(bf16[8,3584]{1,0:T(8,128)(2,1)S(1)} %get-tuple-element.39), channel_id=1, source_target_pairs={{0,12},{4,8},{8,4},{12,0},{1,13},{5,9},{9,5},{13,1},{2,14},{6,10},... | collective-permute-start | bytes 172040 | tf_op jit(solution)/shard_map/ppermute | solution.py:180
  41.5 3.9 %collective-permute-start.12 = (bf16[4,3584]{1,0:T(4,128)(2,1)S(1)}, bf16[4,3584]{1,0:T(4,128)(2,1)S(1)}, u32[]{:S(2)}, u32[]{:S(2)}) collective-permute-start(bf16[4,3584]{1,0:T(4,128)(2,1)S(1)} %slice.39), channel_id=1, source_target_pairs={{0,2},{1,3},{2,0},{3,1},{4,6},{5,7},{6,4},{7,5},{8,10},{9,11},{10,... | collective-permute-start | bytes 86024 | tf_op jit(solution)/shard_map/ppermute | solution.py:180

commit v7 on v6

--- a/solution.py
+++ b/solution.py
@@ -11,7 +11,7 @@
 NODE_GROUPS = 8
 LANES = 128
 MIB = 2**20
-NEAR_PLAN = (0, 4, 1)
+NEAR_PLAN = (0, 4, 0)
 DIRECT = 4
 WORTH = 40 * 10**9
 
@@ -50,20 +50,21 @@
     out_ref[:, count:] = total.astype(jnp.bfloat16)
 
 
-def shared_in_kernel(node_ref, x_ref, gate_ref, up_ref, out_ref):
+def shared_in_kernel(node_ref, x_ref, *refs):
+    weights, out_ref = refs[:-1], refs[-1]
     contract = (((1,), (1,)), ((), ()))
-    block, slab = gate_ref.shape
+    block, slab = weights[0].shape
     x = x_ref[...]
     if x.shape[1] != slab:
         x = x_ref[:, pl.ds(pl.multiple_of(node_ref[0] * slab, LANES), slab)]
-    for i, ref in enumerate((gate_ref, up_ref)):
+    for i, ref in enumerate(weights):
         part = lax.dot_general(x, ref[...], contract, preferred_element_type=jnp.float32)
         out_ref[:, i * block : (i + 1) * block] = part.astype(jnp.bfloat16)
 
 
 def routed_kernel(near_count, node_ref, x_ref, gate_hbm, up_ref, down_ref, *refs):
-    near_refs, out_ref = refs[:near_count], refs[near_count]
-    far_refs, sems = refs[near_count + 1 : -1], refs[-1]
+    near_refs, (keep_ref, send_ref) = refs[:near_count], refs[near_count : near_count + 2]
+    far_refs, out_ref, sems = refs[near_count + 2 : -2], refs[-2], refs[-1]
     held, count, _ = up_ref.shape
     copies = []
     for i, there in enumerate(far_refs):
@@ -99,11 +100,14 @@
             out_ref[...] += term
         if e + 1 < held:
             gate, up = later
-
-
-def shared_out_kernel(unit, node_ref, routed_ref, down_ref, *refs):
-    parts, out_ref = refs[:-1], refs[-1]
-    block, slab = down_ref.shape
+    half = keep_ref.shape[0]
+    keep_ref[...] = out_ref[:half, :]
+    send_ref[...] = out_ref[half:, :].astype(jnp.bfloat16)
+
+
+def shared_out_kernel(unit, node_ref, routed_ref, *refs):
+    downs, parts, out_ref = refs[:2], refs[2:-1], refs[-1]
+    block, slab = downs[0].shape
     count, width = out_ref.shape
     total = parts[0][...].astype(jnp.float32)
     to = lax.broadcasted_iota(jnp.int32, (count, count), 0)
@@ -111,14 +115,18 @@
     for k in range(1, len(parts)):
         place = (come == (to ^ (k * unit))).astype(jnp.bfloat16)
         total += jnp.dot(place, parts[k][...], preferred_element_type=jnp.float32)
-    hidden = (jax.nn.silu(total[:, :block]) * total[:, block:]).astype(jnp.bfloat16)
-    shared = jnp.dot(hidden, down_ref[...], preferred_element_type=jnp.float32)
+    shared = jnp.zeros((count, slab), jnp.float32)
+    for i, down_ref in enumerate(downs):
+        gate = total[:, 2 * i * block : (2 * i + 1) * block]
+        up = total[:, (2 * i + 1) * block : (2 * i + 2) * block]
+        hidden = (jax.nn.silu(gate) * up).astype(jnp.bfloat16)
+        shared += jnp.dot(hidden, down_ref[...], preferred_element_type=jnp.float32)
     if slab == width:
-        out_ref[...] = (routed_ref[...] + shared).astype(jnp.bfloat16)
+        out_ref[...] = routed_ref[...] + shared
     else:
-        out_ref[...] = routed_ref[...].astype(jnp.bfloat16)
+        out_ref[...] = routed_ref[...]
         columns = pl.ds(pl.multiple_of(node_ref[0] * slab, LANES), slab)
-        out_ref[:, columns] = (routed_ref[:, columns] + shared).astype(jnp.bfloat16)
+        out_ref[:, columns] = routed_ref[:, columns] + shared
 
 
 def bring_kernel(which, rows_ref, *refs):
@@ -231,6 +239,8 @@
         doubling = [("node", (1 << i,)) for i in range(node_count.bit_length() - 1)]
         stages = halves[:-1] + doubling + halves[-1:]
     node_unit = token_count << max(len(halves) - 1, 0)
+    aligned = slab % LANES == 0
+    shared_pair = [exchange(w, "local", 1) for w in (shared_gate, shared_up, shared_down)]
     ready = []
     for stage, (axis, bits) in enumerate(stages):
         others = [exchange(rows, axis, bit) for bit in bits]
@@ -243,30 +253,40 @@
             ready += got[: len(wanted)]
             if extra:
                 shared_gate, shared_up = got[len(wanted) :]
+        if stage == len(stages) - 1:
+            mine = rows
+            if not aligned:
+                mine = lax.dynamic_slice_in_dim(rows, node * slab, slab, axis=1)
+            shared_part = pl.pallas_call(
+                shared_in_kernel,
+                out_shape=jax.ShapeDtypeStruct((rows.shape[0], 4 * shared_block), jnp.bfloat16),
+                in_specs=[smem] + [vmem] * 5,
+                compiler_params=params,
+            )(place, mine, shared_gate, shared_up, *shared_pair[:2])
+            others, shared_part = lax.optimization_barrier((others, shared_part))
+            parts = [exchange(shared_part, "node", k) for k in range(1, node_count)]
+            parts = [shared_part] + parts
         rows = join(rows, *others)
     row_count = rows.shape[0]
 
-    aligned = slab % LANES == 0
-    mine = rows if aligned else lax.dynamic_slice_in_dim(rows, node * slab, slab, axis=1)
-    shared_part = pl.pallas_call(
-        shared_in_kernel,
-        out_shape=jax.ShapeDtypeStruct((row_count, 2 * shared_block), jnp.bfloat16),
-        in_specs=[smem, vmem, vmem, vmem],
-        compiler_params=params,
-    )(place, mine, shared_gate, shared_up)
-    parts = [shared_part] + [exchange(shared_part, "node", k) for k in range(1, node_count)]
-
     late = weights[len(ready) :]
     late_bytes = 2 * sum(math.prod(w.shape[1:]) for w, _ in late)
-    routed = pl.pallas_call(
+    half_shape = (row_count // 2, feature_count)
+    kept, sent = pl.pallas_call(
         functools.partial(routed_kernel, len(ready)),
-        out_shape=jax.ShapeDtypeStruct((row_count, feature_count), jnp.float32),
+        out_shape=[
+            jax.ShapeDtypeStruct(half_shape, jnp.float32),
+            jax.ShapeDtypeStruct(half_shape, jnp.bfloat16),
+        ],
         in_specs=[smem, vmem, hbm, vmem, vmem] + [vmem] * len(ready),
-        out_specs=vmem,
+        out_specs=[vmem, vmem],
         scratch_shapes=[pltpu.VMEM(w.shape[1:], jnp.bfloat16) for w, _ in late]
-        + [pltpu.SemaphoreType.DMA((max(len(late), 1),))],
+        + [
+            pltpu.VMEM((row_count, feature_count), jnp.float32),
+            pltpu.SemaphoreType.DMA((max(len(late), 1),)),
+        ],
         compiler_params=pltpu.CompilerParams(
-            vmem_limit_bytes=late_bytes + 12 * row_count * width + 4 * MIB
+            vmem_limit_bytes=late_bytes + 16 * row_count * width + 4 * MIB
         ),
     )(
         place,
@@ -277,19 +297,22 @@
         *ready,
     )
 
+    downs = [shared_down, shared_pair[2]]
     if not aligned:
-        shared_down = lax.dynamic_update_slice_in_dim(
-            jnp.zeros((shared_block, feature_count), shared_down.dtype), shared_down, node * slab, axis=1
-        )
-    out = pl.pallas_call(
+        wide = jnp.zeros((shared_block, feature_count), shared_down.dtype)
+        downs = [lax.dynamic_update_slice_in_dim(wide, w, node * slab, axis=1) for w in downs]
+    kept, sent, parts = lax.optimization_barrier((kept, sent, parts))
+    came = exchange(sent, "local", 1)
+    kept = pl.pallas_call(
         functools.partial(shared_out_kernel, node_unit),
-        out_shape=jax.ShapeDtypeStruct((row_count, feature_count), jnp.bfloat16),
-        in_specs=[smem] + [vmem] * (2 + node_count),
+        out_shape=jax.ShapeDtypeStruct(kept.shape, jnp.float32),
+        in_specs=[smem] + [vmem] * (3 + node_count),
         out_specs=vmem,
         compiler_params=params,
-    )(place, routed, shared_down, *parts)
-
-    for axis, bits in reversed(stages):
+    )(place, kept, *downs, *parts)
+    out = (kept + came.astype(jnp.float32)).astype(jnp.bfloat16)
+
+    for axis, bits in reversed(stages[:-1]):
         unit = out.shape[0] // (len(bits) + 1)
         total = out[:unit].astype(jnp.float32)
         for i in reversed(range(len(bits))):

time: 46.3 us -> 45.9 us (level)
  starting transfers between devices: 18.4 us -> 19.3 us
  Pallas kernels: 14.9 us -> 14.1 us
    ppermute x13 -> x16, starting transfers between devices: 18.4 us -> 19.3 us  [exchange(): return lax.ppermute(value, axis, [(i, i ^ bit) for i in range(size)])]
    pallas_call x2 -> x1, Pallas kernels: 4.88 us -> 4.17 us  [bring(): pl.pallas_call(functools.partial(bring_kernel, [e for _, e in wanted]), o...]
    ppermute x13 -> x16, waiting for transfers between devices: 11.7 us -> 11.3 us  [exchange(): return lax.ppermute(value, axis, [(i, i ^ bit) for i in range(size)])]
  transfers between devices with their start and end apart: 13 -> 16, of which waited for: 7 -> 7; matrix products, arithmetic and copies ran while one was open for 0% -> 0% of each run, Pallas kernels for 28% -> 31%
where the time goes in v7:
time: 45.9 us; the launch traced here: 45.7 us
  starting transfers between devices  19.3 us (42%)
  Pallas kernels  14.1 us (31%)
  waiting for transfers between devices  11.3 us (25%)
  other arithmetic  0.7 us (2%)
    ppermute x16, starting transfers between devices, exchange(): return lax.ppermute(value, axis, [(i, i ^ bit) for i in range(size)])  19.3 us
    ppermute x16, waiting for transfers between devices, exchange(): return lax.ppermute(value, axis, [(i, i ^ bit) for i in range(size)])  11.3 us
    pallas_call x1, Pallas kernels, local(): pl.pallas_call(functools.partial(routed_kernel, len(ready)), out_shape=[j...  7.87 us
    pallas_call x1, Pallas kernels, bring(): pl.pallas_call(functools.partial(bring_kernel, [e for _, e in wanted]), o...  4.17 us
    pallas_call x1, Pallas kernels, local(): pl.pallas_call(functools.partial(pack_kernel, per_group), out_shape=jax.S...  0.95 us
  transfers between devices with their start and end apart: 16, of which 7 were waited for; matrix products, arithmetic and copies ran while one was open for 0% of the time, Pallas kernels for 31%

profile of v7, /device:TPU:0, one launch (start us, length us, event | category | flops | bytes accessed | tf_op | source)
XLA Modules:
  0.0 45.7 jit_solution(3684072223823419301)
XLA Ops:
  0.0 0.5 collective-permute-start.5
  0.5 1.0 %shard_map.109.refs_0_ = bf16[4,3712]{1,0:T(4,128)(2,1)S(1)} custom-call(s32[1]{0:T(128)} %bitcast.node_ref, bf16[4,3584]{1,0:T(4,128)(2,1)} %refs_0_.3, f32[3584]{0:T(1024)} %refs_1_.2, s32[4,4]{1,0:T(4,128)} %refs_2_.2, s32[4,8]{1,0:T(4,128)} %refs_3_.2, bf16[4,8]{1,0:T(4,128)(2,1)} %refs_4_.2), custom_call_target="tpu_custom_call" | custom-call | flops 40000000000 | tf_op jit(solution)/shard_map/pallas_call | solution.py:223
  1.5 3.0 %collective-permute-start = (bf16[4,3712]{1,0:T(4,128)(2,1)S(1)}, bf16[4,3712]{1,0:T(4,128)(2,1)S(1)}, u32[]{:S(2)}, u32[]{:S(2)}) collective-permute-start(bf16[4,3712]{1,0:T(4,128)(2,1)S(1)} %shard_map.109.refs_0_), channel_id=1, source_target_pairs={{0,2},{1,3},{2,0},{3,1},{4,6},{5,7},{6,4},{7,5},{8,10},{9,11},{10,... | collective-permute-start | bytes 89096 | tf_op jit(solution)/shard_map/ppermute | solution.py:188
  4.5 1.9 %collective-permute-done.refs_1_ = bf16[4,3712]{1,0:T(4,128)(2,1)S(1)} collective-permute-done((bf16[4,3712]{1,0:T(4,128)(2,1)S(1)}, bf16[4,3712]{1,0:T(4,128)(2,1)S(1)}, u32[]{:S(2)}, u32[]{:S(2)}) %collective-permute-start) | collective-permute-done | bytes 29728 | tf_op jit(solution)/shard_map/ppermute | solution.py:188
  6.4 2.2 %collective-permute-start.1 = (bf16[8,3712]{1,0:T(8,128)(2,1)S(1)}, bf16[8,3712]{1,0:T(8,128)(2,1)S(1)}, u32[]{:S(2)}, u32[]{:S(2)}) collective-permute-start(bf16[8,3712]{1,0:T(8,128)(2,1)S(1)} %shard_map.110.rows_ref.refs_0_), channel_id=1, source_target_pairs={{0,4},{4,0},{8,12},{12,8},{1,5},{5,1},{9,13},{13,9},{2,6},{6,2},{1... | collective-permute-start | bytes 178184 | tf_op jit(solution)/shard_map/ppermute | solution.py:188
  8.6 2.6 %collective-permute-start.2 = (bf16[8,3712]{1,0:T(8,128)(2,1)S(1)}, bf16[8,3712]{1,0:T(8,128)(2,1)S(1)}, u32[]{:S(2)}, u32[]{:S(2)}) collective-permute-start(bf16[8,3712]{1,0:T(8,128)(2,1)S(1)} %shard_map.110.rows_ref.refs_0_), channel_id=1, source_target_pairs={{0,8},{4,12},{8,0},{12,4},{1,9},{5,13},{9,1},{13,5},{2,10},{6,14},... | collective-permute-start | bytes 178184 | tf_op jit(solution)/shard_map/ppermute | solution.py:188
  11.2 4.2 %shard_map.111 = (bf16[3584,256]{1,0:T(8,128)(2,1)S(1)}, bf16[3584,256]{1,0:T(8,128)(2,1)S(1)}, bf16[3584,256]{1,0:T(8,128)(2,1)S(1)}, bf16[3584,256]{1,0:T(8,12...) custom-call(bf16[8,3712]{1,0:T(8,128)(2,1)S(1)} %shard_map.110.rows_ref.refs_0_, ...), custom_call_target="tpu_custom_call" | custom-call | tf_op jit(solution)/shard_map/pallas_call | solution.py:147
  15.4 1.8 %collective-permute-done.3.refs_3_ = bf16[8,3712]{1,0:T(8,128)(2,1)S(1)} collective-permute-done((bf16[8,3712]{1,0:T(8,128)(2,1)S(1)}, bf16[8,3712]{1,0:T(8,128)(2,1)S(1)}, u32[]{:S(2)}, u32[]{:S(2)}) %collective-permute-start.3) | collective-permute-done | bytes 59424 | tf_op jit(solution)/shard_map/ppermute | solution.py:188
  17.3 0.5 %collective-permute-start.10 = (bf16[256,896]{1,0:T(8,128)(2,1)S(1)}, bf16[256,896]{1,0:T(8,128)(2,1)S(1)}, u32[]{:S(2)}, u32[]{:S(2)}) collective-permute-start(bf16[256,896]{1,0:T(8,128)(2,1)S(1)} %copy-done), channel_id=1, source_target_pairs={{0,1},{1,0},{2,3},{3,2},{4,5},{5,4},{6,7},{7,6},{8,9},{9,8},{10,11... | collective-permute-start | bytes 1376264 | tf_op jit(solution)/shard_map/ppermute | solution.py:188
  17.8 0.6 %shard_map.113.refs_2_ = bf16[32,1024]{1,0:T(8,128)(2,1)S(1)} custom-call(s32[1]{0:T(128)} %bitcast.node_ref, bf16[32,3712]{1,0:T(8,128)(2,1)S(1)} %shard_map.112.x_ref.refs_0_, bf16[256,896]{1,0:T(8,128)(2,1)S(1)} %get-tuple-element.39.refs_0_, bf16[256,896]{1,0:T(8,128)(2,1)S(1)} %get-tuple-element.40.refs_1_, ...), custom_call_target="tpu_custom_call" | custom-call | tf_op jit(solution)/shard_map/pallas_call | solution.py:260
  18.4 0.4 collective-permute-done.4.refs_1_
  18.8 2.6 %collective-permute-start.8 = (bf16[32,1024]{1,0:T(8,128)(2,1)S(1)}, bf16[32,1024]{1,0:T(8,128)(2,1)S(1)}, u32[]{:S(2)}, u32[]{:S(2)}) collective-permute-start(bf16[32,1024]{1,0:T(8,128)(2,1)S(1)} %shard_map.113.refs_2_), channel_id=1, source_target_pairs={{0,8},{4,12},{8,0},{12,4},{1,9},{5,13},{9,1},{13,5},{2,10},{6,14},... | collective-permute-start | bytes 196616 | tf_op jit(solution)/shard_map/ppermute | solution.py:188
  21.4 1.8 %collective-permute-start.9 = (bf16[32,1024]{1,0:T(8,128)(2,1)S(1)}, bf16[32,1024]{1,0:T(8,128)(2,1)S(1)}, u32[]{:S(2)}, u32[]{:S(2)}) collective-permute-start(bf16[32,1024]{1,0:T(8,128)(2,1)S(1)} %shard_map.113.refs_2_), channel_id=1, source_target_pairs={{0,12},{4,8},{8,4},{12,0},{1,13},{5,9},{9,5},{13,1},{2,14},{6,10},... | collective-permute-start | bytes 196616 | tf_op jit(solution)/shard_map/ppermute | solution.py:188
  23.3 7.9 %shard_map.115 = (f32[32,3584]{1,0:T(8,128)S(1)}, bf16[32,3584]{1,0:T(8,128)(2,1)S(1)}) custom-call(s32[1]{0:T(128)} %bitcast.node_ref, bf16[64,3712]{1,0:T(8,128)(2,1)S(1)} %shard_map.114.x_ref, bf16[8,3584,256]{2,1,0:T(8,128)(2,1)} %gate_hbm.1, bf16[8,3584,256]{2,1,0:T(8,128)(2,1)S(1)} %bitcast.2, bf16[8,256,3584]{2,1,0:T(8,128)(2,1)S(1)} %bitcast.4, ...), custom_call_target="tpu_custom_call" | custom-call | tf_op jit(solution)/shard_map/pallas_call | solution.py:275
  31.2 0.1 collective-permute-start.11
  31.3 0.4 shard_map.116
  31.7 1.0 %collective-permute-done.11 = bf16[32,3584]{1,0:T(8,128)(2,1)S(1)} collective-permute-done((bf16[32,3584]{1,0:T(8,128)(2,1)S(1)}, bf16[32,3584]{1,0:T(8,128)(2,1)S(1)}, u32[]{:S(2)}, u32[]{:S(2)}) %collective-permute-start.11) | collective-permute-done | bytes 229408 | tf_op jit(solution)/shard_map/ppermute | solution.py:188
  32.8 2.1 %collective-permute-start.12 = (bf16[8,3584]{1,0:T(8,128)(2,1)S(1)}, bf16[8,3584]{1,0:T(8,128)(2,1)S(1)}, u32[]{:S(2)}, u32[]{:S(2)}) collective-permute-start(bf16[8,3584]{1,0:T(8,128)(2,1)S(1)} %get-tuple-element.55), channel_id=1, source_target_pairs={{0,12},{4,8},{8,4},{12,0},{1,13},{5,9},{9,5},{13,1},{2,14},{6,10},... | collective-permute-start | bytes 172040 | tf_op jit(solution)/shard_map/ppermute | solution.py:188
  34.9 2.4 %collective-permute-start.14 = (bf16[8,3584]{1,0:T(8,128)(2,1)S(1)}, bf16[8,3584]{1,0:T(8,128)(2,1)S(1)}, u32[]{:S(2)}, u32[]{:S(2)}) collective-permute-start(bf16[8,3584]{1,0:T(8,128)(2,1)S(1)} %get-tuple-element.56), channel_id=1, source_target_pairs={{0,4},{4,0},{8,12},{12,8},{1,5},{5,1},{9,13},{13,9},{2,6},{6,2},{1... | collective-permute-start | bytes 172040 | tf_op jit(solution)/shard_map/ppermute | solution.py:188
  37.3 2.1 %collective-permute-done.12 = bf16[8,3584]{1,0:T(8,128)(2,1)S(1)} collective-permute-done((bf16[8,3584]{1,0:T(8,128)(2,1)S(1)}, bf16[8,3584]{1,0:T(8,128)(2,1)S(1)}, u32[]{:S(2)}, u32[]{:S(2)}) %collective-permute-start.12) | collective-permute-done | bytes 57376 | tf_op jit(solution)/shard_map/ppermute | solution.py:188
  39.4 1.7 %collective-permute-done.13 = bf16[8,3584]{1,0:T(8,128)(2,1)S(1)} collective-permute-done((bf16[8,3584]{1,0:T(8,128)(2,1)S(1)}, bf16[8,3584]{1,0:T(8,128)(2,1)S(1)}, u32[]{:S(2)}, u32[]{:S(2)}) %collective-permute-start.13) | collective-permute-done | bytes 57376 | tf_op jit(solution)/shard_map/ppermute | solution.py:188
  41.2 1.6 %collective-permute-start.15 = (bf16[4,3584]{1,0:T(4,128)(2,1)S(1)}, bf16[4,3584]{1,0:T(4,128)(2,1)S(1)}, u32[]{:S(2)}, u32[]{:S(2)}) collective-permute-start(bf16[4,3584]{1,0:T(4,128)(2,1)S(1)} %slice.29), channel_id=1, source_target_pairs={{0,2},{1,3},{2,0},{3,1},{4,6},{5,7},{6,4},{7,5},{8,10},{9,11},{10,... | collective-permute-start | bytes 86024 | tf_op jit(solution)/shard_map/ppermute | solution.py:188
  42.7 2.4 %collective-permute-done.15 = bf16[4,3584]{1,0:T(4,128)(2,1)S(1)} collective-permute-done((bf16[4,3584]{1,0:T(4,128)(2,1)S(1)}, bf16[4,3584]{1,0:T(4,128)(2,1)S(1)}, u32[]{:S(2)}, u32[]{:S(2)}) %collective-permute-start.15) | collective-permute-done | bytes 28704 | tf_op jit(solution)/shard_map/ppermute | solution.py:188
  45.1 0.6 %add_convert_fusion.2 = bf16[4,3584]{1,0:T(4,128)(2,1)} fusion(bf16[4,3584]{1,0:T(4,128)(2,1)S(1)} %collective-permute-done.15, bf16[8,3584]{1,0:T(8,128)(2,1)S(1)} %add_convert_fusion.1), kind=kLoop, calls=%fused_computation.2 | loop fusion | flops 57344 | bytes 86016 | tf_op jit(solution)/shard_map/convert_element_type | solution.py:321
  (41 shorter events, 0.4 us)
Async XLA Ops:
  0.0 17.8 %collective-permute-start.5 = (bf16[256,896]{1,0:T(8,128)(2,1)}, bf16[256,896]{1,0:T(8,128)(2,1)S(1)}, u32[]{:S(2)}, u32[]{:S(2)}) collective-permute-start(bf16[256,896]{1,0:T(8,128)(2,1)} %refs_4_.3), channel_id=1, source_target_pairs={{0,1},{1,0},{2,3},{3,2},{4,5},{5,4},{6,7},{7,6},{8,9},{9,8},{10,11... | collective-permute-start | bytes 1376264 | tf_op jit(solution)/shard_map/ppermute | solution.py:188
  0.5 17.4 %collective-permute-start.6 = (bf16[256,896]{1,0:T(8,128)(2,1)}, bf16[256,896]{1,0:T(8,128)(2,1)S(1)}, u32[]{:S(2)}, u32[]{:S(2)}) collective-permute-start(bf16[256,896]{1,0:T(8,128)(2,1)} %refs_5_.1), channel_id=1, source_target_pairs={{0,1},{1,0},{2,3},{3,2},{4,5},{5,4},{6,7},{7,6},{8,9},{9,8},{10,11... | collective-permute-start | bytes 1376264 | tf_op jit(solution)/shard_map/ppermute | solution.py:188
  1.5 4.9 %collective-permute-start = (bf16[4,3712]{1,0:T(4,128)(2,1)S(1)}, bf16[4,3712]{1,0:T(4,128)(2,1)S(1)}, u32[]{:S(2)}, u32[]{:S(2)}) collective-permute-start(bf16[4,3712]{1,0:T(4,128)(2,1)S(1)} %shard_map.109.refs_0_), channel_id=1, source_target_pairs={{0,2},{1,3},{2,0},{3,1},{4,6},{5,7},{6,4},{7,5},{8,10},{9,11},{10,... | collective-permute-start | bytes 89096 | tf_op jit(solution)/shard_map/ppermute | solution.py:188
  6.3 16.9 %slice-start = ((s8[14680064]{0:T(1024)(128)(4,1)}), s8[4194304]{0:T(1024)(128)(4,1)S(1)}, s32[]{:S(2)}) async-start(s8[14680064]{0:T(1024)(128)(4,1)} %bitcast.1), calls=%async_computation | async-start | bytes 8388608
  6.3 16.9 %slice-start.4 = ((s8[14680064]{0:T(1024)(128)(4,1)}), s8[4194304]{0:T(1024)(128)(4,1)S(1)}, s32[]{:S(2)}) async-start(s8[14680064]{0:T(1024)(128)(4,1)} %bitcast.3), calls=%async_computation.4 | async-start | bytes 8388608
  6.4 16.9 %slice-start.1 = ((s8[14680064]{0:T(1024)(128)(4,1)}), s8[4194304]{0:T(1024)(128)(4,1)S(1)}, s32[]{:S(2)}) async-start(s8[14680064]{0:T(1024)(128)(4,1)} %bitcast.1), calls=%async_computation.1 | async-start | bytes 8388608
  6.4 16.9 %slice-start.2 = ((s8[14680064]{0:T(1024)(128)(4,1)}), s8[4194304]{0:T(1024)(128)(4,1)S(1)}, s32[]{:S(2)}) async-start(s8[14680064]{0:T(1024)(128)(4,1)} %bitcast.1), calls=%async_computation.2 | async-start | bytes 8388608
  6.4 16.9 %slice-start.3 = ((s8[14680064]{0:T(1024)(128)(4,1)}), s8[2097152]{0:T(1024)(128)(4,1)S(1)}, s32[]{:S(2)}) async-start(s8[14680064]{0:T(1024)(128)(4,1)} %bitcast.1), calls=%async_computation.3 | async-start | bytes 4194304
  6.4 16.9 %slice-start.5 = ((s8[14680064]{0:T(1024)(128)(4,1)}), s8[4194304]{0:T(1024)(128)(4,1)S(1)}, s32[]{:S(2)}) async-start(s8[14680064]{0:T(1024)(128)(4,1)} %bitcast.3), calls=%async_computation.5 | async-start | bytes 8388608
  6.4 16.9 %slice-start.6 = ((s8[14680064]{0:T(1024)(128)(4,1)}), s8[4194304]{0:T(1024)(128)(4,1)S(1)}, s32[]{:S(2)}) async-start(s8[14680064]{0:T(1024)(128)(4,1)} %bitcast.3), calls=%async_computation.6 | async-start | bytes 8388608
  6.4 16.9 %slice-start.7 = ((s8[14680064]{0:T(1024)(128)(4,1)}), s8[2097152]{0:T(1024)(128)(4,1)S(1)}, s32[]{:S(2)}) async-start(s8[14680064]{0:T(1024)(128)(4,1)} %bitcast.3), calls=%async_computation.7 | async-start | bytes 4194304
  6.4 8.9 %collective-permute-start.1 = (bf16[8,3712]{1,0:T(8,128)(2,1)S(1)}, bf16[8,3712]{1,0:T(8,128)(2,1)S(1)}, u32[]{:S(2)}, u32[]{:S(2)}) collective-permute-start(bf16[8,3712]{1,0:T(8,128)(2,1)S(1)} %shard_map.110.rows_ref.refs_0_), channel_id=1, source_target_pairs={{0,4},{4,0},{8,12},{12,8},{1,5},{5,1},{9,13},{13,9},{2,6},{6,2},{1... | collective-permute-start | bytes 178184 | tf_op jit(solution)/shard_map/ppermute | solution.py:188
  8.6 6.8 %collective-permute-start.2 = (bf16[8,3712]{1,0:T(8,128)(2,1)S(1)}, bf16[8,3712]{1,0:T(8,128)(2,1)S(1)}, u32[]{:S(2)}, u32[]{:S(2)}) collective-permute-start(bf16[8,3712]{1,0:T(8,128)(2,1)S(1)} %shard_map.110.rows_ref.refs_0_), channel_id=1, source_target_pairs={{0,8},{4,12},{8,0},{12,4},{1,9},{5,13},{9,1},{13,5},{2,10},{6,14},... | collective-permute-start | bytes 178184 | tf_op jit(solution)/shard_map/ppermute | solution.py:188
  11.2 6.0 %collective-permute-start.3 = (bf16[8,3712]{1,0:T(8,128)(2,1)S(1)}, bf16[8,3712]{1,0:T(8,128)(2,1)S(1)}, u32[]{:S(2)}, u32[]{:S(2)}) collective-permute-start(bf16[8,3712]{1,0:T(8,128)(2,1)S(1)} %shard_map.110.rows_ref.refs_0_), channel_id=1, source_target_pairs={{0,12},{4,8},{8,4},{12,0},{1,13},{5,9},{9,5},{13,1},{2,14},{6,10},... | collective-permute-start | bytes 178184 | tf_op jit(solution)/shard_map/ppermute | solution.py:188
  17.2 1.6 %collective-permute-start.4 = (bf16[32,3712]{1,0:T(8,128)(2,1)S(1)}, bf16[32,3712]{1,0:T(8,128)(2,1)S(1)}, u32[]{:S(2)}, u32[]{:S(2)}) collective-permute-start(bf16[32,3712]{1,0:T(8,128)(2,1)S(1)} %shard_map.112.x_ref.refs_0_), channel_id=1, source_target_pairs={{0,1},{1,0},{2,3},{3,2},{4,5},{5,4},{6,7},{7,6},{8,9},{9,8},{10,11... | collective-permute-start | bytes 712712 | tf_op jit(solution)/shard_map/ppermute | solution.py:188
  17.3 14.0 %collective-permute-start.10 = (bf16[256,896]{1,0:T(8,128)(2,1)S(1)}, bf16[256,896]{1,0:T(8,128)(2,1)S(1)}, u32[]{:S(2)}, u32[]{:S(2)}) collective-permute-start(bf16[256,896]{1,0:T(8,128)(2,1)S(1)} %copy-done), channel_id=1, source_target_pairs={{0,1},{1,0},{2,3},{3,2},{4,5},{5,4},{6,7},{7,6},{8,9},{9,8},{10,11... | collective-permute-start | bytes 1376264 | tf_op jit(solution)/shard_map/ppermute | solution.py:188
  18.8 12.4 %collective-permute-start.7 = (bf16[32,1024]{1,0:T(8,128)(2,1)S(1)}, bf16[32,1024]{1,0:T(8,128)(2,1)S(1)}, u32[]{:S(2)}, u32[]{:S(2)}) collective-permute-start(bf16[32,1024]{1,0:T(8,128)(2,1)S(1)} %shard_map.113.refs_2_), channel_id=1, source_target_pairs={{0,4},{4,0},{8,12},{12,8},{1,5},{5,1},{9,13},{13,9},{2,6},{6,2},{1... | collective-permute-start | bytes 196616 | tf_op jit(solution)/shard_map/ppermute | solution.py:188
  18.8 12.4 %collective-permute-start.8 = (bf16[32,1024]{1,0:T(8,128)(2,1)S(1)}, bf16[32,1024]{1,0:T(8,128)(2,1)S(1)}, u32[]{:S(2)}, u32[]{:S(2)}) collective-permute-start(bf16[32,1024]{1,0:T(8,128)(2,1)S(1)} %shard_map.113.refs_2_), channel_id=1, source_target_pairs={{0,8},{4,12},{8,0},{12,4},{1,9},{5,13},{9,1},{13,5},{2,10},{6,14},... | collective-permute-start | bytes 196616 | tf_op jit(solution)/shard_map/ppermute | solution.py:188
  21.4 9.8 %collective-permute-start.9 = (bf16[32,1024]{1,0:T(8,128)(2,1)S(1)}, bf16[32,1024]{1,0:T(8,128)(2,1)S(1)}, u32[]{:S(2)}, u32[]{:S(2)}) collective-permute-start(bf16[32,1024]{1,0:T(8,128)(2,1)S(1)} %shard_map.113.refs_2_), channel_id=1, source_target_pairs={{0,12},{4,8},{8,4},{12,0},{1,13},{5,9},{9,5},{13,1},{2,14},{6,10},... | collective-permute-start | bytes 196616 | tf_op jit(solution)/shard_map/ppermute | solution.py:188
  31.2 1.6 %collective-permute-start.11 = (bf16[32,3584]{1,0:T(8,128)(2,1)S(1)}, bf16[32,3584]{1,0:T(8,128)(2,1)S(1)}, u32[]{:S(2)}, u32[]{:S(2)}) collective-permute-start(bf16[32,3584]{1,0:T(8,128)(2,1)S(1)} %get-tuple-element.54), channel_id=1, source_target_pairs={{0,1},{1,0},{2,3},{3,2},{4,5},{5,4},{6,7},{7,6},{8,9},{9,8},{10,11... | collective-permute-start | bytes 688136 | tf_op jit(solution)/shard_map/ppermute | solution.py:188
  32.8 6.6 %collective-permute-start.12 = (bf16[8,3584]{1,0:T(8,128)(2,1)S(1)}, bf16[8,3584]{1,0:T(8,128)(2,1)S(1)}, u32[]{:S(2)}, u32[]{:S(2)}) collective-permute-start(bf16[8,3584]{1,0:T(8,128)(2,1)S(1)} %get-tuple-element.55), channel_id=1, source_target_pairs={{0,12},{4,8},{8,4},{12,0},{1,13},{5,9},{9,5},{13,1},{2,14},{6,10},... | collective-permute-start | bytes 172040 | tf_op jit(solution)/shard_map/ppermute | solution.py:188
  34.9 6.2 %collective-permute-start.13 = (bf16[8,3584]{1,0:T(8,128)(2,1)S(1)}, bf16[8,3584]{1,0:T(8,128)(2,1)S(1)}, u32[]{:S(2)}, u32[]{:S(2)}) collective-permute-start(bf16[8,3584]{1,0:T(8,128)(2,1)S(1)} %get-tuple-element.57), channel_id=1, source_target_pairs={{0,8},{4,12},{8,0},{12,4},{1,9},{5,13},{9,1},{13,5},{2,10},{6,14},... | collective-permute-start | bytes 172040 | tf_op jit(solution)/shard_map/ppermute | solution.py:188
  34.9 6.2 %collective-permute-start.14 = (bf16[8,3584]{1,0:T(8,128)(2,1)S(1)}, bf16[8,3584]{1,0:T(8,128)(2,1)S(1)}, u32[]{:S(2)}, u32[]{:S(2)}) collective-permute-start(bf16[8,3584]{1,0:T(8,128)(2,1)S(1)} %get-tuple-element.56), channel_id=1, source_target_pairs={{0,4},{4,0},{8,12},{12,8},{1,5},{5,1},{9,13},{13,9},{2,6},{6,2},{1... | collective-permute-start | bytes 172040 | tf_op jit(solution)/shard_map/ppermute | solution.py:188
  41.2 3.9 %collective-permute-start.15 = (bf16[4,3584]{1,0:T(4,128)(2,1)S(1)}, bf16[4,3584]{1,0:T(4,128)(2,1)S(1)}, u32[]{:S(2)}, u32[]{:S(2)}) collective-permute-start(bf16[4,3584]{1,0:T(4,128)(2,1)S(1)} %slice.29), channel_id=1, source_target_pairs={{0,2},{1,3},{2,0},{3,1},{4,6},{5,7},{6,4},{7,5},{8,10},{9,11},{10,... | collective-permute-start | bytes 86024 | tf_op jit(solution)/shard_map/ppermute | solution.py:188
  (1 other events, 10.9 us)

commit v8 on v7

--- a/solution.py
+++ b/solution.py
@@ -13,7 +13,7 @@
 MIB = 2**20
 NEAR_PLAN = (0, 4, 0)
 DIRECT = 4
-WORTH = 40 * 10**9
+WORTH = 80 * 10**9
 
 
 def pack_kernel(per_group, node_ref, *refs):
@@ -263,8 +263,8 @@
                 in_specs=[smem] + [vmem] * 5,
                 compiler_params=params,
             )(place, mine, shared_gate, shared_up, *shared_pair[:2])
+            parts = [exchange(shared_part, "node", k) for k in range(1, node_count)]
             others, shared_part = lax.optimization_barrier((others, shared_part))
-            parts = [exchange(shared_part, "node", k) for k in range(1, node_count)]
             parts = [shared_part] + parts
         rows = join(rows, *others)
     row_count = rows.shape[0]

time: 45.9 us -> 45.6 us (level)
  transfers between devices with their start and end apart: 16 -> 16, of which waited for: 7 -> 6; matrix products, arithmetic and copies ran while one was open for 0% -> 0% of each run, Pallas kernels for 31% -> 31%
where the time goes in v8:
time: 45.6 us; the launch traced here: 45.4 us
  starting transfers between devices  19.3 us (42%)
  Pallas kernels  14.1 us (31%)
  waiting for transfers between devices  10.9 us (24%)
  other arithmetic  0.7 us (2%)
    ppermute x16, starting transfers between devices, exchange(): return lax.ppermute(value, axis, [(i, i ^ bit) for i in range(size)])  19.3 us
    ppermute x16, waiting for transfers between devices, exchange(): return lax.ppermute(value, axis, [(i, i ^ bit) for i in range(size)])  10.9 us
    pallas_call x1, Pallas kernels, local(): pl.pallas_call(functools.partial(routed_kernel, len(ready)), out_shape=[j...  7.86 us
    pallas_call x1, Pallas kernels, bring(): pl.pallas_call(functools.partial(bring_kernel, [e for _, e in wanted]), o...  4.17 us
    pallas_call x1, Pallas kernels, local(): pl.pallas_call(functools.partial(pack_kernel, per_group), out_shape=jax.S...  0.95 us
  transfers between devices with their start and end apart: 16, of which 6 were waited for; matrix products, arithmetic and copies ran while one was open for 0% of the time, Pallas kernels for 31%

profile of v8, /device:TPU:0, one launch (start us, length us, event | category | flops | bytes accessed | tf_op | source)
XLA Modules:
  0.0 45.4 jit_solution(4425197585551926851)
XLA Ops:
  0.0 0.5 collective-permute-start.5
  0.5 1.0 %shard_map.109.refs_0_ = bf16[4,3712]{1,0:T(4,128)(2,1)S(1)} custom-call(s32[1]{0:T(128)} %bitcast.node_ref, bf16[4,3584]{1,0:T(4,128)(2,1)} %refs_0_.3, f32[3584]{0:T(1024)} %refs_1_.2, s32[4,4]{1,0:T(4,128)} %refs_2_.2, s32[4,8]{1,0:T(4,128)} %refs_3_.2, bf16[4,8]{1,0:T(4,128)(2,1)} %refs_4_.2), custom_call_target="tpu_custom_call" | custom-call | flops 80000000000 | tf_op jit(solution)/shard_map/pallas_call | solution.py:223
  1.5 3.0 %collective-permute-start = (bf16[4,3712]{1,0:T(4,128)(2,1)S(1)}, bf16[4,3712]{1,0:T(4,128)(2,1)S(1)}, u32[]{:S(2)}, u32[]{:S(2)}) collective-permute-start(bf16[4,3712]{1,0:T(4,128)(2,1)S(1)} %shard_map.109.refs_0_), channel_id=1, source_target_pairs={{0,2},{1,3},{2,0},{3,1},{4,6},{5,7},{6,4},{7,5},{8,10},{9,11},{10,... | collective-permute-start | bytes 89096 | tf_op jit(solution)/shard_map/ppermute | solution.py:188
  4.5 1.9 %collective-permute-done.refs_1_ = bf16[4,3712]{1,0:T(4,128)(2,1)S(1)} collective-permute-done((bf16[4,3712]{1,0:T(4,128)(2,1)S(1)}, bf16[4,3712]{1,0:T(4,128)(2,1)S(1)}, u32[]{:S(2)}, u32[]{:S(2)}) %collective-permute-start) | collective-permute-done | bytes 29728 | tf_op jit(solution)/shard_map/ppermute | solution.py:188
  6.4 2.2 %collective-permute-start.1 = (bf16[8,3712]{1,0:T(8,128)(2,1)S(1)}, bf16[8,3712]{1,0:T(8,128)(2,1)S(1)}, u32[]{:S(2)}, u32[]{:S(2)}) collective-permute-start(bf16[8,3712]{1,0:T(8,128)(2,1)S(1)} %shard_map.110.rows_ref.refs_0_), channel_id=1, source_target_pairs={{0,4},{4,0},{8,12},{12,8},{1,5},{5,1},{9,13},{13,9},{2,6},{6,2},{1... | collective-permute-start | bytes 178184 | tf_op jit(solution)/shard_map/ppermute | solution.py:188
  8.6 2.6 %collective-permute-start.2 = (bf16[8,3712]{1,0:T(8,128)(2,1)S(1)}, bf16[8,3712]{1,0:T(8,128)(2,1)S(1)}, u32[]{:S(2)}, u32[]{:S(2)}) collective-permute-start(bf16[8,3712]{1,0:T(8,128)(2,1)S(1)} %shard_map.110.rows_ref.refs_0_), channel_id=1, source_target_pairs={{0,8},{4,12},{8,0},{12,4},{1,9},{5,13},{9,1},{13,5},{2,10},{6,14},... | collective-permute-start | bytes 178184 | tf_op jit(solution)/shard_map/ppermute | solution.py:188
  11.2 4.2 %shard_map.111 = (bf16[3584,256]{1,0:T(8,128)(2,1)S(1)}, bf16[3584,256]{1,0:T(8,128)(2,1)S(1)}, bf16[3584,256]{1,0:T(8,128)(2,1)S(1)}, bf16[3584,256]{1,0:T(8,12...) custom-call(bf16[8,3712]{1,0:T(8,128)(2,1)S(1)} %shard_map.110.rows_ref.refs_0_, ...), custom_call_target="tpu_custom_call" | custom-call | tf_op jit(solution)/shard_map/pallas_call | solution.py:147
  15.4 1.8 %collective-permute-done.3.refs_3_ = bf16[8,3712]{1,0:T(8,128)(2,1)S(1)} collective-permute-done((bf16[8,3712]{1,0:T(8,128)(2,1)S(1)}, bf16[8,3712]{1,0:T(8,128)(2,1)S(1)}, u32[]{:S(2)}, u32[]{:S(2)}) %collective-permute-start.3) | collective-permute-done | bytes 59424 | tf_op jit(solution)/shard_map/ppermute | solution.py:188
  17.2 0.1 collective-permute-start.4
  17.3 0.5 %collective-permute-start.10 = (bf16[256,896]{1,0:T(8,128)(2,1)S(1)}, bf16[256,896]{1,0:T(8,128)(2,1)S(1)}, u32[]{:S(2)}, u32[]{:S(2)}) collective-permute-start(bf16[256,896]{1,0:T(8,128)(2,1)S(1)} %copy-done), channel_id=1, source_target_pairs={{0,1},{1,0},{2,3},{3,2},{4,5},{5,4},{6,7},{7,6},{8,9},{9,8},{10,11... | collective-permute-start | bytes 1376264 | tf_op jit(solution)/shard_map/ppermute | solution.py:188
  17.8 0.6 %shard_map.113.refs_2_ = bf16[32,1024]{1,0:T(8,128)(2,1)S(1)} custom-call(s32[1]{0:T(128)} %bitcast.node_ref, bf16[32,3712]{1,0:T(8,128)(2,1)S(1)} %shard_map.112.x_ref.refs_0_, bf16[256,896]{1,0:T(8,128)(2,1)S(1)} %get-tuple-element.39.refs_0_, bf16[256,896]{1,0:T(8,128)(2,1)S(1)} %get-tuple-element.40.refs_1_, ...), custom_call_target="tpu_custom_call" | custom-call | tf_op jit(solution)/shard_map/pallas_call | solution.py:260
  18.5 2.6 %collective-permute-start.8 = (bf16[32,1024]{1,0:T(8,128)(2,1)S(1)}, bf16[32,1024]{1,0:T(8,128)(2,1)S(1)}, u32[]{:S(2)}, u32[]{:S(2)}) collective-permute-start(bf16[32,1024]{1,0:T(8,128)(2,1)S(1)} %shard_map.113.refs_2_), channel_id=1, source_target_pairs={{0,8},{4,12},{8,0},{12,4},{1,9},{5,13},{9,1},{13,5},{2,10},{6,14},... | collective-permute-start | bytes 196616 | tf_op jit(solution)/shard_map/ppermute | solution.py:188
  21.1 1.8 %collective-permute-start.9 = (bf16[32,1024]{1,0:T(8,128)(2,1)S(1)}, bf16[32,1024]{1,0:T(8,128)(2,1)S(1)}, u32[]{:S(2)}, u32[]{:S(2)}) collective-permute-start(bf16[32,1024]{1,0:T(8,128)(2,1)S(1)} %shard_map.113.refs_2_), channel_id=1, source_target_pairs={{0,12},{4,8},{8,4},{12,0},{1,13},{5,9},{9,5},{13,1},{2,14},{6,10},... | collective-permute-start | bytes 196616 | tf_op jit(solution)/shard_map/ppermute | solution.py:188
  23.0 7.9 %shard_map.115 = (f32[32,3584]{1,0:T(8,128)S(1)}, bf16[32,3584]{1,0:T(8,128)(2,1)S(1)}) custom-call(s32[1]{0:T(128)} %bitcast.node_ref, bf16[64,3712]{1,0:T(8,128)(2,1)S(1)} %shard_map.114.x_ref, bf16[8,3584,256]{2,1,0:T(8,128)(2,1)} %gate_hbm.1, bf16[8,3584,256]{2,1,0:T(8,128)(2,1)S(1)} %bitcast.2, bf16[8,256,3584]{2,1,0:T(8,128)(2,1)S(1)} %bitcast.4, ...), custom_call_target="tpu_custom_call" | custom-call | tf_op jit(solution)/shard_map/pallas_call | solution.py:275
  30.9 0.1 collective-permute-start.11
  31.0 0.4 shard_map.116
  31.4 1.0 %collective-permute-done.11 = bf16[32,3584]{1,0:T(8,128)(2,1)S(1)} collective-permute-done((bf16[32,3584]{1,0:T(8,128)(2,1)S(1)}, bf16[32,3584]{1,0:T(8,128)(2,1)S(1)}, u32[]{:S(2)}, u32[]{:S(2)}) %collective-permute-start.11) | collective-permute-done | bytes 229408 | tf_op jit(solution)/shard_map/ppermute | solution.py:188
  32.5 2.1 %collective-permute-start.12 = (bf16[8,3584]{1,0:T(8,128)(2,1)S(1)}, bf16[8,3584]{1,0:T(8,128)(2,1)S(1)}, u32[]{:S(2)}, u32[]{:S(2)}) collective-permute-start(bf16[8,3584]{1,0:T(8,128)(2,1)S(1)} %get-tuple-element.55), channel_id=1, source_target_pairs={{0,12},{4,8},{8,4},{12,0},{1,13},{5,9},{9,5},{13,1},{2,14},{6,10},... | collective-permute-start | bytes 172040 | tf_op jit(solution)/shard_map/ppermute | solution.py:188
  34.6 2.3 %collective-permute-start.14 = (bf16[8,3584]{1,0:T(8,128)(2,1)S(1)}, bf16[8,3584]{1,0:T(8,128)(2,1)S(1)}, u32[]{:S(2)}, u32[]{:S(2)}) collective-permute-start(bf16[8,3584]{1,0:T(8,128)(2,1)S(1)} %get-tuple-element.56), channel_id=1, source_target_pairs={{0,4},{4,0},{8,12},{12,8},{1,5},{5,1},{9,13},{13,9},{2,6},{6,2},{1... | collective-permute-start | bytes 172040 | tf_op jit(solution)/shard_map/ppermute | solution.py:188
  37.0 2.1 %collective-permute-done.12 = bf16[8,3584]{1,0:T(8,128)(2,1)S(1)} collective-permute-done((bf16[8,3584]{1,0:T(8,128)(2,1)S(1)}, bf16[8,3584]{1,0:T(8,128)(2,1)S(1)}, u32[]{:S(2)}, u32[]{:S(2)}) %collective-permute-start.12) | collective-permute-done | bytes 57376 | tf_op jit(solution)/shard_map/ppermute | solution.py:188
  39.1 1.7 %collective-permute-done.13 = bf16[8,3584]{1,0:T(8,128)(2,1)S(1)} collective-permute-done((bf16[8,3584]{1,0:T(8,128)(2,1)S(1)}, bf16[8,3584]{1,0:T(8,128)(2,1)S(1)}, u32[]{:S(2)}, u32[]{:S(2)}) %collective-permute-start.13) | collective-permute-done | bytes 57376 | tf_op jit(solution)/shard_map/ppermute | solution.py:188
  40.9 1.6 %collective-permute-start.15 = (bf16[4,3584]{1,0:T(4,128)(2,1)S(1)}, bf16[4,3584]{1,0:T(4,128)(2,1)S(1)}, u32[]{:S(2)}, u32[]{:S(2)}) collective-permute-start(bf16[4,3584]{1,0:T(4,128)(2,1)S(1)} %slice.29), channel_id=1, source_target_pairs={{0,2},{1,3},{2,0},{3,1},{4,6},{5,7},{6,4},{7,5},{8,10},{9,11},{10,... | collective-permute-start | bytes 86024 | tf_op jit(solution)/shard_map/ppermute | solution.py:188
  42.4 2.4 %collective-permute-done.15 = bf16[4,3584]{1,0:T(4,128)(2,1)S(1)} collective-permute-done((bf16[4,3584]{1,0:T(4,128)(2,1)S(1)}, bf16[4,3584]{1,0:T(4,128)(2,1)S(1)}, u32[]{:S(2)}, u32[]{:S(2)}) %collective-permute-start.15) | collective-permute-done | bytes 28704 | tf_op jit(solution)/shard_map/ppermute | solution.py:188
  44.8 0.6 %add_convert_fusion.2 = bf16[4,3584]{1,0:T(4,128)(2,1)} fusion(bf16[4,3584]{1,0:T(4,128)(2,1)S(1)} %collective-permute-done.15, bf16[8,3584]{1,0:T(8,128)(2,1)S(1)} %add_convert_fusion.1), kind=kLoop, calls=%fused_computation.2 | loop fusion | flops 57344 | bytes 86016 | tf_op jit(solution)/shard_map/convert_element_type | solution.py:321
  (41 shorter events, 0.4 us)
Async XLA Ops:
  0.0 17.8 %collective-permute-start.5 = (bf16[256,896]{1,0:T(8,128)(2,1)}, bf16[256,896]{1,0:T(8,128)(2,1)S(1)}, u32[]{:S(2)}, u32[]{:S(2)}) collective-permute-start(bf16[256,896]{1,0:T(8,128)(2,1)} %refs_4_.3), channel_id=1, source_target_pairs={{0,1},{1,0},{2,3},{3,2},{4,5},{5,4},{6,7},{7,6},{8,9},{9,8},{10,11... | collective-permute-start | bytes 1376264 | tf_op jit(solution)/shard_map/ppermute | solution.py:188
  0.5 17.4 %collective-permute-start.6 = (bf16[256,896]{1,0:T(8,128)(2,1)}, bf16[256,896]{1,0:T(8,128)(2,1)S(1)}, u32[]{:S(2)}, u32[]{:S(2)}) collective-permute-start(bf16[256,896]{1,0:T(8,128)(2,1)} %refs_5_.1), channel_id=1, source_target_pairs={{0,1},{1,0},{2,3},{3,2},{4,5},{5,4},{6,7},{7,6},{8,9},{9,8},{10,11... | collective-permute-start | bytes 1376264 | tf_op jit(solution)/shard_map/ppermute | solution.py:188
  1.5 4.9 %collective-permute-start = (bf16[4,3712]{1,0:T(4,128)(2,1)S(1)}, bf16[4,3712]{1,0:T(4,128)(2,1)S(1)}, u32[]{:S(2)}, u32[]{:S(2)}) collective-permute-start(bf16[4,3712]{1,0:T(4,128)(2,1)S(1)} %shard_map.109.refs_0_), channel_id=1, source_target_pairs={{0,2},{1,3},{2,0},{3,1},{4,6},{5,7},{6,4},{7,5},{8,10},{9,11},{10,... | collective-permute-start | bytes 89096 | tf_op jit(solution)/shard_map/ppermute | solution.py:188
  6.3 16.6 %slice-start = ((s8[14680064]{0:T(1024)(128)(4,1)}), s8[4194304]{0:T(1024)(128)(4,1)S(1)}, s32[]{:S(2)}) async-start(s8[14680064]{0:T(1024)(128)(4,1)} %bitcast.1), calls=%async_computation | async-start | bytes 8388608
  6.3 16.6 %slice-start.4 = ((s8[14680064]{0:T(1024)(128)(4,1)}), s8[4194304]{0:T(1024)(128)(4,1)S(1)}, s32[]{:S(2)}) async-start(s8[14680064]{0:T(1024)(128)(4,1)} %bitcast.3), calls=%async_computation.4 | async-start | bytes 8388608
  6.4 16.5 %slice-start.1 = ((s8[14680064]{0:T(1024)(128)(4,1)}), s8[4194304]{0:T(1024)(128)(4,1)S(1)}, s32[]{:S(2)}) async-start(s8[14680064]{0:T(1024)(128)(4,1)} %bitcast.1), calls=%async_computation.1 | async-start | bytes 8388608
  6.4 16.5 %slice-start.2 = ((s8[14680064]{0:T(1024)(128)(4,1)}), s8[4194304]{0:T(1024)(128)(4,1)S(1)}, s32[]{:S(2)}) async-start(s8[14680064]{0:T(1024)(128)(4,1)} %bitcast.1), calls=%async_computation.2 | async-start | bytes 8388608
  6.4 16.5 %slice-start.3 = ((s8[14680064]{0:T(1024)(128)(4,1)}), s8[2097152]{0:T(1024)(128)(4,1)S(1)}, s32[]{:S(2)}) async-start(s8[14680064]{0:T(1024)(128)(4,1)} %bitcast.1), calls=%async_computation.3 | async-start | bytes 4194304
  6.4 16.5 %slice-start.5 = ((s8[14680064]{0:T(1024)(128)(4,1)}), s8[4194304]{0:T(1024)(128)(4,1)S(1)}, s32[]{:S(2)}) async-start(s8[14680064]{0:T(1024)(128)(4,1)} %bitcast.3), calls=%async_computation.5 | async-start | bytes 8388608
  6.4 16.5 %slice-start.6 = ((s8[14680064]{0:T(1024)(128)(4,1)}), s8[4194304]{0:T(1024)(128)(4,1)S(1)}, s32[]{:S(2)}) async-start(s8[14680064]{0:T(1024)(128)(4,1)} %bitcast.3), calls=%async_computation.6 | async-start | bytes 8388608
  6.4 16.5 %slice-start.7 = ((s8[14680064]{0:T(1024)(128)(4,1)}), s8[2097152]{0:T(1024)(128)(4,1)S(1)}, s32[]{:S(2)}) async-start(s8[14680064]{0:T(1024)(128)(4,1)} %bitcast.3), calls=%async_computation.7 | async-start | bytes 4194304
  6.4 8.9 %collective-permute-start.1 = (bf16[8,3712]{1,0:T(8,128)(2,1)S(1)}, bf16[8,3712]{1,0:T(8,128)(2,1)S(1)}, u32[]{:S(2)}, u32[]{:S(2)}) collective-permute-start(bf16[8,3712]{1,0:T(8,128)(2,1)S(1)} %shard_map.110.rows_ref.refs_0_), channel_id=1, source_target_pairs={{0,4},{4,0},{8,12},{12,8},{1,5},{5,1},{9,13},{13,9},{2,6},{6,2},{1... | collective-permute-start | bytes 178184 | tf_op jit(solution)/shard_map/ppermute | solution.py:188
  8.6 6.8 %collective-permute-start.2 = (bf16[8,3712]{1,0:T(8,128)(2,1)S(1)}, bf16[8,3712]{1,0:T(8,128)(2,1)S(1)}, u32[]{:S(2)}, u32[]{:S(2)}) collective-permute-start(bf16[8,3712]{1,0:T(8,128)(2,1)S(1)} %shard_map.110.rows_ref.refs_0_), channel_id=1, source_target_pairs={{0,8},{4,12},{8,0},{12,4},{1,9},{5,13},{9,1},{13,5},{2,10},{6,14},... | collective-permute-start | bytes 178184 | tf_op jit(solution)/shard_map/ppermute | solution.py:188
  11.2 6.0 %collective-permute-start.3 = (bf16[8,3712]{1,0:T(8,128)(2,1)S(1)}, bf16[8,3712]{1,0:T(8,128)(2,1)S(1)}, u32[]{:S(2)}, u32[]{:S(2)}) collective-permute-start(bf16[8,3712]{1,0:T(8,128)(2,1)S(1)} %shard_map.110.rows_ref.refs_0_), channel_id=1, source_target_pairs={{0,12},{4,8},{8,4},{12,0},{1,13},{5,9},{9,5},{13,1},{2,14},{6,10},... | collective-permute-start | bytes 178184 | tf_op jit(solution)/shard_map/ppermute | solution.py:188
  17.2 5.6 %collective-permute-start.4 = (bf16[32,3712]{1,0:T(8,128)(2,1)S(1)}, bf16[32,3712]{1,0:T(8,128)(2,1)S(1)}, u32[]{:S(2)}, u32[]{:S(2)}) collective-permute-start(bf16[32,3712]{1,0:T(8,128)(2,1)S(1)} %shard_map.112.x_ref.refs_0_), channel_id=1, source_target_pairs={{0,1},{1,0},{2,3},{3,2},{4,5},{5,4},{6,7},{7,6},{8,9},{9,8},{10,11... | collective-permute-start | bytes 712712 | tf_op jit(solution)/shard_map/ppermute | solution.py:188
  17.3 13.7 %collective-permute-start.10 = (bf16[256,896]{1,0:T(8,128)(2,1)S(1)}, bf16[256,896]{1,0:T(8,128)(2,1)S(1)}, u32[]{:S(2)}, u32[]{:S(2)}) collective-permute-start(bf16[256,896]{1,0:T(8,128)(2,1)S(1)} %copy-done), channel_id=1, source_target_pairs={{0,1},{1,0},{2,3},{3,2},{4,5},{5,4},{6,7},{7,6},{8,9},{9,8},{10,11... | collective-permute-start | bytes 1376264 | tf_op jit(solution)/shard_map/ppermute | solution.py:188
  18.4 12.4 %collective-permute-start.7 = (bf16[32,1024]{1,0:T(8,128)(2,1)S(1)}, bf16[32,1024]{1,0:T(8,128)(2,1)S(1)}, u32[]{:S(2)}, u32[]{:S(2)}) collective-permute-start(bf16[32,1024]{1,0:T(8,128)(2,1)S(1)} %shard_map.113.refs_2_), channel_id=1, source_target_pairs={{0,4},{4,0},{8,12},{12,8},{1,5},{5,1},{9,13},{13,9},{2,6},{6,2},{1... | collective-permute-start | bytes 196616 | tf_op jit(solution)/shard_map/ppermute | solution.py:188
  18.5 12.4 %collective-permute-start.8 = (bf16[32,1024]{1,0:T(8,128)(2,1)S(1)}, bf16[32,1024]{1,0:T(8,128)(2,1)S(1)}, u32[]{:S(2)}, u32[]{:S(2)}) collective-permute-start(bf16[32,1024]{1,0:T(8,128)(2,1)S(1)} %shard_map.113.refs_2_), channel_id=1, source_target_pairs={{0,8},{4,12},{8,0},{12,4},{1,9},{5,13},{9,1},{13,5},{2,10},{6,14},... | collective-permute-start | bytes 196616 | tf_op jit(solution)/shard_map/ppermute | solution.py:188
  21.1 9.8 %collective-permute-start.9 = (bf16[32,1024]{1,0:T(8,128)(2,1)S(1)}, bf16[32,1024]{1,0:T(8,128)(2,1)S(1)}, u32[]{:S(2)}, u32[]{:S(2)}) collective-permute-start(bf16[32,1024]{1,0:T(8,128)(2,1)S(1)} %shard_map.113.refs_2_), channel_id=1, source_target_pairs={{0,12},{4,8},{8,4},{12,0},{1,13},{5,9},{9,5},{13,1},{2,14},{6,10},... | collective-permute-start | bytes 196616 | tf_op jit(solution)/shard_map/ppermute | solution.py:188
  30.9 1.6 %collective-permute-start.11 = (bf16[32,3584]{1,0:T(8,128)(2,1)S(1)}, bf16[32,3584]{1,0:T(8,128)(2,1)S(1)}, u32[]{:S(2)}, u32[]{:S(2)}) collective-permute-start(bf16[32,3584]{1,0:T(8,128)(2,1)S(1)} %get-tuple-element.54), channel_id=1, source_target_pairs={{0,1},{1,0},{2,3},{3,2},{4,5},{5,4},{6,7},{7,6},{8,9},{9,8},{10,11... | collective-permute-start | bytes 688136 | tf_op jit(solution)/shard_map/ppermute | solution.py:188
  32.5 6.6 %collective-permute-start.12 = (bf16[8,3584]{1,0:T(8,128)(2,1)S(1)}, bf16[8,3584]{1,0:T(8,128)(2,1)S(1)}, u32[]{:S(2)}, u32[]{:S(2)}) collective-permute-start(bf16[8,3584]{1,0:T(8,128)(2,1)S(1)} %get-tuple-element.55), channel_id=1, source_target_pairs={{0,12},{4,8},{8,4},{12,0},{1,13},{5,9},{9,5},{13,1},{2,14},{6,10},... | collective-permute-start | bytes 172040 | tf_op jit(solution)/shard_map/ppermute | solution.py:188
  34.6 6.2 %collective-permute-start.13 = (bf16[8,3584]{1,0:T(8,128)(2,1)S(1)}, bf16[8,3584]{1,0:T(8,128)(2,1)S(1)}, u32[]{:S(2)}, u32[]{:S(2)}) collective-permute-start(bf16[8,3584]{1,0:T(8,128)(2,1)S(1)} %get-tuple-element.57), channel_id=1, source_target_pairs={{0,8},{4,12},{8,0},{12,4},{1,9},{5,13},{9,1},{13,5},{2,10},{6,14},... | collective-permute-start | bytes 172040 | tf_op jit(solution)/shard_map/ppermute | solution.py:188
  34.6 6.2 %collective-permute-start.14 = (bf16[8,3584]{1,0:T(8,128)(2,1)S(1)}, bf16[8,3584]{1,0:T(8,128)(2,1)S(1)}, u32[]{:S(2)}, u32[]{:S(2)}) collective-permute-start(bf16[8,3584]{1,0:T(8,128)(2,1)S(1)} %get-tuple-element.56), channel_id=1, source_target_pairs={{0,4},{4,0},{8,12},{12,8},{1,5},{5,1},{9,13},{13,9},{2,6},{6,2},{1... | collective-permute-start | bytes 172040 | tf_op jit(solution)/shard_map/ppermute | solution.py:188
  40.9 3.9 %collective-permute-start.15 = (bf16[4,3584]{1,0:T(4,128)(2,1)S(1)}, bf16[4,3584]{1,0:T(4,128)(2,1)S(1)}, u32[]{:S(2)}, u32[]{:S(2)}) collective-permute-start(bf16[4,3584]{1,0:T(4,128)(2,1)S(1)} %slice.29), channel_id=1, source_target_pairs={{0,2},{1,3},{2,0},{3,1},{4,6},{5,7},{6,4},{7,5},{8,10},{9,11},{10,... | collective-permute-start | bytes 86024 | tf_op jit(solution)/shard_map/ppermute | solution.py:188
  (1 other events, 10.9 us)

commit v9 on v8

--- a/solution.py
+++ b/solution.py
@@ -315,7 +315,7 @@
     for axis, bits in reversed(stages[:-1]):
         unit = out.shape[0] // (len(bits) + 1)
         total = out[:unit].astype(jnp.float32)
-        for i in reversed(range(len(bits))):
+        for i in ([1, 2, 0] if len(bits) == 3 else reversed(range(len(bits)))):
             piece = out[unit * (i + 1) : unit * (i + 2)]
             total = total + exchange(piece, axis, bits[i]).astype(jnp.float32)
         out = total.astype(jnp.bfloat16)

time: 45.6 us -> 45.3 us (level)
  starting transfers between devices: 19.3 us -> 18.4 us
  waiting for transfers between devices: 10.9 us -> 11.5 us
    ppermute x16, starting transfers between devices: 19.3 us -> 18.4 us  [exchange(): return lax.ppermute(value, axis, [(i, i ^ bit) for i in range(size)])]
    ppermute x16, waiting for transfers between devices: 10.9 us -> 11.5 us  [exchange(): return lax.ppermute(value, axis, [(i, i ^ bit) for i in range(size)])]
where the time goes in v9:
time: 45.3 us; the launch traced here: 45.2 us
  starting transfers between devices  18.4 us (41%)
  Pallas kernels  14.1 us (31%)
  waiting for transfers between devices  11.5 us (25%)
  other arithmetic  0.7 us (2%)
    ppermute x16, starting transfers between devices, exchange(): return lax.ppermute(value, axis, [(i, i ^ bit) for i in range(size)])  18.4 us
    ppermute x16, waiting for transfers between devices, exchange(): return lax.ppermute(value, axis, [(i, i ^ bit) for i in range(size)])  11.5 us
    pallas_call x1, Pallas kernels, local(): pl.pallas_call(functools.partial(routed_kernel, len(ready)), out_shape=[j...  7.86 us
    pallas_call x1, Pallas kernels, bring(): pl.pallas_call(functools.partial(bring_kernel, [e for _, e in wanted]), o...  4.17 us
    pallas_call x1, Pallas kernels, local(): pl.pallas_call(functools.partial(pack_kernel, per_group), out_shape=jax.S...  0.95 us
  transfers between devices with their start and end apart: 16, of which 6 were waited for; matrix products, arithmetic and copies ran while one was open for 0% of the time, Pallas kernels for 31%

profile of v9, /device:TPU:0, one launch (start us, length us, event | category | flops | bytes accessed | tf_op | source)
XLA Modules:
  0.0 45.2 jit_solution(14473589136763191960)
XLA Ops:
  0.0 0.5 %collective-permute-start.5 = (bf16[256,896]{1,0:T(8,128)(2,1)}, bf16[256,896]{1,0:T(8,128)(2,1)S(1)}, u32[]{:S(2)}, u32[]{:S(2)}) collective-permute-start(bf16[256,896]{1,0:T(8,128)(2,1)} %refs_4_.3), channel_id=1, source_target_pairs={{0,1},{1,0},{2,3},{3,2},{4,5},{5,4},{6,7},{7,6},{8,9},{9,8},{10,11... | collective-permute-start | bytes 1376264 | tf_op jit(solution)/shard_map/ppermute | solution.py:188
  0.5 1.0 %shard_map.109.refs_0_ = bf16[4,3712]{1,0:T(4,128)(2,1)S(1)} custom-call(s32[1]{0:T(128)} %bitcast.node_ref, bf16[4,3584]{1,0:T(4,128)(2,1)} %refs_0_.3, f32[3584]{0:T(1024)} %refs_1_.2, s32[4,4]{1,0:T(4,128)} %refs_2_.2, s32[4,8]{1,0:T(4,128)} %refs_3_.2, bf16[4,8]{1,0:T(4,128)(2,1)} %refs_4_.2), custom_call_target="tpu_custom_call" | custom-call | flops 80000000000 | tf_op jit(solution)/shard_map/pallas_call | solution.py:223
  1.5 3.0 %collective-permute-start = (bf16[4,3712]{1,0:T(4,128)(2,1)S(1)}, bf16[4,3712]{1,0:T(4,128)(2,1)S(1)}, u32[]{:S(2)}, u32[]{:S(2)}) collective-permute-start(bf16[4,3712]{1,0:T(4,128)(2,1)S(1)} %shard_map.109.refs_0_), channel_id=1, source_target_pairs={{0,2},{1,3},{2,0},{3,1},{4,6},{5,7},{6,4},{7,5},{8,10},{9,11},{10,... | collective-permute-start | bytes 89096 | tf_op jit(solution)/shard_map/ppermute | solution.py:188
  4.5 1.9 %collective-permute-done.refs_1_ = bf16[4,3712]{1,0:T(4,128)(2,1)S(1)} collective-permute-done((bf16[4,3712]{1,0:T(4,128)(2,1)S(1)}, bf16[4,3712]{1,0:T(4,128)(2,1)S(1)}, u32[]{:S(2)}, u32[]{:S(2)}) %collective-permute-start) | collective-permute-done | bytes 29728 | tf_op jit(solution)/shard_map/ppermute | solution.py:188
  6.4 2.2 %collective-permute-start.1 = (bf16[8,3712]{1,0:T(8,128)(2,1)S(1)}, bf16[8,3712]{1,0:T(8,128)(2,1)S(1)}, u32[]{:S(2)}, u32[]{:S(2)}) collective-permute-start(bf16[8,3712]{1,0:T(8,128)(2,1)S(1)} %shard_map.110.rows_ref.refs_0_), channel_id=1, source_target_pairs={{0,4},{4,0},{8,12},{12,8},{1,5},{5,1},{9,13},{13,9},{2,6},{6,2},{1... | collective-permute-start | bytes 178184 | tf_op jit(solution)/shard_map/ppermute | solution.py:188
  8.6 2.6 %collective-permute-start.2 = (bf16[8,3712]{1,0:T(8,128)(2,1)S(1)}, bf16[8,3712]{1,0:T(8,128)(2,1)S(1)}, u32[]{:S(2)}, u32[]{:S(2)}) collective-permute-start(bf16[8,3712]{1,0:T(8,128)(2,1)S(1)} %shard_map.110.rows_ref.refs_0_), channel_id=1, source_target_pairs={{0,8},{4,12},{8,0},{12,4},{1,9},{5,13},{9,1},{13,5},{2,10},{6,14},... | collective-permute-start | bytes 178184 | tf_op jit(solution)/shard_map/ppermute | solution.py:188
  11.2 4.2 %shard_map.111 = (bf16[3584,256]{1,0:T(8,128)(2,1)S(1)}, bf16[3584,256]{1,0:T(8,128)(2,1)S(1)}, bf16[3584,256]{1,0:T(8,128)(2,1)S(1)}, bf16[3584,256]{1,0:T(8,12...) custom-call(bf16[8,3712]{1,0:T(8,128)(2,1)S(1)} %shard_map.110.rows_ref.refs_0_, ...), custom_call_target="tpu_custom_call" | custom-call | tf_op jit(solution)/shard_map/pallas_call | solution.py:147
  15.4 1.8 %collective-permute-done.3.refs_3_ = bf16[8,3712]{1,0:T(8,128)(2,1)S(1)} collective-permute-done((bf16[8,3712]{1,0:T(8,128)(2,1)S(1)}, bf16[8,3712]{1,0:T(8,128)(2,1)S(1)}, u32[]{:S(2)}, u32[]{:S(2)}) %collective-permute-start.3) | collective-permute-done | bytes 59424 | tf_op jit(solution)/shard_map/ppermute | solution.py:188
  17.2 0.1 collective-permute-start.4
  17.3 0.5 %collective-permute-start.10 = (bf16[256,896]{1,0:T(8,128)(2,1)S(1)}, bf16[256,896]{1,0:T(8,128)(2,1)S(1)}, u32[]{:S(2)}, u32[]{:S(2)}) collective-permute-start(bf16[256,896]{1,0:T(8,128)(2,1)S(1)} %copy-done), channel_id=1, source_target_pairs={{0,1},{1,0},{2,3},{3,2},{4,5},{5,4},{6,7},{7,6},{8,9},{9,8},{10,11... | collective-permute-start | bytes 1376264 | tf_op jit(solution)/shard_map/ppermute | solution.py:188
  17.8 0.6 %shard_map.113.refs_2_ = bf16[32,1024]{1,0:T(8,128)(2,1)S(1)} custom-call(s32[1]{0:T(128)} %bitcast.node_ref, bf16[32,3712]{1,0:T(8,128)(2,1)S(1)} %shard_map.112.x_ref.refs_0_, bf16[256,896]{1,0:T(8,128)(2,1)S(1)} %get-tuple-element.39.refs_0_, bf16[256,896]{1,0:T(8,128)(2,1)S(1)} %get-tuple-element.40.refs_1_, ...), custom_call_target="tpu_custom_call" | custom-call | tf_op jit(solution)/shard_map/pallas_call | solution.py:260
  18.5 2.6 %collective-permute-start.8 = (bf16[32,1024]{1,0:T(8,128)(2,1)S(1)}, bf16[32,1024]{1,0:T(8,128)(2,1)S(1)}, u32[]{:S(2)}, u32[]{:S(2)}) collective-permute-start(bf16[32,1024]{1,0:T(8,128)(2,1)S(1)} %shard_map.113.refs_2_), channel_id=1, source_target_pairs={{0,8},{4,12},{8,0},{12,4},{1,9},{5,13},{9,1},{13,5},{2,10},{6,14},... | collective-permute-start | bytes 196616 | tf_op jit(solution)/shard_map/ppermute | solution.py:188
  21.1 1.8 %collective-permute-start.9 = (bf16[32,1024]{1,0:T(8,128)(2,1)S(1)}, bf16[32,1024]{1,0:T(8,128)(2,1)S(1)}, u32[]{:S(2)}, u32[]{:S(2)}) collective-permute-start(bf16[32,1024]{1,0:T(8,128)(2,1)S(1)} %shard_map.113.refs_2_), channel_id=1, source_target_pairs={{0,12},{4,8},{8,4},{12,0},{1,13},{5,9},{9,5},{13,1},{2,14},{6,10},... | collective-permute-start | bytes 196616 | tf_op jit(solution)/shard_map/ppermute | solution.py:188
  23.0 7.9 %shard_map.115 = (f32[32,3584]{1,0:T(8,128)S(1)}, bf16[32,3584]{1,0:T(8,128)(2,1)S(1)}) custom-call(s32[1]{0:T(128)} %bitcast.node_ref, bf16[64,3712]{1,0:T(8,128)(2,1)S(1)} %shard_map.114.x_ref, bf16[8,3584,256]{2,1,0:T(8,128)(2,1)} %gate_hbm.1, bf16[8,3584,256]{2,1,0:T(8,128)(2,1)S(1)} %bitcast.2, bf16[8,256,3584]{2,1,0:T(8,128)(2,1)S(1)} %bitcast.4, ...), custom_call_target="tpu_custom_call" | custom-call | tf_op jit(solution)/shard_map/pallas_call | solution.py:275
  30.9 0.1 collective-permute-start.11
  31.0 0.4 shard_map.116
  31.4 1.0 %collective-permute-done.11 = bf16[32,3584]{1,0:T(8,128)(2,1)S(1)} collective-permute-done((bf16[32,3584]{1,0:T(8,128)(2,1)S(1)}, bf16[32,3584]{1,0:T(8,128)(2,1)S(1)}, u32[]{:S(2)}, u32[]{:S(2)}) %collective-permute-start.11) | collective-permute-done | bytes 229408 | tf_op jit(solution)/shard_map/ppermute | solution.py:188
  32.6 2.1 %collective-permute-start.13 = (bf16[8,3584]{1,0:T(8,128)(2,1)S(1)}, bf16[8,3584]{1,0:T(8,128)(2,1)S(1)}, u32[]{:S(2)}, u32[]{:S(2)}) collective-permute-start(bf16[8,3584]{1,0:T(8,128)(2,1)S(1)} %get-tuple-element.57), channel_id=1, source_target_pairs={{0,12},{4,8},{8,4},{12,0},{1,13},{5,9},{9,5},{13,1},{2,14},{6,10},... | collective-permute-start | bytes 172040 | tf_op jit(solution)/shard_map/ppermute | solution.py:188
  34.7 1.4 %collective-permute-start.14 = (bf16[8,3584]{1,0:T(8,128)(2,1)S(1)}, bf16[8,3584]{1,0:T(8,128)(2,1)S(1)}, u32[]{:S(2)}, u32[]{:S(2)}) collective-permute-start(bf16[8,3584]{1,0:T(8,128)(2,1)S(1)} %get-tuple-element.56), channel_id=1, source_target_pairs={{0,4},{4,0},{8,12},{12,8},{1,5},{5,1},{9,13},{13,9},{2,6},{6,2},{1... | collective-permute-start | bytes 172040 | tf_op jit(solution)/shard_map/ppermute | solution.py:188
  36.1 3.5 %collective-permute-done.12 = bf16[8,3584]{1,0:T(8,128)(2,1)S(1)} collective-permute-done((bf16[8,3584]{1,0:T(8,128)(2,1)S(1)}, bf16[8,3584]{1,0:T(8,128)(2,1)S(1)}, u32[]{:S(2)}, u32[]{:S(2)}) %collective-permute-start.12) | collective-permute-done | bytes 57376 | tf_op jit(solution)/shard_map/ppermute | solution.py:188
  39.5 1.0 %collective-permute-done.14 = bf16[8,3584]{1,0:T(8,128)(2,1)S(1)} collective-permute-done((bf16[8,3584]{1,0:T(8,128)(2,1)S(1)}, bf16[8,3584]{1,0:T(8,128)(2,1)S(1)}, u32[]{:S(2)}, u32[]{:S(2)}) %collective-permute-start.14) | collective-permute-done | bytes 57376 | tf_op jit(solution)/shard_map/ppermute | solution.py:188
  40.6 1.6 %collective-permute-start.15 = (bf16[4,3584]{1,0:T(4,128)(2,1)S(1)}, bf16[4,3584]{1,0:T(4,128)(2,1)S(1)}, u32[]{:S(2)}, u32[]{:S(2)}) collective-permute-start(bf16[4,3584]{1,0:T(4,128)(2,1)S(1)} %slice.29), channel_id=1, source_target_pairs={{0,2},{1,3},{2,0},{3,1},{4,6},{5,7},{6,4},{7,5},{8,10},{9,11},{10,... | collective-permute-start | bytes 86024 | tf_op jit(solution)/shard_map/ppermute | solution.py:188
  42.2 2.4 %collective-permute-done.15 = bf16[4,3584]{1,0:T(4,128)(2,1)S(1)} collective-permute-done((bf16[4,3584]{1,0:T(4,128)(2,1)S(1)}, bf16[4,3584]{1,0:T(4,128)(2,1)S(1)}, u32[]{:S(2)}, u32[]{:S(2)}) %collective-permute-start.15) | collective-permute-done | bytes 28704 | tf_op jit(solution)/shard_map/ppermute | solution.py:188
  44.5 0.6 %add_convert_fusion.2 = bf16[4,3584]{1,0:T(4,128)(2,1)} fusion(bf16[4,3584]{1,0:T(4,128)(2,1)S(1)} %collective-permute-done.15, bf16[8,3584]{1,0:T(8,128)(2,1)S(1)} %add_convert_fusion.1), kind=kLoop, calls=%fused_computation.2 | loop fusion | flops 57344 | bytes 86016 | tf_op jit(solution)/shard_map/convert_element_type | solution.py:321
  (41 shorter events, 0.4 us)
Async XLA Ops:
  0.0 17.8 %collective-permute-start.5 = (bf16[256,896]{1,0:T(8,128)(2,1)}, bf16[256,896]{1,0:T(8,128)(2,1)S(1)}, u32[]{:S(2)}, u32[]{:S(2)}) collective-permute-start(bf16[256,896]{1,0:T(8,128)(2,1)} %refs_4_.3), channel_id=1, source_target_pairs={{0,1},{1,0},{2,3},{3,2},{4,5},{5,4},{6,7},{7,6},{8,9},{9,8},{10,11... | collective-permute-start | bytes 1376264 | tf_op jit(solution)/shard_map/ppermute | solution.py:188
  0.5 17.4 %collective-permute-start.6 = (bf16[256,896]{1,0:T(8,128)(2,1)}, bf16[256,896]{1,0:T(8,128)(2,1)S(1)}, u32[]{:S(2)}, u32[]{:S(2)}) collective-permute-start(bf16[256,896]{1,0:T(8,128)(2,1)} %refs_5_.1), channel_id=1, source_target_pairs={{0,1},{1,0},{2,3},{3,2},{4,5},{5,4},{6,7},{7,6},{8,9},{9,8},{10,11... | collective-permute-start | bytes 1376264 | tf_op jit(solution)/shard_map/ppermute | solution.py:188
  1.5 4.9 %collective-permute-start = (bf16[4,3712]{1,0:T(4,128)(2,1)S(1)}, bf16[4,3712]{1,0:T(4,128)(2,1)S(1)}, u32[]{:S(2)}, u32[]{:S(2)}) collective-permute-start(bf16[4,3712]{1,0:T(4,128)(2,1)S(1)} %shard_map.109.refs_0_), channel_id=1, source_target_pairs={{0,2},{1,3},{2,0},{3,1},{4,6},{5,7},{6,4},{7,5},{8,10},{9,11},{10,... | collective-permute-start | bytes 89096 | tf_op jit(solution)/shard_map/ppermute | solution.py:188
  6.3 16.6 %slice-start = ((s8[14680064]{0:T(1024)(128)(4,1)}), s8[4194304]{0:T(1024)(128)(4,1)S(1)}, s32[]{:S(2)}) async-start(s8[14680064]{0:T(1024)(128)(4,1)} %bitcast.1), calls=%async_computation | async-start | bytes 8388608
  6.3 16.6 %slice-start.4 = ((s8[14680064]{0:T(1024)(128)(4,1)}), s8[4194304]{0:T(1024)(128)(4,1)S(1)}, s32[]{:S(2)}) async-start(s8[14680064]{0:T(1024)(128)(4,1)} %bitcast.3), calls=%async_computation.4 | async-start | bytes 8388608
  6.4 16.5 %slice-start.1 = ((s8[14680064]{0:T(1024)(128)(4,1)}), s8[4194304]{0:T(1024)(128)(4,1)S(1)}, s32[]{:S(2)}) async-start(s8[14680064]{0:T(1024)(128)(4,1)} %bitcast.1), calls=%async_computation.1 | async-start | bytes 8388608
  6.4 16.5 %slice-start.2 = ((s8[14680064]{0:T(1024)(128)(4,1)}), s8[4194304]{0:T(1024)(128)(4,1)S(1)}, s32[]{:S(2)}) async-start(s8[14680064]{0:T(1024)(128)(4,1)} %bitcast.1), calls=%async_computation.2 | async-start | bytes 8388608
  6.4 16.5 %slice-start.3 = ((s8[14680064]{0:T(1024)(128)(4,1)}), s8[2097152]{0:T(1024)(128)(4,1)S(1)}, s32[]{:S(2)}) async-start(s8[14680064]{0:T(1024)(128)(4,1)} %bitcast.1), calls=%async_computation.3 | async-start | bytes 4194304
  6.4 16.5 %slice-start.5 = ((s8[14680064]{0:T(1024)(128)(4,1)}), s8[4194304]{0:T(1024)(128)(4,1)S(1)}, s32[]{:S(2)}) async-start(s8[14680064]{0:T(1024)(128)(4,1)} %bitcast.3), calls=%async_computation.5 | async-start | bytes 8388608
  6.4 16.5 %slice-start.6 = ((s8[14680064]{0:T(1024)(128)(4,1)}), s8[4194304]{0:T(1024)(128)(4,1)S(1)}, s32[]{:S(2)}) async-start(s8[14680064]{0:T(1024)(128)(4,1)} %bitcast.3), calls=%async_computation.6 | async-start | bytes 8388608
  6.4 16.5 %slice-start.7 = ((s8[14680064]{0:T(1024)(128)(4,1)}), s8[2097152]{0:T(1024)(128)(4,1)S(1)}, s32[]{:S(2)}) async-start(s8[14680064]{0:T(1024)(128)(4,1)} %bitcast.3), calls=%async_computation.7 | async-start | bytes 4194304
  6.4 8.9 %collective-permute-start.1 = (bf16[8,3712]{1,0:T(8,128)(2,1)S(1)}, bf16[8,3712]{1,0:T(8,128)(2,1)S(1)}, u32[]{:S(2)}, u32[]{:S(2)}) collective-permute-start(bf16[8,3712]{1,0:T(8,128)(2,1)S(1)} %shard_map.110.rows_ref.refs_0_), channel_id=1, source_target_pairs={{0,4},{4,0},{8,12},{12,8},{1,5},{5,1},{9,13},{13,9},{2,6},{6,2},{1... | collective-permute-start | bytes 178184 | tf_op jit(solution)/shard_map/ppermute | solution.py:188
  8.6 6.8 %collective-permute-start.2 = (bf16[8,3712]{1,0:T(8,128)(2,1)S(1)}, bf16[8,3712]{1,0:T(8,128)(2,1)S(1)}, u32[]{:S(2)}, u32[]{:S(2)}) collective-permute-start(bf16[8,3712]{1,0:T(8,128)(2,1)S(1)} %shard_map.110.rows_ref.refs_0_), channel_id=1, source_target_pairs={{0,8},{4,12},{8,0},{12,4},{1,9},{5,13},{9,1},{13,5},{2,10},{6,14},... | collective-permute-start | bytes 178184 | tf_op jit(solution)/shard_map/ppermute | solution.py:188
  11.2 6.0 %collective-permute-start.3 = (bf16[8,3712]{1,0:T(8,128)(2,1)S(1)}, bf16[8,3712]{1,0:T(8,128)(2,1)S(1)}, u32[]{:S(2)}, u32[]{:S(2)}) collective-permute-start(bf16[8,3712]{1,0:T(8,128)(2,1)S(1)} %shard_map.110.rows_ref.refs_0_), channel_id=1, source_target_pairs={{0,12},{4,8},{8,4},{12,0},{1,13},{5,9},{9,5},{13,1},{2,14},{6,10},... | collective-permute-start | bytes 178184 | tf_op jit(solution)/shard_map/ppermute | solution.py:188
  17.2 5.6 %collective-permute-start.4 = (bf16[32,3712]{1,0:T(8,128)(2,1)S(1)}, bf16[32,3712]{1,0:T(8,128)(2,1)S(1)}, u32[]{:S(2)}, u32[]{:S(2)}) collective-permute-start(bf16[32,3712]{1,0:T(8,128)(2,1)S(1)} %shard_map.112.x_ref.refs_0_), channel_id=1, source_target_pairs={{0,1},{1,0},{2,3},{3,2},{4,5},{5,4},{6,7},{7,6},{8,9},{9,8},{10,11... | collective-permute-start | bytes 712712 | tf_op jit(solution)/shard_map/ppermute | solution.py:188
  17.3 13.7 %collective-permute-start.10 = (bf16[256,896]{1,0:T(8,128)(2,1)S(1)}, bf16[256,896]{1,0:T(8,128)(2,1)S(1)}, u32[]{:S(2)}, u32[]{:S(2)}) collective-permute-start(bf16[256,896]{1,0:T(8,128)(2,1)S(1)} %copy-done), channel_id=1, source_target_pairs={{0,1},{1,0},{2,3},{3,2},{4,5},{5,4},{6,7},{7,6},{8,9},{9,8},{10,11... | collective-permute-start | bytes 1376264 | tf_op jit(solution)/shard_map/ppermute | solution.py:188
  18.4 12.4 %collective-permute-start.7 = (bf16[32,1024]{1,0:T(8,128)(2,1)S(1)}, bf16[32,1024]{1,0:T(8,128)(2,1)S(1)}, u32[]{:S(2)}, u32[]{:S(2)}) collective-permute-start(bf16[32,1024]{1,0:T(8,128)(2,1)S(1)} %shard_map.113.refs_2_), channel_id=1, source_target_pairs={{0,4},{4,0},{8,12},{12,8},{1,5},{5,1},{9,13},{13,9},{2,6},{6,2},{1... | collective-permute-start | bytes 196616 | tf_op jit(solution)/shard_map/ppermute | solution.py:188
  18.5 12.4 %collective-permute-start.8 = (bf16[32,1024]{1,0:T(8,128)(2,1)S(1)}, bf16[32,1024]{1,0:T(8,128)(2,1)S(1)}, u32[]{:S(2)}, u32[]{:S(2)}) collective-permute-start(bf16[32,1024]{1,0:T(8,128)(2,1)S(1)} %shard_map.113.refs_2_), channel_id=1, source_target_pairs={{0,8},{4,12},{8,0},{12,4},{1,9},{5,13},{9,1},{13,5},{2,10},{6,14},... | collective-permute-start | bytes 196616 | tf_op jit(solution)/shard_map/ppermute | solution.py:188
  21.1 9.8 %collective-permute-start.9 = (bf16[32,1024]{1,0:T(8,128)(2,1)S(1)}, bf16[32,1024]{1,0:T(8,128)(2,1)S(1)}, u32[]{:S(2)}, u32[]{:S(2)}) collective-permute-start(bf16[32,1024]{1,0:T(8,128)(2,1)S(1)} %shard_map.113.refs_2_), channel_id=1, source_target_pairs={{0,12},{4,8},{8,4},{12,0},{1,13},{5,9},{9,5},{13,1},{2,14},{6,10},... | collective-permute-start | bytes 196616 | tf_op jit(solution)/shard_map/ppermute | solution.py:188
  30.9 1.6 %collective-permute-start.11 = (bf16[32,3584]{1,0:T(8,128)(2,1)S(1)}, bf16[32,3584]{1,0:T(8,128)(2,1)S(1)}, u32[]{:S(2)}, u32[]{:S(2)}) collective-permute-start(bf16[32,3584]{1,0:T(8,128)(2,1)S(1)} %get-tuple-element.54), channel_id=1, source_target_pairs={{0,1},{1,0},{2,3},{3,2},{4,5},{5,4},{6,7},{7,6},{8,9},{9,8},{10,11... | collective-permute-start | bytes 688136 | tf_op jit(solution)/shard_map/ppermute | solution.py:188
  32.5 7.0 %collective-permute-start.12 = (bf16[8,3584]{1,0:T(8,128)(2,1)S(1)}, bf16[8,3584]{1,0:T(8,128)(2,1)S(1)}, u32[]{:S(2)}, u32[]{:S(2)}) collective-permute-start(bf16[8,3584]{1,0:T(8,128)(2,1)S(1)} %get-tuple-element.55), channel_id=1, source_target_pairs={{0,8},{4,12},{8,0},{12,4},{1,9},{5,13},{9,1},{13,5},{2,10},{6,14},... | collective-permute-start | bytes 172040 | tf_op jit(solution)/shard_map/ppermute | solution.py:188
  32.6 7.0 %collective-permute-start.13 = (bf16[8,3584]{1,0:T(8,128)(2,1)S(1)}, bf16[8,3584]{1,0:T(8,128)(2,1)S(1)}, u32[]{:S(2)}, u32[]{:S(2)}) collective-permute-start(bf16[8,3584]{1,0:T(8,128)(2,1)S(1)} %get-tuple-element.57), channel_id=1, source_target_pairs={{0,12},{4,8},{8,4},{12,0},{1,13},{5,9},{9,5},{13,1},{2,14},{6,10},... | collective-permute-start | bytes 172040 | tf_op jit(solution)/shard_map/ppermute | solution.py:188
  34.7 5.8 %collective-permute-start.14 = (bf16[8,3584]{1,0:T(8,128)(2,1)S(1)}, bf16[8,3584]{1,0:T(8,128)(2,1)S(1)}, u32[]{:S(2)}, u32[]{:S(2)}) collective-permute-start(bf16[8,3584]{1,0:T(8,128)(2,1)S(1)} %get-tuple-element.56), channel_id=1, source_target_pairs={{0,4},{4,0},{8,12},{12,8},{1,5},{5,1},{9,13},{13,9},{2,6},{6,2},{1... | collective-permute-start | bytes 172040 | tf_op jit(solution)/shard_map/ppermute | solution.py:188
  40.6 3.9 %collective-permute-start.15 = (bf16[4,3584]{1,0:T(4,128)(2,1)S(1)}, bf16[4,3584]{1,0:T(4,128)(2,1)S(1)}, u32[]{:S(2)}, u32[]{:S(2)}) collective-permute-start(bf16[4,3584]{1,0:T(4,128)(2,1)S(1)} %slice.29), channel_id=1, source_target_pairs={{0,2},{1,3},{2,0},{3,1},{4,6},{5,7},{6,4},{7,5},{8,10},{9,11},{10,... | collective-permute-start | bytes 86024 | tf_op jit(solution)/shard_map/ppermute | solution.py:188
  (1 other events, 10.9 us)
